TPU v7x, 32 devices: a whole 2x2x4 slice. The times are simulated.
32 devices in a mesh: groups: 2 (over y), dom: 4 (over z), sub: 2 (over x), inner: 2 (over core).
Axes of the slice: x: 2, y: 2, z: 4, core: 2. Of those that a mesh axis runs over, the one named last changes fastest.
Arguments:
- node_state: bfloat16 [8192, 128], P(('groups', 'dom', 'sub')), parts along dimension 0, may hold values from -6 to 6
- edge_state: bfloat16 [49152, 128], P(('groups', 'dom', 'sub', 'inner')), parts along dimension 0, may hold values from -6 to 6
- edge_count: int32 [32], P(('groups', 'dom', 'sub', 'inner')), parts along dimension 0, may hold values from 768 to 1536, as said below
- block_start: int32 [192], P(('groups', 'dom', 'sub', 'inner')), parts along dimension 0, may hold values from 0 to 384, as said below
- edge_offset: int32 [49152], P(('groups', 'dom', 'sub', 'inner')), parts along dimension 0, may hold values from 0 to 127
- edge_other: int32 [49152], P(('groups', 'dom', 'sub', 'inner')), parts along dimension 0, may hold values from 0 to 2047, as said below
- send_index: int32 [4096], P(('groups', 'dom', 'sub')), parts along dimension 0, may hold values from 0 to 511, as said below
- edge_entry: bfloat16 [384, 128], replicated, may hold values from -0.3125 to 0.3125
- edge_middle: bfloat16 [128, 128], replicated, may hold values from -0.5 to 0.5
- edge_outlet: bfloat16 [128, 128], replicated, may hold values from -0.5 to 0.5
- edge_gain: float32 [128], replicated, may hold values from 0.1 to 1.9
- node_entry: bfloat16 [256, 128], replicated, may hold values from -0.375 to 0.375
- node_middle: bfloat16 [128, 128], replicated, may hold values from -0.5 to 0.5
- node_outlet: bfloat16 [128, 128], replicated, may hold values from -0.5 to 0.5
- node_gain: float32 [128], replicated, may hold values from 0.1 to 1.9
- node_cotangent: bfloat16 [8192, 128], P(('groups', 'dom', 'sub')), parts along dimension 0, may hold values from -6 to 6
- edge_cotangent: bfloat16 [49152, 128], P(('groups', 'dom', 'sub', 'inner')), parts along dimension 0, may hold values from -6 to 6
Outputs:
- new_nodes: bfloat16 [8192, 128], P(('groups', 'dom', 'sub')), parts along dimension 0
- new_edges: bfloat16 [49152, 128], P(('groups', 'dom', 'sub', 'inner')), parts along dimension 0
- node_adjoint: bfloat16 [8192, 128], P(('groups', 'dom', 'sub')), parts along dimension 0
- edge_adjoint: bfloat16 [49152, 128], P(('groups', 'dom', 'sub', 'inner')), parts along dimension 0
- edge_gradient: float32 [1280, 128], P('groups'), parts along dimension 0
- node_gradient: float32 [1024, 128], P('groups'), parts along dimension 0
- gain_gradient: float32 [4, 128], P('groups'), parts along dimension 0
There are 2 independent parts, one for each index of `groups`. A program takes and returns all parts, laid end to end along the dimension named above; an argument that names none is the same for every part. Nothing has to cross between parts.
Inputs may be any that keep to these rules, and one draw needn't show every extreme that they name: `edge_count`: number of live slots at the head of each shard; some shard is full and some holds exactly half. `block_start`: each incidence block's window of 128 rows lies inside its node block. `edge_other`: values of 512 or more name border slot s = value - 512 of the slab below (r = 0), the own slab (r = 1) or the slab above (r = 2); the first slab never names r = 0 and the last never r = 2. `send_index`: the 256 rows of one block are distinct.
All inputs are finite; a program needn't handle non-finite values.
Results may differ from a plain program's by a relative error of at most 0.013.
Values may be sent and summed in bfloat16 or wider, within the bound.
No kernel may reach another device: no remote copies, remote signals or barrier semaphores. Data moves between devices by JAX's collectives and lax.ppermute only.
A program may use at most 64 MiB of HBM per device.

v0:
```python
import math

import jax
import jax.numpy as jnp
from jax import lax
from jax.sharding import PartitionSpec as P

WINDOW = 128


EPS = 1e-05


def extended_2(cells, sides, width):
    for axis, dim in sides:
        count = lax.axis_size(axis)
        ends = count - 1
        head = lax.slice_in_dim(cells, 0, width, axis=dim)
        tail = lax.slice_in_dim(cells, cells.shape[dim] - width, cells.shape[dim], axis=dim)
        cells = jnp.concatenate(
            [
                lax.ppermute(tail, axis, [(i, (i + 1) % count) for i in range(ends)]),
                cells,
                lax.ppermute(head, axis, [((i + 1) % count, i) for i in range(ends)]),
            ],
            axis=dim,
        )
    return cells


def silu_pair(pre_act):
    logistic = jax.nn.sigmoid(pre_act)
    return (pre_act * logistic, logistic * (1.0 + pre_act * (1.0 - logistic)))


def matmul(left, right):
    return jnp.dot(left, right, preferred_element_type=jnp.float32)


def contract(left, right):
    return lax.dot_general(
        left, right, (((0,), (0,)), ((), ())), preferred_element_type=jnp.float32
    )


def transposed(left, right):
    return lax.dot_general(
        left, right, (((1,), (1,)), ((), ())), preferred_element_type=jnp.float32
    )


def mlp_forward(inputs, entry_weight, middle_weight, outlet_weight):
    first_act, first_slope = silu_pair(matmul(inputs, entry_weight))
    first_hidden = first_act.astype(jnp.bfloat16)
    second_act, second_slope = silu_pair(matmul(first_hidden, middle_weight))
    second_hidden = second_act.astype(jnp.bfloat16)
    output_pre = matmul(second_hidden, outlet_weight)
    centred = output_pre - jnp.mean(output_pre, axis=-1, keepdims=True)
    inverse = lax.rsqrt(jnp.mean(centred * centred, axis=-1, keepdims=True) + EPS)
    normed = centred * inverse
    return (normed, (first_hidden, second_hidden, first_slope, second_slope, inverse))


def mlp_backward(
    upstream, inputs, entry_weight, middle_weight, outlet_weight, gain_vec, normed, saved
):
    first_hidden, second_hidden, first_slope, second_slope, inverse = saved
    gain_grad = jnp.sum(upstream * normed, axis=0)
    scaled = upstream * gain_vec
    output_grad = inverse * (
        scaled
        - jnp.mean(scaled, axis=-1, keepdims=True)
        - normed * jnp.mean(scaled * normed, axis=-1, keepdims=True)
    )
    output_grad = output_grad.astype(jnp.bfloat16)
    outlet_grad = contract(second_hidden, output_grad)
    second_grad = (transposed(output_grad, outlet_weight) * second_slope).astype(jnp.bfloat16)
    middle_grad = contract(first_hidden, second_grad)
    first_grad = (transposed(second_grad, middle_weight) * first_slope).astype(jnp.bfloat16)
    entry_grad = contract(inputs, first_grad)
    input_grad = transposed(first_grad, entry_weight)
    return (input_grad, (entry_grad, middle_grad, outlet_grad, gain_grad))


def one_hots(block_start, edge_offset):
    offsets = edge_offset.reshape(block_start.shape[0], -1)
    columns = jnp.arange(WINDOW, dtype=jnp.int32)
    return (offsets[:, :, None] == columns[None, None, :]).astype(jnp.bfloat16)


def pick_near(table, selector, block_start):
    windows = jax.vmap(lambda first_row: lax.dynamic_slice_in_dim(table, first_row, WINDOW, 0))(
        block_start
    )
    picked = jnp.einsum("bew,bwh->beh", selector, windows, preferred_element_type=jnp.float32)
    return picked.reshape(-1, table.shape[1])


def add_near(values, selector, block_start, node_rows):
    feature = values.shape[1]
    blocks = values.reshape(block_start.shape[0], -1, feature)
    partial_sums = jnp.einsum("bew,beh->bwh", selector, blocks, preferred_element_type=jnp.float32)
    targets = (block_start[:, None] + jnp.arange(WINDOW, dtype=jnp.int32)[None, :]).reshape(-1)
    return (
        jnp.zeros((node_rows, feature), jnp.float32)
        .at[targets]
        .add(partial_sums.reshape(-1, feature))
    )


def fetch(border):
    gathered = lax.all_gather(border, "sub", axis=0, tiled=True)
    return extended_2(gathered, (("dom", 0),), gathered.shape[0])


def give_back(slot_sums):
    feature = slot_sums.shape[1]
    layer_rows = slot_sums.shape[0] // 3
    blocks = slot_sums.reshape(3, layer_rows, feature)
    outer_pair = jnp.concatenate([blocks[0], blocks[2]], axis=0)
    padded = extended_2(outer_pair, (("dom", 0),), layer_rows)
    own_sums = blocks[1] + padded[:layer_rows] + padded[3 * layer_rows :]
    return lax.psum_scatter(own_sums, "sub", scatter_dimension=0, tiled=True)


def per_device(
    node_state,
    edge_state,
    edge_count,
    block_start,
    edge_offset,
    edge_other,
    send_index,
    edge_entry,
    edge_middle,
    edge_outlet,
    edge_gain,
    node_entry,
    node_middle,
    node_outlet,
    node_gain,
    node_cotangent,
    edge_cotangent,
):
    node_rows, feature = node_state.shape
    edge_rows = edge_state.shape[0]
    is_live = (jnp.arange(edge_rows, dtype=jnp.int32) < edge_count[0]).astype(jnp.float32)[:, None]
    selector = one_hots(block_start, edge_offset)
    near_rows = pick_near(node_state, selector, block_start).astype(jnp.bfloat16)
    halo_rows = fetch(node_state[send_index])
    extended = jnp.concatenate([node_state, halo_rows], axis=0)
    ext_rows = extended.shape[0]
    far_rows = extended[edge_other]
    edge_inputs = jnp.concatenate([edge_state, near_rows, far_rows], axis=1)
    edge_normed, edge_saved = mlp_forward(edge_inputs, edge_entry, edge_middle, edge_outlet)
    new_edges = (edge_state.astype(jnp.float32) + is_live * edge_gain * edge_normed).astype(
        jnp.bfloat16
    )
    messages = new_edges * is_live.astype(jnp.bfloat16)
    partial_totals = add_near(messages, selector, block_start, node_rows)
    spread = (
        jnp.zeros((ext_rows, feature), jnp.float32).at[edge_other].add(messages.astype(jnp.float32))
    )
    partial_totals = partial_totals + spread[:node_rows]
    partial_totals = partial_totals.at[send_index].add(give_back(spread[node_rows:]))
    totals = lax.psum(partial_totals, "inner")
    node_inputs = jnp.concatenate([node_state, totals.astype(jnp.bfloat16)], axis=1)
    node_normed, node_saved = mlp_forward(node_inputs, node_entry, node_middle, node_outlet)
    own_new = (node_state.astype(jnp.float32) + node_gain * node_normed).astype(jnp.bfloat16)
    node_upstream = node_cotangent.astype(jnp.float32)
    node_input_grad, node_weight_grads = mlp_backward(
        node_upstream,
        node_inputs,
        node_entry,
        node_middle,
        node_outlet,
        node_gain,
        node_normed,
        node_saved,
    )
    own_pulls = node_input_grad[:, feature:].astype(jnp.bfloat16)
    direct = node_upstream + node_input_grad[:, :feature]
    near_pulls = pick_near(own_pulls, selector, block_start)
    far_table = jnp.concatenate([own_pulls, fetch(own_pulls[send_index])], axis=0)
    far_pulls = far_table[edge_other].astype(jnp.float32)
    edge_upstream = edge_cotangent.astype(jnp.float32) + is_live * (near_pulls + far_pulls)
    edge_input_grad, edge_weight_grads = mlp_backward(
        is_live * edge_upstream,
        edge_inputs,
        edge_entry,
        edge_middle,
        edge_outlet,
        edge_gain,
        edge_normed,
        edge_saved,
    )
    edge_adjoint = (edge_upstream + edge_input_grad[:, :feature]).astype(jnp.bfloat16)
    near_grad = edge_input_grad[:, feature : 2 * feature].astype(jnp.bfloat16)
    far_grad = edge_input_grad[:, 2 * feature :].astype(jnp.bfloat16)
    back_part = add_near(near_grad, selector, block_start, node_rows)
    back_spread = (
        jnp.zeros((ext_rows, feature), jnp.float32).at[edge_other].add(far_grad.astype(jnp.float32))
    )
    back_part = back_part + back_spread[:node_rows]
    back_part = back_part.at[send_index].add(give_back(back_spread[node_rows:]))
    node_adjoint = (lax.psum(back_part, "inner") + direct).astype(jnp.bfloat16)
    edge_sums = lax.psum(
        (edge_weight_grads[0], edge_weight_grads[1], edge_weight_grads[2], edge_weight_grads[3]),
        ("dom", "sub", "inner"),
    )
    node_sums = lax.psum(
        (node_weight_grads[0], node_weight_grads[1], node_weight_grads[2], node_weight_grads[3]),
        ("dom", "sub"),
    )
    block_total = lax.axis_size("dom") * lax.axis_size("sub")
    edge_scale = 1.0 / math.sqrt(edge_rows * block_total * lax.axis_size("inner"))
    node_scale = 1.0 / math.sqrt(node_rows * block_total)
    edge_gradient = jnp.concatenate([edge_sums[0], edge_sums[1], edge_sums[2]], axis=0) * edge_scale
    node_gradient = jnp.concatenate([node_sums[0], node_sums[1], node_sums[2]], axis=0) * node_scale
    gain_gradient = jnp.stack([edge_sums[3] * edge_scale, node_sums[3] * node_scale])
    return (
        own_new,
        new_edges,
        node_adjoint,
        edge_adjoint,
        edge_gradient,
        node_gradient,
        gain_gradient,
    )


def solution(mesh):
    return jax.shard_map(
        per_device,
        mesh=mesh,
        in_specs=(
            P(("groups", "dom", "sub"), None),
            P(("groups", "dom", "sub", "inner"), None),
            P(("groups", "dom", "sub", "inner")),
            P(("groups", "dom", "sub", "inner")),
            P(("groups", "dom", "sub", "inner")),
            P(("groups", "dom", "sub", "inner")),
            P(("groups", "dom", "sub")),
            P(),
            P(),
            P(),
            P(),
            P(),
            P(),
            P(),
            P(),
            P(("groups", "dom", "sub"), None),
            P(("groups", "dom", "sub", "inner"), None),
        ),
        out_specs=(
            P(("groups", "dom", "sub"), None),
            P(("groups", "dom", "sub", "inner"), None),
            P(("groups", "dom", "sub"), None),
            P(("groups", "dom", "sub", "inner"), None),
            P("groups", None),
            P("groups", None),
            P("groups", None),
        ),
        check_vma=False,
    )
```

profile of v0, /device:TPU:0, one launch (start us, length us, event | category | flops | bytes accessed | tf_op | source)
XLA Modules:
  0.0 372.2 jit_solution(9850722264546121267)
XLA Ops:
  9.6 5.8 %all-gather = bf16[512,128]{1,0:T(8,128)(2,1)S(1)} all-gather(bf16[256,128]{1,0:T(8,128)(2,1)S(1)} %gather_fusion), channel_id=2, replica_groups=mesh['groups'=2,'dom'=4,'sub'=2,'inner'=2] {'sub'}, dimensions={0}, use_global_device_ids=true | all-gather | bytes 196608 | tf_op jit(solution)/shard_map/all_gather | solution.py:112
  16.7 4.7 %collective-permute-start = (bf16[512,128]{1,0:T(8,128)(2,1)S(1)}, bf16[512,128]{1,0:T(8,128)(2,1)S(1)}, u32[]{:S(2)}, u32[]{:S(2)}) collective-permute-start(bf16[512,128]{1,0:T(8,128)(2,1)S(1)} %all-gather), channel_id=1, source_target_pairs={{0,4},{4,8},{8,12},{1,5},{5,9},{9,13},{2,6},{6,10},{10,14},{3,7},{... | collective-permute-start | bytes 393224 | tf_op jit(solution)/shard_map/ppermute | solution.py:22
  23.5 12.2 %while.2 = (s32[]{:T(128)}, bf16[512,128]{1,0:T(8,128)(2,1)}, s32[6,2]{0,1:T(2,128)S(1)}, bf16[6,128,128]{2,1,0:T(8,128)(2,1)S(1)}, s32[]{:T(128)}) while((s32[]{:T(128)}, bf16[512,128]{1,0:T(8,128)(2,1)}, s32[6,2]{0,1:T(2,128)S(1)}, bf16[6,128,128]{2,1,0:T(8,128)(2,1)S(1)}, s32[]{:T(128)}) %tuple.52), condition=%wide.while_cond, body=%wide.while_body.sunk | while | flops 2 | bytes 65641 | solution.py:92
  37.8 3.2 gather_fusion.1
  45.4 2.0 broadcast_multiply_fusion
  47.4 9.0 %scatter_custom_fusion = f32[2048,128]{1,0:T(8,128)S(1)} fusion(s32[1536]{0:T(1024)S(1)} %compare_select_fusion, bf16[1536,128]{1,0:T(8,128)(2,1)S(1)} %get-tuple-element.66, f32[]{:T(128)} %constant.9.clone.1), kind=kCustom, calls=%fused_computation.34 | custom fusion | flops 393216 | bytes 1441796 | tf_op jit(solution)/shard_map/scatter-add | solution.py:162
  57.2 3.9 %collective-permute-start.2 = (f32[512,128]{1,0:T(8,128)}, f32[512,128]{1,0:T(8,128)S(1)}, u32[]{:S(2)}, u32[]{:S(2)}) collective-permute-start(f32[512,128]{1,0:T(8,128)} %get-tuple-element.74), channel_id=1, source_target_pairs={{0,4},{4,8},{8,12},{1,5},{5,9},{9,13},{2,6},{6,10},{10,14},{3,7},{... | collective-permute-start | bytes 786440 | tf_op jit(solution)/shard_map/ppermute | solution.py:22
  62.7 2.6 collective-permute-done.2
  65.3 4.2 %collective-permute-done.3 = f32[512,128]{1,0:T(8,128)} collective-permute-done((f32[512,128]{1,0:T(8,128)S(1)}, f32[512,128]{1,0:T(8,128)}, u32[]{:S(2)}, u32[]{:S(2)}) %collective-permute-start.3) | collective-permute-done | bytes 262176 | tf_op jit(solution)/shard_map/ppermute | solution.py:24
  71.6 6.2 %scatter_fusion = f32[512,128]{1,0:T(8,128)S(1)} fusion(f32[512,128]{1,0:T(8,128)S(1)} %get-tuple-element.73, s32[768]{0:T(1024)S(1)} %fusion.40, f32[768,128]{1,0:T(8,128)S(1)} %bitcast.79), kind=kCustom, calls=%fused_computation.5 | custom fusion | flops 98304 | bytes 1182720 | tf_op jit(solution)/shard_map/scatter-add | solution.py:107
  77.8 4.4 %reduce-scatter.3.cloned.1.call-done = f32[256,128]{1,0:T(8,128)} async-done(((f32[512,128]{1,0:T(8,128)}), f32[256,128]{1,0:T(8,128)}) %reduce-scatter.3.cloned.1.call-update) | async-done | bytes 131088 | tf_op jit(solution)/shard_map/reduce_scatter | solution.py:123
  82.2 2.4 scatter_fusion.1
  84.7 4.2 %all-reduce.13 = bf16[512,128]{1,0:T(8,128)(2,1)S(1)} all-reduce(f32[512,128]{1,0:T(8,128)S(1)} %scatter_fusion.1), channel_id=1, replica_groups=mesh['groups'=2,'dom'=4,'sub'=2,'inner'=2] {'inner'}, use_global_device_ids=true, to_apply=%region_6.0 | all-reduce | flops 65536 | bytes 393216 | tf_op jit(solution)/shard_map/psum | solution.py:166
  94.1 5.0 %all-gather.1 = bf16[512,128]{1,0:T(8,128)(2,1)S(1)} all-gather(bf16[256,128]{1,0:T(8,128)(2,1)S(1)} %gather_fusion.2), channel_id=3, replica_groups=mesh['groups'=2,'dom'=4,'sub'=2,'inner'=2] {'sub'}, dimensions={0}, use_global_device_ids=true | all-gather | bytes 196608 | tf_op jit(solution)/shard_map/all_gather | solution.py:112
  100.4 5.4 %collective-permute-start.4 = (bf16[512,128]{1,0:T(8,128)(2,1)S(1)}, bf16[512,128]{1,0:T(8,128)(2,1)}, u32[]{:S(2)}, u32[]{:S(2)}) collective-permute-start(bf16[512,128]{1,0:T(8,128)(2,1)S(1)} %all-gather.1), channel_id=1, source_target_pairs={{0,4},{4,8},{8,12},{1,5},{5,9},{9,13},{2,6},{6,10},{10,14},{3,7},{... | collective-permute-start | bytes 393224 | tf_op jit(solution)/shard_map/ppermute | solution.py:22
  105.8 7.7 %while.3 = (s32[]{:T(128)}, bf16[512,128]{1,0:T(8,128)(2,1)S(1)}, s32[6,2]{0,1:T(2,128)S(1)}, bf16[6,128,128]{2,1,0:T(8,128)(2,1)S(1)}, s32[]{:T(128)}) while((s32[]{:T(128)}, bf16[512,128]{1,0:T(8,128)(2,1)S(1)}, s32[6,2]{0,1:T(2,128)S(1)}, bf16[6,128,128]{2,1,0:T(8,128)(2,1)S(1)}, s32[]{:T(128)}) %tuple.70), condition=%wide.while_cond.1, body=%wide.while_body.1.sunk | while | flops 2 | bytes 65641 | solution.py:92
  114.8 4.1 %gather_fusion.3 = bf16[1536,128]{1,0:T(8,128)(2,1)} fusion(bf16[2048,128]{1,0:T(8,128)(2,1)S(1)} %pad_maximum_fusion.2, s32[2048]{0:T(1024)S(1)} %pad_clamp_fusion), kind=kCustom, calls=%fused_computation.3 | custom fusion | bytes 792576 | tf_op jit(solution)/shard_map/gather | solution.py:185
  118.9 3.1 multiply_reduce_fusion
  125.0 2.2 fusion.51
  127.3 9.4 %scatter_custom_fusion.3 = f32[2048,128]{1,0:T(8,128)S(1)} fusion(s32[1536]{0:T(1024)} %copy-done.33, f32[]{:T(128)} %constant.9.clone.1, bf16[1536,384]{1,0:T(8,128)(2,1)} %get-tuple-element.90), kind=kCustom, calls=%fused_computation.30 | custom fusion | flops 393216 | bytes 1442304 | tf_op jit(solution)/shard_map/scatter-add | solution.py:202
  137.5 2.7 collective-permute-start.6
  141.5 20.8 %psum.79 = f32[128]{0:T(128)S(1)} all-reduce(f32[128]{0:T(128)S(1)} %copy-done.37), channel_id=1, replica_groups=mesh['groups'=2,'dom'=4,'sub'=2,'inner'=2] {'dom','sub'}, use_global_device_ids=true, to_apply=%region_27.0 | all-reduce | flops 128 | bytes 1024 | tf_op jit(solution)/shard_map/psum | solution.py:211
  163.3 1.7 fusion.34
  166.1 1.8 fusion.55
  170.8 2.1 fusion.4
  174.4 29.6 %psum.78 = f32[128]{0:T(128)S(1)} all-reduce(f32[128]{0:T(128)S(1)} %copy-done.38), channel_id=1, replica_groups=mesh['groups'=2,'dom'=4,'sub'=2,'inner'=2] {'dom','sub','inner'}, use_global_device_ids=true, to_apply=%region_25.0 | all-reduce | flops 128 | bytes 1024 | tf_op jit(solution)/shard_map/psum | solution.py:207
  205.0 6.2 %scatter_fusion.2 = f32[512,128]{1,0:T(8,128)S(1)} fusion(f32[512,128]{1,0:T(8,128)S(1)} %get-tuple-element.69, s32[768]{0:T(1024)S(1)} %fusion.40, f32[768,128]{1,0:T(8,128)S(1)} %bitcast.77), kind=kCustom, calls=%fused_computation.8 | custom fusion | flops 98304 | bytes 1182720 | tf_op jit(solution)/shard_map/scatter-add | solution.py:107
  211.2 2.4 scatter_fusion.3
  215.0 34.1 %all-reduce.12.cloned.1.call-done = (f32[128,128]{1,0:T(8,128)}, f32[128,128]{1,0:T(8,128)}, f32[256,128]{1,0:T(8,128)}) async-done(((f32[128,128]{1,0:T(8,128)}, f32[128,128]{1,0:T(8,128)}, f32[256,128]{1,0:T(8,128)}), (f32[128,128]{1,0:T(8,128)}, f32[128,128]{1,0:T(8,128)}, f32[256,128]{1,0:T(8,128)})) %all-reduce.12.cloned.1.call-update) | async-done | bytes 262160 | tf_op jit(solution)/shard_map/psum | solution.py:211
  250.8 91.5 %all-reduce.10.cloned.1.call-done = (f32[128,128]{1,0:T(8,128)}, f32[128,128]{1,0:T(8,128)}, f32[384,128]{1,0:T(8,128)}) async-done(((f32[128,128]{1,0:T(8,128)}, f32[128,128]{1,0:T(8,128)}, f32[384,128]{1,0:T(8,128)}), (f32[128,128]{1,0:T(8,128)}, f32[128,128]{1,0:T(8,128)}, f32[384,128]{1,0:T(8,128)})) %all-reduce.10.cloned.1.call-update) | async-done | bytes 327696 | tf_op jit(solution)/shard_map/psum | solution.py:207
  342.3 1.7 maximum_multiply_fusion
  344.1 19.8 %all-reduce.8.cloned.1.call-done = f32[512,128]{0,1:T(8,128)} async-done(((f32[512,128]{0,1:T(8,128)}), f32[512,128]{0,1:T(8,128)}) %all-reduce.8.cloned.1.call-update) | async-done | bytes 262160 | tf_op jit(solution)/shard_map/psum | solution.py:206
  (213 shorter events, 60.4 us)
Async XLA Ops:
  7.2 33.9 %copy-start = (bf16[384,128]{1,0:T(8,128)(2,1)S(1)}, bf16[384,128]{1,0:T(8,128)(2,1)}, u32[]{:S(2)}) copy-start(bf16[384,128]{1,0:T(8,128)(2,1)} %param.24) | copy-start | bytes 294916
  7.2 75.1 %reduce-scatter.3.cloned.1.call-start = ((), (), s32[]{:S(2)}) async-start(), calls=%async_computation.2 | async-start | bytes 393216 | tf_op jit(solution)/shard_map/reduce_scatter | solution.py:123
  15.4 21.4 %collective-permute-start.1 = (bf16[512,128]{1,0:T(8,128)(2,1)S(1)}, bf16[512,128]{1,0:T(8,128)(2,1)S(1)}, u32[]{:S(2)}, u32[]{:S(2)}) collective-permute-start(bf16[512,128]{1,0:T(8,128)(2,1)S(1)} %all-gather), channel_id=1, source_target_pairs={{4,0},{8,4},{12,8},{5,1},{9,5},{13,9},{6,2},{10,6},{14,10},{7,3},{... | collective-permute-start | bytes 393224 | tf_op jit(solution)/shard_map/ppermute | solution.py:24
  16.7 20.1 %collective-permute-start = (bf16[512,128]{1,0:T(8,128)(2,1)S(1)}, bf16[512,128]{1,0:T(8,128)(2,1)S(1)}, u32[]{:S(2)}, u32[]{:S(2)}) collective-permute-start(bf16[512,128]{1,0:T(8,128)(2,1)S(1)} %all-gather), channel_id=1, source_target_pairs={{0,4},{4,8},{8,12},{1,5},{5,9},{9,13},{2,6},{6,10},{10,14},{3,7},{... | collective-permute-start | bytes 393224 | tf_op jit(solution)/shard_map/ppermute | solution.py:22
  23.4 24.0 %copy-start.33 = (s32[1536]{0:T(1024)}, s32[1536]{0:T(1024)S(1)}, u32[]{:S(2)}) copy-start(s32[1536]{0:T(1024)S(1)} %compare_select_fusion) | copy-start | bytes 18436
  36.1 4.9 %copy-start.13 = (bf16[6,256,128]{2,1,0:T(8,128)(2,1)}, bf16[6,256,128]{2,1,0:T(8,128)(2,1)S(1)}, u32[]{:S(2)}) copy-start(bf16[6,256,128]{2,1,0:T(8,128)(2,1)S(1)} %convolution_convert_fusion) | copy-start | bytes 1179652
  37.8 3.3 copy-start.15
  47.4 15.0 %copy-start.1 = (bf16[512,128]{1,0:T(8,128)(2,1)S(1)}, bf16[512,128]{1,0:T(8,128)(2,1)}, u32[]{:S(2)}) copy-start(bf16[512,128]{1,0:T(8,128)(2,1)} %get-tuple-element.189) | copy-start | bytes 393220
  47.4 15.2 %copy-start.25 = (bf16[512,128]{1,0:T(8,128)(2,1)S(1)}, bf16[512,128]{1,0:T(8,128)(2,1)}, u32[]{:S(2)}) copy-start(bf16[512,128]{1,0:T(8,128)(2,1)} %param.32) | copy-start | bytes 393220
  57.2 8.1 %collective-permute-start.2 = (f32[512,128]{1,0:T(8,128)}, f32[512,128]{1,0:T(8,128)S(1)}, u32[]{:S(2)}, u32[]{:S(2)}) collective-permute-start(f32[512,128]{1,0:T(8,128)} %get-tuple-element.74), channel_id=1, source_target_pairs={{0,4},{4,8},{8,12},{1,5},{5,9},{9,13},{2,6},{6,10},{10,14},{3,7},{... | collective-permute-start | bytes 786440 | tf_op jit(solution)/shard_map/ppermute | solution.py:22
  61.1 10.2 %copy-start.39 = (s32[6]{0:T(128)S(1)}, s32[6]{0:T(128)}, u32[]{:S(2)}) copy-start(s32[6]{0:T(128)} %param.20) | copy-start | bytes 76
  61.1 8.4 %collective-permute-start.3 = (f32[512,128]{1,0:T(8,128)S(1)}, f32[512,128]{1,0:T(8,128)}, u32[]{:S(2)}, u32[]{:S(2)}) collective-permute-start(f32[512,128]{1,0:T(8,128)S(1)} %get-tuple-element.75), channel_id=1, source_target_pairs={{4,0},{8,4},{12,8},{5,1},{9,5},{13,9},{6,2},{10,6},{14,10},{7,3},{... | collective-permute-start | bytes 786440 | tf_op jit(solution)/shard_map/ppermute | solution.py:24
  71.2 139.9 %reduce-scatter.5.cloned.1.call-start = ((), (), s32[]{:S(2)}) async-start(), calls=%async_computation.3 | async-start | bytes 393216 | tf_op jit(solution)/shard_map/reduce_scatter | solution.py:123
  77.8 11.0 %copy-start.31 = (bf16[256,128]{1,0:T(8,128)(2,1)S(1)}, bf16[256,128]{1,0:T(8,128)(2,1)}, u32[]{:S(2)}) copy-start(bf16[256,128]{1,0:T(8,128)(2,1)} %param.28) | copy-start | bytes 196612
  84.7 4.5 %copy-start.40 = (bf16[128,128]{1,0:T(8,128)(2,1)S(1)}, bf16[128,128]{1,0:T(8,128)(2,1)}, u32[]{:S(2)}) copy-start(bf16[128,128]{1,0:T(8,128)(2,1)} %param.29) | copy-start | bytes 98308
  99.1 14.8 %collective-permute-start.5 = (bf16[512,128]{1,0:T(8,128)(2,1)S(1)}, bf16[512,128]{1,0:T(8,128)(2,1)S(1)}, u32[]{:S(2)}, u32[]{:S(2)}) collective-permute-start(bf16[512,128]{1,0:T(8,128)(2,1)S(1)} %all-gather.1), channel_id=1, source_target_pairs={{4,0},{8,4},{12,8},{5,1},{9,5},{13,9},{6,2},{10,6},{14,10},{7,3},{... | collective-permute-start | bytes 393224 | tf_op jit(solution)/shard_map/ppermute | solution.py:24
  100.4 13.5 %collective-permute-start.4 = (bf16[512,128]{1,0:T(8,128)(2,1)S(1)}, bf16[512,128]{1,0:T(8,128)(2,1)}, u32[]{:S(2)}, u32[]{:S(2)}) collective-permute-start(bf16[512,128]{1,0:T(8,128)(2,1)S(1)} %all-gather.1), channel_id=1, source_target_pairs={{0,4},{4,8},{8,12},{1,5},{5,9},{9,13},{2,6},{6,10},{10,14},{3,7},{... | collective-permute-start | bytes 393224 | tf_op jit(solution)/shard_map/ppermute | solution.py:22
  127.3 14.3 %copy-start.37 = (f32[128]{0:T(128)S(1)}, f32[128]{0:T(128)}, u32[]{:S(2)}) copy-start(f32[128]{0:T(128)} %get-tuple-element.40) | copy-start | bytes 1540
  127.3 35.1 %copy-start.24 = (bf16[512,128]{1,0:T(8,128)(2,1)S(1)}, bf16[512,128]{1,0:T(8,128)(2,1)}, u32[]{:S(2)}) copy-start(bf16[512,128]{1,0:T(8,128)(2,1)} %copy-done.23) | copy-start | bytes 393220
  127.3 35.1 %copy-start.30 = (bf16[512,128]{1,0:T(8,128)(2,1)S(1)}, bf16[512,128]{1,0:T(8,128)(2,1)}, u32[]{:S(2)}) copy-start(bf16[512,128]{1,0:T(8,128)(2,1)} %copy-done.29) | copy-start | bytes 393220
  137.5 25.8 %collective-permute-start.6 = (f32[512,128]{1,0:T(8,128)}, f32[512,128]{1,0:T(8,128)S(1)}, u32[]{:S(2)}, u32[]{:S(2)}) collective-permute-start(f32[512,128]{1,0:T(8,128)} %get-tuple-element.70), channel_id=1, source_target_pairs={{0,4},{4,8},{8,12},{1,5},{5,9},{9,13},{2,6},{6,10},{10,14},{3,7},{... | collective-permute-start | bytes 786440 | tf_op jit(solution)/shard_map/ppermute | solution.py:22
  140.2 23.0 %collective-permute-start.7 = (f32[512,128]{1,0:T(8,128)S(1)}, f32[512,128]{1,0:T(8,128)}, u32[]{:S(2)}, u32[]{:S(2)}) collective-permute-start(f32[512,128]{1,0:T(8,128)S(1)} %get-tuple-element.71), channel_id=1, source_target_pairs={{4,0},{8,4},{12,8},{5,1},{9,5},{13,9},{6,2},{10,6},{14,10},{7,3},{... | collective-permute-start | bytes 786440 | tf_op jit(solution)/shard_map/ppermute | solution.py:24
  165.0 2.8 copy-start.7
  165.0 2.8 copy-start.9
  165.0 3.7 copy-start.3
  165.0 3.7 copy-start.5
  165.1 84.1 %all-reduce.12.cloned.1.call-start = ((), (), s32[]{:S(2)}) async-start(), calls=%async_computation.6 | async-start | bytes 524288 | tf_op jit(solution)/shard_map/psum | solution.py:211
  168.7 173.7 %all-reduce.10.cloned.1.call-start = ((), (), s32[]{:S(2)}) async-start(), calls=%async_computation.5 | async-start | bytes 655360 | tf_op jit(solution)/shard_map/psum | solution.py:207
  170.7 2.4 copy-start.12
  173.1 30.8 %copy-start.18 = (bf16[1536,128]{1,0:T(8,128)(2,1)S(1)}, bf16[1536,128]{1,0:T(8,128)(2,1)}, u32[]{:S(2)}) copy-start(bf16[1536,128]{1,0:T(8,128)(2,1)} %copy-done.17) | copy-start | bytes 1179652
  173.2 30.8 %copy-start.20 = (bf16[1536,128]{1,0:T(8,128)(2,1)S(1)}, bf16[1536,128]{1,0:T(8,128)(2,1)}, u32[]{:S(2)}) copy-start(bf16[1536,128]{1,0:T(8,128)(2,1)} %copy-done.19) | copy-start | bytes 1179652
  204.9 159.0 %all-reduce.8.cloned.1.call-start = ((), (), s32[]{:S(2)}) async-start(), calls=%async_computation.4 | async-start | bytes 524288 | tf_op jit(solution)/shard_map/psum | solution.py:206
  (26 other events, 35.1 us)
Sparse Core Ops, SparseCore 0:
  71.3 10.8 reduce-scatter.2
  165.2 8.8 reduce-scatter.4
  177.8 71.3 all-reduce.11
  253.7 88.5 all-reduce.9
  344.5 19.3 all-reduce.7
where the time goes:
time: 374 us; the launch traced here: 372 us
  waiting for transfers between devices  157 us (42%)
  blocking collectives  65.4 us (17%)
  other arithmetic  58.6 us (16%)
  local copies, waits for them, and re-layouts  38.6 us (10%)
  starting transfers between devices  22.1 us (6%)
  between operations  15.3 us (4%)
  matrix products  15.2 us (4%)
    psum x1, waiting for transfers between devices, per_device(): lax.psum((edge_weight_grads[0], edge_weight_grads[1], edge_weight_grads[2...  91.5 us
    psum x1, waiting for transfers between devices, per_device(): lax.psum((node_weight_grads[0], node_weight_grads[1], node_weight_grads[2...  34.1 us
    psum x1, blocking collectives, per_device(): lax.psum((edge_weight_grads[0], edge_weight_grads[1], edge_weight_grads[2...  29.6 us
    psum x1, blocking collectives, per_device(): lax.psum((node_weight_grads[0], node_weight_grads[1], node_weight_grads[2...  20.8 us
    psum x1, waiting for transfers between devices, per_device(): node_adjoint = (lax.psum(back_part, 'inner') + direct).astype(jnp.bfloat16)  19.8 us
    gather x36, local copies, waits for them, and re-layouts  19.7 us
    scatter-add x2, other arithmetic, per_device(): jnp.zeros((ext_rows, feature), jnp.float32).at[edge_other]  18.5 us
    ppermute x4, starting transfers between devices, extended_2(): lax.ppermute(tail, axis, [(i, (i + 1) % count) for i in range(ends)])  16.7 us
  transfers between devices with their start and end apart: 13, of which 6 were waited for; matrix products, arithmetic and copies ran while one was open for 14% of the time, Pallas kernels for 0%

commit v1 on v0

v1 whole, which is shorter than its diff:
```python
import math

import jax
import jax.numpy as jnp
from jax import lax
from jax.experimental import pallas as pl
from jax.experimental.pallas import tpu as pltpu
from jax.sharding import PartitionSpec as P

EPS = 1e-05
BF = jnp.bfloat16
F32 = jnp.float32
AXES = ("dom", "sub", "inner")
VMEM_LIMIT = 48 * 1024 * 1024


def mm(left, right):
    return jnp.dot(left, right, preferred_element_type=F32)


def mm_tn(left, right):
    return lax.dot_general(left, right, (((0,), (0,)), ((), ())), preferred_element_type=F32)


def mm_nt(left, right):
    return lax.dot_general(left, right, (((1,), (1,)), ((), ())), preferred_element_type=F32)


def silu_pair(pre_act):
    logistic = jax.nn.sigmoid(pre_act)
    act = pre_act * logistic
    return act, logistic + act * (1.0 - logistic)


def layer_norm(output_pre):
    centred = output_pre - jnp.mean(output_pre, axis=-1, keepdims=True)
    inverse = lax.rsqrt(jnp.mean(centred * centred, axis=-1, keepdims=True) + EPS)
    return centred * inverse, inverse


def norm_backward(scaled, normed, inverse):
    return inverse * (
        scaled
        - jnp.mean(scaled, axis=-1, keepdims=True)
        - normed * jnp.mean(scaled * normed, axis=-1, keepdims=True)
    )


def hot_rows(index_row, rows, base=0):
    place = lax.broadcasted_iota(jnp.int32, (rows, index_row.shape[1]), 0) + base
    return jnp.where(place == index_row, 1.0, 0.0).astype(BF)


def hot_cols(index_col, cols, base=0):
    place = lax.broadcasted_iota(jnp.int32, (index_col.shape[0], cols), 1) + base
    return jnp.where(place == index_col, 1.0, 0.0).astype(BF)


def column(row):
    wide = jnp.broadcast_to(row, (8, row.shape[1]))
    return jnp.transpose(wide)[:, :1]


class Layout:
    def __init__(self, nodes, send):
        self.nodes, self.send = nodes, send
        self.sub = lax.axis_size("sub")
        self.dom = lax.axis_size("dom")
        self.groups = [(a, x) for a in range(3) for x in range(self.sub)]
        self.remote = self.groups[1:]
        self.halo = len(self.remote) * send

    def place(self, other):
        d, t = lax.axis_index("dom"), lax.axis_index("sub")
        slot = jnp.maximum(other - self.nodes, 0)
        layer = slot // (self.sub * self.send)
        rest = slot - layer * (self.sub * self.send)
        peer = rest // self.send
        k = rest - peer * self.send
        upper = (layer == 2).astype(jnp.int32)
        even = 1 - lax.rem(d, 2)
        swap = jnp.where(layer == 1, 0, jnp.where(upper == even, 1, 2))
        row = self.nodes + (swap * self.sub + (peer ^ t)) * self.send + k
        return jnp.where(other < self.nodes, other, row)

    def exchange(self, arrays):
        inner = lax.axis_size("inner")
        out = []
        for (a, x), value in zip(self.remote, arrays):
            pairs = []
            for d in range(self.dom):
                other = d if a == 0 else (d ^ 1 if a == 1 else ((d + 1) ^ 1) - 1)
                if not 0 <= other < self.dom:
                    continue
                for t in range(self.sub):
                    for i in range(inner):
                        pairs.append(
                            (
                                (d * self.sub + t) * inner + i,
                                (other * self.sub + (t ^ x)) * inner + i,
                            )
                        )
            out.append(lax.ppermute(value, AXES, pairs))
        return out


def swap_axis(value, axis, mask):
    count = lax.axis_size(axis)
    return lax.ppermute(value, axis, [(j, j ^ mask) for j in range(count)])


def call(body, outs, *args, smem=(), scratch=(), flops=0):
    specs = [
        pl.BlockSpec(memory_space=pltpu.SMEM if j in smem else pltpu.VMEM)
        for j in range(len(args))
    ]
    size = sum(math.prod(a.shape) * a.dtype.itemsize for a in (*args, *outs))
    return pl.pallas_call(
        body,
        out_shape=outs,
        in_specs=specs,
        out_specs=[pl.BlockSpec(memory_space=pltpu.VMEM) for _ in outs],
        scratch_shapes=list(scratch),
        compiler_params=pltpu.CompilerParams(vmem_limit_bytes=VMEM_LIMIT),
        cost_estimate=pl.CostEstimate(flops=flops, bytes_accessed=size, transcendentals=0),
    )(*args)


def shape(rows, cols, dtype):
    return jax.ShapeDtypeStruct((rows, cols), dtype)


def border_kernel(send_ref, table_ref, out_ref):
    hot = hot_rows(send_ref[...], table_ref.shape[0])
    out_ref[...] = mm_tn(hot, table_ref[...]).astype(BF)


def near_row(offset_ref, start_ref, b):
    return offset_ref[b : b + 1, :] + start_ref[b]


def live_column(count_ref, b, size):
    return lax.broadcasted_iota(jnp.int32, (size, 1), 0) + b * size < count_ref[0]


def per_device(
    node_state,
    edge_state,
    edge_count,
    block_start,
    edge_offset,
    edge_other,
    send_index,
    edge_entry,
    edge_middle,
    edge_outlet,
    edge_gain,
    node_entry,
    node_middle,
    node_outlet,
    node_gain,
    node_cotangent,
    edge_cotangent,
):
    nodes, feat = node_state.shape
    edges = edge_state.shape[0]
    blocks = block_start.shape[0]
    size = edges // blocks
    send = send_index.shape[0]
    lay = Layout(nodes, send)
    remote = len(lay.remote)
    halo_base = nodes + send
    f = feat

    offset = edge_offset.reshape(blocks, size)
    other = edge_other.reshape(blocks, size)
    sends = send_index.reshape(1, send)
    gain_e = edge_gain.reshape(1, f)
    gain_n = node_gain.reshape(1, f)

    (border,) = call(border_kernel, [shape(send, f, BF)], sends, node_state)
    halo = lay.exchange([border] * remote)

    def edge_local(
        off_ref, oth_ref, start_ref, node_ref, border_ref, edge_ref, entry_ref,
        near_ref, far_ref, pre_ref, place_ref,
    ):
        place_ref[...] = lay.place(oth_ref[...])
        for b in range(blocks):
            rows = pl.ds(b * size, size)
            near = hot_cols(column(near_row(off_ref, start_ref, b)), nodes)
            near = mm(near, node_ref[...]).astype(BF)
            far = hot_cols(column(place_ref[b : b + 1, :]), nodes + send)
            far = mm(far[:, :nodes], node_ref[...]) + mm(far[:, nodes:], border_ref[...])
            near_ref[rows, :] = near
            far_ref[rows, :] = far.astype(BF)
            pre_ref[rows, :] = mm(edge_ref[rows, :], entry_ref[:f, :]) + mm(
                near, entry_ref[f : 2 * f, :]
            )

    near_rows, far_own, pre_own, place = call(
        edge_local,
        [
            shape(edges, f, BF),
            shape(edges, f, BF),
            shape(edges, f, F32),
            shape(blocks, size, jnp.int32),
        ],
        offset, other, block_start, node_state, border, edge_state, edge_entry,
        smem=(2,),
        flops=2 * edges * f * (2 * nodes + send + 2 * f),
    )

    def edge_forward(*refs):
        (place_ref, count_ref, edge_ref, far_own_ref, pre_ref, entry_ref, middle_ref,
         outlet_ref, gain_ref) = refs[:9]
        halo_refs = refs[9 : 9 + remote]
        (new_ref, message_ref, far_ref, h1_ref, h2_ref, s1_ref, s2_ref, normed_ref,
         inverse_ref) = refs[9 + remote : 18 + remote]
        slot_refs = refs[18 + remote : 18 + 2 * remote]
        table, sums = refs[18 + 2 * remote :]
        for j in range(remote):
            table[pl.ds(j * send, send), :] = halo_refs[j][...]
        for b in range(blocks):
            rows = pl.ds(b * size, size)
            place_b = place_ref[b : b + 1, :]
            hot = hot_cols(column(place_b), lay.halo, halo_base)
            far = (mm(hot, table[...]) + far_own_ref[rows, :].astype(F32)).astype(BF)
            far_ref[rows, :] = far
            act, slope = silu_pair(pre_ref[rows, :] + mm(far, entry_ref[2 * f :, :]))
            h1 = act.astype(BF)
            h1_ref[rows, :] = h1
            s1_ref[rows, :] = slope
            act, slope = silu_pair(mm(h1, middle_ref[...]))
            h2 = act.astype(BF)
            h2_ref[rows, :] = h2
            s2_ref[rows, :] = slope
            normed, inverse = layer_norm(mm(h2, outlet_ref[...]))
            normed_ref[rows, :] = normed
            inverse_ref[rows, :] = inverse
            live = jnp.where(live_column(count_ref, b, size), 1.0, 0.0)
            state = edge_ref[rows, :].astype(F32)
            new = (state + live * gain_ref[...] * normed).astype(BF)
            new_ref[rows, :] = new
            message = (new.astype(F32) * live).astype(BF)
            message_ref[rows, :] = message
            part = mm(hot_rows(place_b, lay.halo, halo_base), message)
            if b == 0:
                sums[...] = part
            else:
                sums[...] += part
        for j in range(remote):
            slot_refs[j][...] = sums[pl.ds(j * send, send), :].astype(BF)

    edge_outs = call(
        edge_forward,
        [
            shape(edges, f, BF),
            shape(edges, f, BF),
            shape(edges, f, BF),
            shape(edges, f, BF),
            shape(edges, f, BF),
            shape(edges, f, F32),
            shape(edges, f, F32),
            shape(edges, f, F32),
            shape(edges, 1, F32),
        ]
        + [shape(send, f, BF)] * remote,
        place, edge_count, edge_state, far_own, pre_own, edge_entry, edge_middle, edge_outlet,
        gain_e, *halo,
        smem=(1,),
        scratch=[pltpu.VMEM((lay.halo, f), BF), pltpu.VMEM((lay.halo, f), F32)],
        flops=2 * edges * f * (2 * lay.halo + 3 * f),
    )
    new_edges, message, far_rows, h1, h2, s1, s2, normed, inverse = edge_outs[:9]
    received = lay.exchange(edge_outs[9:])

    def local_sums(off_ref, place_ref, start_ref, send_ref, near_ref, far_ref, out_ref):
        slot = jnp.zeros((send, f), F32)
        total = jnp.zeros((nodes, f), F32)
        for b in range(blocks):
            rows = pl.ds(b * size, size)
            place_b = place_ref[b : b + 1, :]
            total += mm(hot_rows(near_row(off_ref, start_ref, b), nodes), near_ref[rows, :])
            hot = hot_rows(place_b, nodes + send)
            total += mm(hot[:nodes], far_ref[rows, :])
            slot += mm(hot[nodes:], far_ref[rows, :])
        out_ref[...] = total + mm(hot_rows(send_ref[...], nodes), slot.astype(BF))

    def gather_back(near, far):
        (out,) = call(
            local_sums,
            [shape(nodes, f, F32)],
            offset, place, block_start, sends, near, far,
            smem=(2,),
            flops=2 * edges * f * (2 * nodes + send),
        )
        return out

    def join_kernel(send_ref, own_ref, *refs):
        hot = hot_rows(send_ref[...], nodes)
        total = own_ref[...]
        for ref in refs[:-1]:
            total += mm(hot, ref[...])
        refs[-1][...] = total.astype(BF)

    def join(own, arrived):
        (out,) = call(
            join_kernel, [shape(nodes, f, BF)], sends, own, *arrived,
            flops=2 * nodes * send * f * remote,
        )
        return out, swap_axis(out, "inner", 1)

    part, part_other = join(gather_back(message, message), received)

    def node_kernel(
        part_ref, other_ref, node_ref, cot_ref, send_ref, entry_ref, middle_ref, outlet_ref,
        gain_ref, new_ref, pulls_ref, border_ref, direct_ref, weight_ref, gain_grad_ref,
    ):
        totals = (part_ref[...].astype(F32) + other_ref[...].astype(F32)).astype(BF)
        state = node_ref[...]
        act, s1n = silu_pair(mm(state, entry_ref[:f, :]) + mm(totals, entry_ref[f:, :]))
        h1n = act.astype(BF)
        act, s2n = silu_pair(mm(h1n, middle_ref[...]))
        h2n = act.astype(BF)
        normed_n, inverse_n = layer_norm(mm(h2n, outlet_ref[...]))
        new_ref[...] = (state.astype(F32) + gain_ref[...] * normed_n).astype(BF)
        up = cot_ref[...].astype(F32)
        og = norm_backward(up * gain_ref[...], normed_n, inverse_n).astype(BF)
        second = (mm_nt(og, outlet_ref[...]) * s2n).astype(BF)
        first = (mm_nt(second, middle_ref[...]) * s1n).astype(BF)
        pulls = mm_nt(first, entry_ref[f:, :]).astype(BF)
        pulls_ref[...] = pulls
        border_ref[...] = mm_tn(hot_rows(send_ref[...], nodes), pulls).astype(BF)
        direct_ref[...] = up + mm_nt(first, entry_ref[:f, :])
        weight_ref[:f, :] = mm_tn(state, first)
        weight_ref[f : 2 * f, :] = mm_tn(totals, first)
        weight_ref[2 * f : 3 * f, :] = mm_tn(h1n, second)
        weight_ref[3 * f :, :] = mm_tn(h2n, og)
        gain_grad_ref[...] = jnp.sum(up * normed_n, axis=0, keepdims=True)

    own_new, pulls, pull_border, direct, node_weights, node_gain_grad = call(
        node_kernel,
        [
            shape(nodes, f, BF),
            shape(nodes, f, BF),
            shape(send, f, BF),
            shape(nodes, f, F32),
            shape(4 * f, f, F32),
            shape(1, f, F32),
        ],
        part, part_other, node_state, node_cotangent, sends, node_entry, node_middle,
        node_outlet, gain_n,
        flops=2 * nodes * f * f * 12,
    )
    pull_halo = lay.exchange([pull_border] * remote)

    def pull_local(
        off_ref, place_ref, start_ref, count_ref, pulls_ref, border_ref, cot_ref, up_ref
    ):
        for b in range(blocks):
            rows = pl.ds(b * size, size)
            near = hot_cols(column(near_row(off_ref, start_ref, b)), nodes)
            far = hot_cols(column(place_ref[b : b + 1, :]), nodes + send)
            got = mm(near + far[:, :nodes], pulls_ref[...]) + mm(far[:, nodes:], border_ref[...])
            live = jnp.where(live_column(count_ref, b, size), 1.0, 0.0)
            up_ref[rows, :] = cot_ref[rows, :].astype(F32) + live * got

    (up_own,) = call(
        pull_local,
        [shape(edges, f, F32)],
        offset, place, block_start, edge_count, pulls, pull_border, edge_cotangent,
        smem=(2, 3),
        flops=2 * edges * f * (nodes + send),
    )

    def edge_backward(*refs):
        (place_ref, count_ref, up_own_ref, normed_ref, inverse_ref, s1_ref, s2_ref, entry_ref,
         middle_ref, outlet_ref, gain_ref) = refs[:11]
        halo_refs = refs[11 : 11 + remote]
        (adjoint_ref, near_ref, far_ref, first_ref, second_ref, og_ref, gain_grad_ref) = refs[
            11 + remote : 18 + remote
        ]
        slot_refs = refs[18 + remote : 18 + 2 * remote]
        table, sums = refs[18 + 2 * remote :]
        for j in range(remote):
            table[pl.ds(j * send, send), :] = halo_refs[j][...]
        gain_sum = jnp.zeros((1, f), F32)
        for b in range(blocks):
            rows = pl.ds(b * size, size)
            place_b = place_ref[b : b + 1, :]
            live = jnp.where(live_column(count_ref, b, size), 1.0, 0.0)
            hot = hot_cols(column(place_b), lay.halo, halo_base)
            up = up_own_ref[rows, :] + live * mm(hot, table[...])
            into = live * up
            normed_b = normed_ref[rows, :]
            gain_sum += jnp.sum(into * normed_b, axis=0, keepdims=True)
            og = norm_backward(into * gain_ref[...], normed_b, inverse_ref[rows, :]).astype(BF)
            og_ref[rows, :] = og
            second = (mm_nt(og, outlet_ref[...]) * s2_ref[rows, :]).astype(BF)
            second_ref[rows, :] = second
            first = (mm_nt(second, middle_ref[...]) * s1_ref[rows, :]).astype(BF)
            first_ref[rows, :] = first
            adjoint_ref[rows, :] = (up + mm_nt(first, entry_ref[:f, :])).astype(BF)
            near_ref[rows, :] = mm_nt(first, entry_ref[f : 2 * f, :]).astype(BF)
            far = mm_nt(first, entry_ref[2 * f :, :]).astype(BF)
            far_ref[rows, :] = far
            part = mm(hot_rows(place_b, lay.halo, halo_base), far)
            if b == 0:
                sums[...] = part
            else:
                sums[...] += part
        gain_grad_ref[...] = gain_sum
        for j in range(remote):
            slot_refs[j][...] = sums[pl.ds(j * send, send), :].astype(BF)

    back_outs = call(
        edge_backward,
        [shape(edges, f, BF)] * 6 + [shape(1, f, F32)] + [shape(send, f, BF)] * remote,
        place, edge_count, up_own, normed, inverse, s1, s2, edge_entry, edge_middle, edge_outlet,
        gain_e, *pull_halo,
        smem=(1,),
        scratch=[pltpu.VMEM((lay.halo, f), BF), pltpu.VMEM((lay.halo, f), F32)],
        flops=2 * edges * f * (2 * lay.halo + 5 * f),
    )
    edge_adjoint, near_grad, far_grad, first_grad, second_grad, output_grad = back_outs[:6]
    edge_gain_grad = back_outs[6]
    back_received = lay.exchange(back_outs[7:])

    subs = lax.axis_size("sub")
    doms = lax.axis_size("dom")
    inners = lax.axis_size("inner")
    weight_rows = 9 * f + 16
    unit = 16 * inners * subs
    weight_rows = -(-weight_rows // unit) * unit
    half = weight_rows // 2
    piece = half // subs
    block_total = doms * subs
    edge_scale = 1.0 / math.sqrt(edges * block_total * inners)
    node_scale = 1.0 / math.sqrt(nodes * block_total)

    def weight_kernel(
        edge_ref, near_ref, far_ref, h1_ref, h2_ref, first_ref, second_ref, og_ref, node_ref,
        edge_gain_ref, node_gain_ref, keep_ref, give_ref, acc,
    ):
        first = first_ref[...]
        acc[:f, :] = mm_tn(edge_ref[...], first).astype(BF)
        acc[f : 2 * f, :] = mm_tn(near_ref[...], first).astype(BF)
        acc[2 * f : 3 * f, :] = mm_tn(far_ref[...], first).astype(BF)
        acc[3 * f : 4 * f, :] = mm_tn(h1_ref[...], second_ref[...]).astype(BF)
        acc[4 * f : 5 * f, :] = mm_tn(h2_ref[...], og_ref[...]).astype(BF)
        acc[5 * f : 9 * f, :] = (node_ref[...] * 0.5).astype(BF)
        row = lax.broadcasted_iota(jnp.int32, (weight_rows - 9 * f, f), 0)
        gains = jnp.where(row == 0, edge_gain_ref[...], 0.0)
        gains = jnp.where(row == 1, node_gain_ref[...] * 0.5, gains)
        acc[9 * f :, :] = gains.astype(BF)
        me = lax.axis_index("inner")
        keep_ref[...] = acc[pl.ds(pl.multiple_of(me * half, 16), half), :]
        give_ref[...] = acc[pl.ds(pl.multiple_of((1 - me) * half, 16), half), :]

    keep, give = call(
        weight_kernel,
        [shape(half, f, BF)] * 2,
        edge_state, near_rows, far_rows, h1, h2, first_grad, second_grad, output_grad,
        node_weights, edge_gain_grad, node_gain_grad,
        scratch=[pltpu.VMEM((weight_rows, f), BF)],
        flops=2 * edges * f * f * 5,
    )

    def split_kernel(keep_ref, got_ref, *refs):
        out_refs, acc = refs[:-1], refs[-1]
        acc[...] = (keep_ref[...].astype(F32) + got_ref[...].astype(F32)).astype(BF)
        t = lax.axis_index("sub")
        for x in range(subs):
            out_refs[x][...] = acc[pl.ds(pl.multiple_of((t ^ x) * piece, 16), piece), :]

    pieces = call(
        split_kernel,
        [shape(piece, f, BF)] * subs,
        keep, swap_axis(give, "inner", 1),
        scratch=[pltpu.VMEM((half, f), BF)],
    )
    arrived = [pieces[0]] + [swap_axis(pieces[x], "sub", x) for x in range(1, subs)]

    def add_all(values):
        values = [v.astype(F32) for v in values]
        while len(values) > 1:
            values = [values[j] + values[j + 1] for j in range(0, len(values), 2)]
        return values[0]

    total = add_all(arrived)
    stride = 1
    while stride < doms:
        step = 4 if stride * 4 <= doms else 2
        sent = total.astype(BF)
        total = add_all(
            [sent] + [swap_axis(sent, "dom", stride * m) for m in range(1, step)]
        )
        stride *= step
    sent = total.astype(BF)
    own_pieces = [sent] + [swap_axis(sent, "sub", x) for x in range(1, subs)]

    def order_kernel(*refs):
        t = lax.axis_index("sub")
        for x in range(subs):
            refs[-1][pl.ds(pl.multiple_of((t ^ x) * piece, 16), piece), :] = refs[x][...]

    (own_half,) = call(order_kernel, [shape(half, f, BF)], *own_pieces)
    other_half = swap_axis(own_half, "inner", 1)

    def finish_kernel(own_ref, other_ref, edge_ref, node_ref, gain_ref, acc):
        me = lax.axis_index("inner")
        acc[pl.ds(pl.multiple_of(me * half, 16), half), :] = own_ref[...]
        acc[pl.ds(pl.multiple_of((1 - me) * half, 16), half), :] = other_ref[...]
        edge_ref[...] = acc[: 5 * f, :].astype(F32) * edge_scale
        node_ref[...] = acc[5 * f : 9 * f, :].astype(F32) * node_scale
        tail = acc[9 * f : 9 * f + 16, :].astype(F32)
        gain_ref[0:1, :] = tail[0:1, :] * edge_scale
        gain_ref[1:2, :] = tail[1:2, :] * node_scale

    edge_gradient, node_gradient, gain_gradient = call(
        finish_kernel,
        [shape(5 * f, f, F32), shape(4 * f, f, F32), shape(2, f, F32)],
        own_half, other_half,
        scratch=[pltpu.VMEM((weight_rows, f), BF)],
    )

    back, back_other = join(gather_back(near_grad, far_grad), back_received)
    node_adjoint = (back.astype(F32) + back_other.astype(F32) + direct).astype(BF)
    return (
        own_new,
        new_edges,
        node_adjoint,
        edge_adjoint,
        edge_gradient,
        node_gradient,
        gain_gradient,
    )


def solution(mesh):
    nodes = P(("groups", "dom", "sub"), None)
    edges = P(("groups", "dom", "sub", "inner"), None)
    slots = P(("groups", "dom", "sub", "inner"))
    return jax.shard_map(
        per_device,
        mesh=mesh,
        in_specs=(
            nodes,
            edges,
            slots,
            slots,
            slots,
            slots,
            P(("groups", "dom", "sub")),
            P(),
            P(),
            P(),
            P(),
            P(),
            P(),
            P(),
            P(),
            nodes,
            edges,
        ),
        out_specs=(
            nodes,
            edges,
            nodes,
            edges,
            P("groups", None),
            P("groups", None),
            P("groups", None),
        ),
        check_vma=False,
    )
```

time: 374 us -> 98.1 us (0.26)
  waiting for transfers between devices: 157 us -> 12.1 us
  blocking collectives: 65.4 us -> 0 us
  other arithmetic: 58.6 us -> 0.79 us
  local copies, waits for them, and re-layouts: 38.6 us -> 5.55 us
  Pallas kernels: 0 us -> 29.9 us
  starting transfers between devices: 22.1 us -> 47.5 us
  matrix products: 15.2 us -> 0 us
  between operations: 15.3 us -> 1.69 us
    psum x3 -> x0, waiting for transfers between devices: 145 us -> none  [the longest x1 91.5 us: per_device(): lax.psum((edge_weight_grads[0], edge_weight_grads[1], edge_weight_grads[2...]
    psum x3 -> x0, blocking collectives: 54.6 us -> none  [the longest x1 29.6 us: per_device(): lax.psum((edge_weight_grads[0], edge_weight_grads[1], edge_weight_grads[2...]
    scatter-add x6 -> x0, other arithmetic: 35.6 us -> none  [the longest x2 18.5 us: per_device(): jnp.zeros((ext_rows, feature), jnp.float32).at[edge_other]]
    pallas_call x0 -> x14, Pallas kernels: none -> 29.9 us  [call(): pl.pallas_call(body, out_shape=outs, in_specs=specs, out_specs=[pl.BlockS...]
    gather x40 -> x0, local copies, waits for them, and re-layouts: 29.5 us -> none
    ppermute x8 -> x29, starting transfers between devices: 21.9 us -> 47.5 us  [the longest x20 37 us: exchange(): out.append(lax.ppermute(value, AXES, pairs))]
    dot_general x22 -> x0, matrix products: 15.2 us -> none  [the longest x6 6.57 us: contract(): lax.dot_general(left, right, (((0,), (0,)), ((), ())), preferred_element_...]
    all_gather x2 -> x0, blocking collectives: 10.9 us -> none  [fetch(): gathered = lax.all_gather(border, 'sub', axis=0, tiled=True)]
  transfers between devices with their start and end apart: 13 -> 29, of which waited for: 6 -> 9; matrix products, arithmetic and copies ran while one was open for 14% -> 2% of each run, Pallas kernels for 0% -> 10%
where the time goes in v1:
time: 98.1 us; the launch traced here: 97.5 us
  starting transfers between devices  47.5 us (48%)
  Pallas kernels  29.9 us (30%)
  waiting for transfers between devices  12.1 us (12%)
  local copies, waits for them, and re-layouts  5.55 us (6%)
  between operations  1.69 us (2%)
    ppermute x20, starting transfers between devices, exchange(): out.append(lax.ppermute(value, AXES, pairs))  37 us
    pallas_call x14, Pallas kernels, call(): pl.pallas_call(body, out_shape=outs, in_specs=specs, out_specs=[pl.BlockS...  29.9 us
    ppermute x9, starting transfers between devices, swap_axis(): return lax.ppermute(value, axis, [(j, j ^ mask) for j in range(count)])  10.4 us
    ppermute x9, waiting for transfers between devices, swap_axis(): return lax.ppermute(value, axis, [(j, j ^ mask) for j in range(count)])  9.84 us
    unnamed x38, local copies, waits for them, and re-layouts  4.14 us
    ppermute x20, waiting for transfers between devices, exchange(): out.append(lax.ppermute(value, AXES, pairs))  2.26 us
  transfers between devices with their start and end apart: 29, of which 9 were waited for; matrix products, arithmetic and copies ran while one was open for 2% of the time, Pallas kernels for 10%

profile of v1, /device:TPU:0, one launch (start us, length us, event | category | flops | bytes accessed | tf_op | source)
XLA Modules:
  0.0 97.5 jit_solution(1205917058792991228)
XLA Ops:
  1.3 0.9 copy-done.3
  3.8 8.5 %collective-permute-start.2 = (bf16[256,128]{1,0:T(8,128)(2,1)S(1)}, bf16[256,128]{1,0:T(8,128)(2,1)S(1)}, u32[]{:S(2)}, u32[]{:S(2)}) collective-permute-start(bf16[256,128]{1,0:T(8,128)(2,1)S(1)} %shard_map.216.border_ref), channel_id=1, source_target_pairs={{0,6},{1,7},{2,4},{3,5},{4,2},{5,3},{6,0},{7,1},{8,14},{9,15},{10,... | collective-permute-start | bytes 196616 | tf_op jit(solution)/shard_map/ppermute | solution.py:103
  12.5 1.4 %collective-permute-start = (bf16[256,128]{1,0:T(8,128)(2,1)S(1)}, bf16[256,128]{1,0:T(8,128)(2,1)S(1)}, u32[]{:S(2)}, u32[]{:S(2)}) collective-permute-start(bf16[256,128]{1,0:T(8,128)(2,1)S(1)} %shard_map.216.border_ref), channel_id=1, source_target_pairs={{0,2},{1,3},{2,0},{3,1},{4,6},{5,7},{6,4},{7,5},{8,10},{9,11},{10,... | collective-permute-start | bytes 196616 | tf_op jit(solution)/shard_map/ppermute | solution.py:103
  15.2 0.7 reshape.31.oth_ref
  15.9 1.0 %copy-done = bf16[1536,128]{1,0:T(8,128)(2,1)S(1)} copy-done((bf16[1536,128]{1,0:T(8,128)(2,1)S(1)}, bf16[1536,128]{1,0:T(8,128)(2,1)}, u32[]{:S(2)}) %copy-start) | copy-done | bytes 393240
  16.9 3.2 %shard_map.217 = (bf16[1536,128]{1,0:T(8,128)(2,1)S(1)}, bf16[1536,128]{1,0:T(8,128)(2,1)S(1)}, f32[1536,128]{1,0:T(8,128)S(1)}, s32[6,256]{1,0:T(8,128)S(1)}) custom-call(s32[6,256]{1,0:T(8,128)S(1)} %reshape.30.off_ref, s32[6,256]{1,0:T(8,128)S(1)} %reshape.31.oth_ref, s32[6]{0:T(128)S(1)} %copy-done.6, bf16[512,128]{1,0:T(8,128)(2,1)S(1)} %copy-done.4, ...), custom_call_target="tpu_custom_call" | custom-call | flops 603979776 | bytes 2279448 | tf_op jit(solution)/shard_map/pallas_call | solution.py:118
  20.1 0.9 copy-done.18
  21.7 8.2 %shard_map.218 = (bf16[1536,128]{1,0:T(8,128)(2,1)}, bf16[1536,128]{1,0:T(8,128)(2,1)S(1)}, bf16[1536,128]{1,0:T(8,128)(2,1)S(1)}, bf16[1536,128]{1,0:T(8,128)(2...) custom-call(s32[6,256]{1,0:T(8,128)S(1)} %get-tuple-element.50.refs_, ...), custom_call_target="tpu_custom_call" | custom-call | flops 1157627904 | bytes 6730244 | tf_op jit(solution)/shard_map/pallas_call | solution.py:118
  30.6 1.9 %collective-permute-start.6 = (bf16[256,128]{1,0:T(8,128)(2,1)S(1)}, bf16[256,128]{1,0:T(8,128)(2,1)S(1)}, u32[]{:S(2)}, u32[]{:S(2)}) collective-permute-start(bf16[256,128]{1,0:T(8,128)(2,1)S(1)} %get-tuple-element.55), channel_id=1, source_target_pairs={{0,4},{1,5},{2,6},{3,7},{4,0},{5,1},{6,2},{7,3},{8,12},{9,13},{10,... | collective-permute-start | bytes 196616 | tf_op jit(solution)/shard_map/ppermute | solution.py:103
  32.5 0.9 collective-permute-start.7
  34.8 2.0 %shard_map.219.own_ref = f32[512,128]{1,0:T(8,128)S(1)} custom-call(s32[6,256]{1,0:T(8,128)S(1)} %reshape.30.off_ref, s32[6,256]{1,0:T(8,128)S(1)} %get-tuple-element.50.refs_0_.place_ref, s32[6]{0:T(128)S(1)} %copy-done.6, s32[1,256]{1,0:T(1,128)S(1)} %bitcast.4, bf16[1536,128]{1,0:T(8,128)(2,1)S(1)} %get-tuple-element.53.near_ref.far_ref, ...), custom_call_target="tpu_custom_call" | custom-call | flops 503316480 | bytes 1061912 | tf_op jit(solution)/shard_map/pallas_call | solution.py:118
  36.9 0.8 collective-permute-done.7.refs_2_
  38.3 1.3 %collective-permute-done.10.other_ref = bf16[512,128]{1,0:T(8,128)(2,1)S(1)} collective-permute-done((bf16[512,128]{1,0:T(8,128)(2,1)S(1)}, bf16[512,128]{1,0:T(8,128)(2,1)S(1)}, u32[]{:S(2)}, u32[]{:S(2)}) %collective-permute-start.10) | collective-permute-done | bytes 131104 | tf_op jit(solution)/shard_map/ppermute | solution.py:109
  39.6 1.5 %shard_map.221 = (bf16[512,128]{1,0:T(8,128)(2,1)}, bf16[512,128]{1,0:T(8,128)(2,1)S(1)}, bf16[256,128]{1,0:T(8,128)(2,1)S(1)}, f32[512,128]{1,0:T(8,128)S(1)}, ...) custom-call(bf16[512,128]{1,0:T(8,128)(2,1)S(1)} %shard_map.220.part_ref, ...), custom_call_target="tpu_custom_call" | custom-call | flops 201326592 | bytes 1509376 | tf_op jit(solution)/shard_map/pallas_call | solution.py:118
  41.2 0.8 collective-permute-start.15
  42.0 0.8 collective-permute-start.14
  42.9 13.8 %collective-permute-start.13 = (bf16[256,128]{1,0:T(8,128)(2,1)S(1)}, bf16[256,128]{1,0:T(8,128)(2,1)S(1)}, u32[]{:S(2)}, u32[]{:S(2)}) collective-permute-start(bf16[256,128]{1,0:T(8,128)(2,1)S(1)} %get-tuple-element.62.border_ref), channel_id=1, source_target_pairs={{0,6},{1,7},{2,4},{3,5},{4,2},{5,3},{6,0},{7,1},{8,14},{9,15},{10,... | collective-permute-start | bytes 196616 | tf_op jit(solution)/shard_map/ppermute | solution.py:103
  57.3 2.2 %shard_map.222.refs_2_ = f32[1536,128]{1,0:T(8,128)S(1)} custom-call(s32[6,256]{1,0:T(8,128)S(1)} %reshape.30.off_ref, s32[6,256]{1,0:T(8,128)S(1)} %get-tuple-element.50.refs_0_.place_ref, s32[6]{0:T(128)S(1)} %copy-done.6, s32[1]{0:T(128)S(6)} %copy.24.refs_1_.count_ref, bf16[512,128]{1,0:T(8,128)(2,1)S(1)} %get-tuple-element.61.pulls_ref, ...), custom_call_target="tpu_custom_call" | custom-call | flops 301989888 | bytes 1388572 | tf_op jit(solution)/shard_map/pallas_call | solution.py:118
  59.5 1.4 %collective-permute-done.12.refs_12_ = bf16[256,128]{1,0:T(8,128)(2,1)S(1)} collective-permute-done((bf16[256,128]{1,0:T(8,128)(2,1)S(1)}, bf16[256,128]{1,0:T(8,128)(2,1)S(1)}, u32[]{:S(2)}, u32[]{:S(2)}) %collective-permute-start.12) | collective-permute-done | bytes 65568 | tf_op jit(solution)/shard_map/ppermute | solution.py:103
  60.9 7.7 %shard_map.223 = (bf16[1536,128]{1,0:T(8,128)(2,1)}, bf16[1536,128]{1,0:T(8,128)(2,1)S(1)}, bf16[1536,128]{1,0:T(8,128)(2,1)S(1)}, bf16[1536,128]{1,0:T(8,128)(2...) custom-call(s32[6,256]{1,0:T(8,128)S(1)} %get-tuple-element.50.refs_, ...), custom_call_target="tpu_custom_call" | custom-call | flops 1258291200 | bytes 6337540 | tf_op jit(solution)/shard_map/pallas_call | solution.py:118
  68.6 0.8 shard_map.226
  69.5 1.4 %collective-permute-done.22.got_ref = bf16[608,128]{1,0:T(8,128)(2,1)S(1)} collective-permute-done((bf16[608,128]{1,0:T(8,128)(2,1)S(1)}, bf16[608,128]{1,0:T(8,128)(2,1)S(1)}, u32[]{:S(2)}, u32[]{:S(2)}) %collective-permute-start.22) | collective-permute-done | bytes 155680 | tf_op jit(solution)/shard_map/ppermute | solution.py:109
  71.7 1.4 %collective-permute-start.16 = (bf16[256,128]{1,0:T(8,128)(2,1)S(1)}, bf16[256,128]{1,0:T(8,128)(2,1)S(1)}, u32[]{:S(2)}, u32[]{:S(2)}) collective-permute-start(bf16[256,128]{1,0:T(8,128)(2,1)S(1)} %get-tuple-element.69), channel_id=1, source_target_pairs={{0,2},{1,3},{2,0},{3,1},{4,6},{5,7},{6,4},{7,5},{8,10},{9,11},{10,... | collective-permute-start | bytes 196616 | tf_op jit(solution)/shard_map/ppermute | solution.py:103
  73.0 2.0 %collective-permute-start.17 = (bf16[256,128]{1,0:T(8,128)(2,1)S(1)}, bf16[256,128]{1,0:T(8,128)(2,1)S(1)}, u32[]{:S(2)}, u32[]{:S(2)}) collective-permute-start(bf16[256,128]{1,0:T(8,128)(2,1)S(1)} %get-tuple-element.70), channel_id=1, source_target_pairs={{0,4},{1,5},{2,6},{3,7},{4,0},{5,1},{6,2},{7,3},{8,12},{9,13},{10,... | collective-permute-start | bytes 196616 | tf_op jit(solution)/shard_map/ppermute | solution.py:103
  76.8 1.4 %collective-permute-start.26 = (bf16[304,128]{1,0:T(8,128)(2,1)S(1)}, bf16[304,128]{1,0:T(8,128)(2,1)S(1)}, u32[]{:S(2)}, u32[]{:S(2)}) collective-permute-start(bf16[304,128]{1,0:T(8,128)(2,1)S(1)} %add_convert_fusion.2), channel_id=1, source_target_pairs={{0,12},{4,8},{8,4},{12,0},{1,13},{5,9},{9,5},{13,1},{2,14},{6,10},... | collective-permute-start | bytes 233480 | tf_op jit(solution)/shard_map/ppermute | solution.py:109
  78.2 7.2 %collective-permute-start.25 = (bf16[304,128]{1,0:T(8,128)(2,1)S(1)}, bf16[304,128]{1,0:T(8,128)(2,1)S(1)}, u32[]{:S(2)}, u32[]{:S(2)}) collective-permute-start(bf16[304,128]{1,0:T(8,128)(2,1)S(1)} %add_convert_fusion.2), channel_id=1, source_target_pairs={{0,8},{4,12},{8,0},{12,4},{1,9},{5,13},{9,1},{13,5},{2,10},{6,14},... | collective-permute-start | bytes 233480 | tf_op jit(solution)/shard_map/ppermute | solution.py:109
  85.4 2.0 %shard_map.224.own_ref = f32[512,128]{1,0:T(8,128)S(1)} custom-call(s32[6,256]{1,0:T(8,128)S(1)} %reshape.30.off_ref, s32[6,256]{1,0:T(8,128)S(1)} %get-tuple-element.50.refs_0_.place_ref, s32[6]{0:T(128)S(1)} %copy-done.6, s32[1,256]{1,0:T(1,128)S(1)} %bitcast.7, bf16[1536,128]{1,0:T(8,128)(2,1)S(1)} %get-tuple-element.67.near_ref, ...), custom_call_target="tpu_custom_call" | custom-call | flops 503316480 | bytes 1061912 | tf_op jit(solution)/shard_map/pallas_call | solution.py:118
  88.1 2.2 %collective-permute-done.25 = bf16[304,128]{1,0:T(8,128)(2,1)S(1)} collective-permute-done((bf16[304,128]{1,0:T(8,128)(2,1)S(1)}, bf16[304,128]{1,0:T(8,128)(2,1)S(1)}, u32[]{:S(2)}, u32[]{:S(2)}) %collective-permute-start.25) | collective-permute-done | bytes 77856 | tf_op jit(solution)/shard_map/ppermute | solution.py:109
  90.7 0.9 collective-permute-start.27
  91.6 3.6 %collective-permute-done.27.refs_1_ = bf16[304,128]{1,0:T(8,128)(2,1)S(1)} collective-permute-done((bf16[304,128]{1,0:T(8,128)(2,1)S(1)}, bf16[304,128]{1,0:T(8,128)(2,1)S(1)}, u32[]{:S(2)}, u32[]{:S(2)}) %collective-permute-start.27) | collective-permute-done | bytes 77856 | tf_op jit(solution)/shard_map/ppermute | solution.py:109
  95.3 0.7 add_convert_fusion
  96.6 0.9 shard_map.229
  (83 shorter events, 11.3 us)
Async XLA Ops:
  2.2 13.7 %copy-start.8 = (bf16[384,128]{1,0:T(8,128)(2,1)S(1)}, bf16[384,128]{1,0:T(8,128)(2,1)}, u32[]{:S(2)}) copy-start(bf16[384,128]{1,0:T(8,128)(2,1)} %refs_7_.3) | copy-start | bytes 294916
  2.5 18.5 %collective-permute-start.4 = (bf16[256,128]{1,0:T(8,128)(2,1)S(1)}, bf16[256,128]{1,0:T(8,128)(2,1)S(1)}, u32[]{:S(2)}, u32[]{:S(2)}) collective-permute-start(bf16[256,128]{1,0:T(8,128)(2,1)S(1)} %shard_map.216.border_ref), channel_id=1, source_target_pairs={{4,10},{5,11},{6,8},{7,9},{8,6},{9,7},{10,4},{11,5},{20,26},{21,27... | collective-permute-start | bytes 196616 | tf_op jit(solution)/shard_map/ppermute | solution.py:103
  3.2 17.8 %collective-permute-start.3 = (bf16[256,128]{1,0:T(8,128)(2,1)S(1)}, bf16[256,128]{1,0:T(8,128)(2,1)S(1)}, u32[]{:S(2)}, u32[]{:S(2)}) collective-permute-start(bf16[256,128]{1,0:T(8,128)(2,1)S(1)} %shard_map.216.border_ref), channel_id=1, source_target_pairs={{4,8},{5,9},{6,10},{7,11},{8,4},{9,5},{10,6},{11,7},{20,24},{21,25... | collective-permute-start | bytes 196616 | tf_op jit(solution)/shard_map/ppermute | solution.py:103
  3.8 17.2 %collective-permute-start.2 = (bf16[256,128]{1,0:T(8,128)(2,1)S(1)}, bf16[256,128]{1,0:T(8,128)(2,1)S(1)}, u32[]{:S(2)}, u32[]{:S(2)}) collective-permute-start(bf16[256,128]{1,0:T(8,128)(2,1)S(1)} %shard_map.216.border_ref), channel_id=1, source_target_pairs={{0,6},{1,7},{2,4},{3,5},{4,2},{5,3},{6,0},{7,1},{8,14},{9,15},{10,... | collective-permute-start | bytes 196616 | tf_op jit(solution)/shard_map/ppermute | solution.py:103
  12.3 8.7 %collective-permute-start.1 = (bf16[256,128]{1,0:T(8,128)(2,1)S(1)}, bf16[256,128]{1,0:T(8,128)(2,1)S(1)}, u32[]{:S(2)}, u32[]{:S(2)}) collective-permute-start(bf16[256,128]{1,0:T(8,128)(2,1)S(1)} %shard_map.216.border_ref), channel_id=1, source_target_pairs={{0,4},{1,5},{2,6},{3,7},{4,0},{5,1},{6,2},{7,3},{8,12},{9,13},{10,... | collective-permute-start | bytes 196616 | tf_op jit(solution)/shard_map/ppermute | solution.py:103
  12.5 8.6 %collective-permute-start = (bf16[256,128]{1,0:T(8,128)(2,1)S(1)}, bf16[256,128]{1,0:T(8,128)(2,1)S(1)}, u32[]{:S(2)}, u32[]{:S(2)}) collective-permute-start(bf16[256,128]{1,0:T(8,128)(2,1)S(1)} %shard_map.216.border_ref), channel_id=1, source_target_pairs={{0,2},{1,3},{2,0},{3,1},{4,6},{5,7},{6,4},{7,5},{8,10},{9,11},{10,... | collective-permute-start | bytes 196616 | tf_op jit(solution)/shard_map/ppermute | solution.py:103
  29.9 6.9 %collective-permute-start.5 = (bf16[256,128]{1,0:T(8,128)(2,1)S(1)}, bf16[256,128]{1,0:T(8,128)(2,1)S(1)}, u32[]{:S(2)}, u32[]{:S(2)}) collective-permute-start(bf16[256,128]{1,0:T(8,128)(2,1)S(1)} %get-tuple-element.54), channel_id=1, source_target_pairs={{0,2},{1,3},{2,0},{3,1},{4,6},{5,7},{6,4},{7,5},{8,10},{9,11},{10,... | collective-permute-start | bytes 196616 | tf_op jit(solution)/shard_map/ppermute | solution.py:103
  30.6 6.3 %collective-permute-start.6 = (bf16[256,128]{1,0:T(8,128)(2,1)S(1)}, bf16[256,128]{1,0:T(8,128)(2,1)S(1)}, u32[]{:S(2)}, u32[]{:S(2)}) collective-permute-start(bf16[256,128]{1,0:T(8,128)(2,1)S(1)} %get-tuple-element.55), channel_id=1, source_target_pairs={{0,4},{1,5},{2,6},{3,7},{4,0},{5,1},{6,2},{7,3},{8,12},{9,13},{10,... | collective-permute-start | bytes 196616 | tf_op jit(solution)/shard_map/ppermute | solution.py:103
  32.5 5.2 %collective-permute-start.7 = (bf16[256,128]{1,0:T(8,128)(2,1)S(1)}, bf16[256,128]{1,0:T(8,128)(2,1)S(1)}, u32[]{:S(2)}, u32[]{:S(2)}) collective-permute-start(bf16[256,128]{1,0:T(8,128)(2,1)S(1)} %get-tuple-element.56), channel_id=1, source_target_pairs={{0,6},{1,7},{2,4},{3,5},{4,2},{5,3},{6,0},{7,1},{8,14},{9,15},{10,... | collective-permute-start | bytes 196616 | tf_op jit(solution)/shard_map/ppermute | solution.py:103
  33.4 4.2 %collective-permute-start.8 = (bf16[256,128]{1,0:T(8,128)(2,1)S(1)}, bf16[256,128]{1,0:T(8,128)(2,1)S(1)}, u32[]{:S(2)}, u32[]{:S(2)}) collective-permute-start(bf16[256,128]{1,0:T(8,128)(2,1)S(1)} %get-tuple-element.57), channel_id=1, source_target_pairs={{4,8},{5,9},{6,10},{7,11},{8,4},{9,5},{10,6},{11,7},{20,24},{21,25... | collective-permute-start | bytes 196616 | tf_op jit(solution)/shard_map/ppermute | solution.py:103
  34.1 3.6 %collective-permute-start.9 = (bf16[256,128]{1,0:T(8,128)(2,1)S(1)}, bf16[256,128]{1,0:T(8,128)(2,1)S(1)}, u32[]{:S(2)}, u32[]{:S(2)}) collective-permute-start(bf16[256,128]{1,0:T(8,128)(2,1)S(1)} %get-tuple-element.58), channel_id=1, source_target_pairs={{4,10},{5,11},{6,8},{7,9},{8,6},{9,7},{10,4},{11,5},{20,26},{21,27... | collective-permute-start | bytes 196616 | tf_op jit(solution)/shard_map/ppermute | solution.py:103
  38.2 19.1 %copy-start.2 = (bf16[1536,128]{1,0:T(8,128)(2,1)S(1)}, bf16[1536,128]{1,0:T(8,128)(2,1)}, u32[]{:S(2)}) copy-start(bf16[1536,128]{1,0:T(8,128)(2,1)} %cot_ref.3) | copy-start | bytes 1179652
  38.2 1.4 %collective-permute-start.10 = (bf16[512,128]{1,0:T(8,128)(2,1)S(1)}, bf16[512,128]{1,0:T(8,128)(2,1)S(1)}, u32[]{:S(2)}, u32[]{:S(2)}) collective-permute-start(bf16[512,128]{1,0:T(8,128)(2,1)S(1)} %shard_map.220.part_ref), channel_id=1, source_target_pairs={{0,1},{1,0},{2,3},{3,2},{4,5},{5,4},{6,7},{7,6},{8,9},{9,8},{10,11... | collective-permute-start | bytes 393224 | tf_op jit(solution)/shard_map/ppermute | solution.py:109
  41.2 19.7 %copy-start.17 = (f32[1536,1]{1,0:T(8,128)S(1)}, f32[1536,1]{1,0:T(8,128)}, u32[]{:S(2)}) copy-start(f32[1536,1]{1,0:T(8,128)} %get-tuple-element.64.refs_4_) | copy-start | bytes 18436
  41.2 18.3 %collective-permute-start.15 = (bf16[256,128]{1,0:T(8,128)(2,1)S(1)}, bf16[256,128]{1,0:T(8,128)(2,1)S(1)}, u32[]{:S(2)}, u32[]{:S(2)}) collective-permute-start(bf16[256,128]{1,0:T(8,128)(2,1)S(1)} %get-tuple-element.62.border_ref), channel_id=1, source_target_pairs={{4,10},{5,11},{6,8},{7,9},{8,6},{9,7},{10,4},{11,5},{20,26},{21,27... | collective-permute-start | bytes 196616 | tf_op jit(solution)/shard_map/ppermute | solution.py:103
  42.0 17.5 %collective-permute-start.14 = (bf16[256,128]{1,0:T(8,128)(2,1)S(1)}, bf16[256,128]{1,0:T(8,128)(2,1)S(1)}, u32[]{:S(2)}, u32[]{:S(2)}) collective-permute-start(bf16[256,128]{1,0:T(8,128)(2,1)S(1)} %get-tuple-element.62.border_ref), channel_id=1, source_target_pairs={{4,8},{5,9},{6,10},{7,11},{8,4},{9,5},{10,6},{11,7},{20,24},{21,25... | collective-permute-start | bytes 196616 | tf_op jit(solution)/shard_map/ppermute | solution.py:103
  42.9 16.6 %collective-permute-start.13 = (bf16[256,128]{1,0:T(8,128)(2,1)S(1)}, bf16[256,128]{1,0:T(8,128)(2,1)S(1)}, u32[]{:S(2)}, u32[]{:S(2)}) collective-permute-start(bf16[256,128]{1,0:T(8,128)(2,1)S(1)} %get-tuple-element.62.border_ref), channel_id=1, source_target_pairs={{0,6},{1,7},{2,4},{3,5},{4,2},{5,3},{6,0},{7,1},{8,14},{9,15},{10,... | collective-permute-start | bytes 196616 | tf_op jit(solution)/shard_map/ppermute | solution.py:103
  56.6 4.3 %collective-permute-start.12 = (bf16[256,128]{1,0:T(8,128)(2,1)S(1)}, bf16[256,128]{1,0:T(8,128)(2,1)S(1)}, u32[]{:S(2)}, u32[]{:S(2)}) collective-permute-start(bf16[256,128]{1,0:T(8,128)(2,1)S(1)} %get-tuple-element.62.border_ref), channel_id=1, source_target_pairs={{0,4},{1,5},{2,6},{3,7},{4,0},{5,1},{6,2},{7,3},{8,12},{9,13},{10,... | collective-permute-start | bytes 196616 | tf_op jit(solution)/shard_map/ppermute | solution.py:103
  56.7 4.3 %collective-permute-start.11 = (bf16[256,128]{1,0:T(8,128)(2,1)S(1)}, bf16[256,128]{1,0:T(8,128)(2,1)S(1)}, u32[]{:S(2)}, u32[]{:S(2)}) collective-permute-start(bf16[256,128]{1,0:T(8,128)(2,1)S(1)} %get-tuple-element.62.border_ref), channel_id=1, source_target_pairs={{0,2},{1,3},{2,0},{3,1},{4,6},{5,7},{6,4},{7,5},{8,10},{9,11},{10,... | collective-permute-start | bytes 196616 | tf_op jit(solution)/shard_map/ppermute | solution.py:103
  69.4 1.4 %collective-permute-start.22 = (bf16[608,128]{1,0:T(8,128)(2,1)S(1)}, bf16[608,128]{1,0:T(8,128)(2,1)S(1)}, u32[]{:S(2)}, u32[]{:S(2)}) collective-permute-start(bf16[608,128]{1,0:T(8,128)(2,1)S(1)} %get-tuple-element.87), channel_id=1, source_target_pairs={{0,1},{1,0},{2,3},{3,2},{4,5},{5,4},{6,7},{7,6},{8,9},{9,8},{10,11... | collective-permute-start | bytes 466952 | tf_op jit(solution)/shard_map/ppermute | solution.py:109
  70.9 5.2 %collective-permute-start.23 = (bf16[304,128]{1,0:T(8,128)(2,1)S(1)}, bf16[304,128]{1,0:T(8,128)(2,1)S(1)}, u32[]{:S(2)}, u32[]{:S(2)}) collective-permute-start(bf16[304,128]{1,0:T(8,128)(2,1)S(1)} %get-tuple-element.89), channel_id=1, source_target_pairs={{0,2},{2,0},{1,3},{3,1},{4,6},{6,4},{5,7},{7,5},{8,10},{10,8},{9,1... | collective-permute-start | bytes 233480 | tf_op jit(solution)/shard_map/ppermute | solution.py:109
  71.7 5.2 %collective-permute-start.16 = (bf16[256,128]{1,0:T(8,128)(2,1)S(1)}, bf16[256,128]{1,0:T(8,128)(2,1)S(1)}, u32[]{:S(2)}, u32[]{:S(2)}) collective-permute-start(bf16[256,128]{1,0:T(8,128)(2,1)S(1)} %get-tuple-element.69), channel_id=1, source_target_pairs={{0,2},{1,3},{2,0},{3,1},{4,6},{5,7},{6,4},{7,5},{8,10},{9,11},{10,... | collective-permute-start | bytes 196616 | tf_op jit(solution)/shard_map/ppermute | solution.py:103
  73.0 5.2 %collective-permute-start.17 = (bf16[256,128]{1,0:T(8,128)(2,1)S(1)}, bf16[256,128]{1,0:T(8,128)(2,1)S(1)}, u32[]{:S(2)}, u32[]{:S(2)}) collective-permute-start(bf16[256,128]{1,0:T(8,128)(2,1)S(1)} %get-tuple-element.70), channel_id=1, source_target_pairs={{0,4},{1,5},{2,6},{3,7},{4,0},{5,1},{6,2},{7,3},{8,12},{9,13},{10,... | collective-permute-start | bytes 196616 | tf_op jit(solution)/shard_map/ppermute | solution.py:103
  75.1 10.4 %collective-permute-start.18 = (bf16[256,128]{1,0:T(8,128)(2,1)S(1)}, bf16[256,128]{1,0:T(8,128)(2,1)S(1)}, u32[]{:S(2)}, u32[]{:S(2)}) collective-permute-start(bf16[256,128]{1,0:T(8,128)(2,1)S(1)} %get-tuple-element.71), channel_id=1, source_target_pairs={{0,6},{1,7},{2,4},{3,5},{4,2},{5,3},{6,0},{7,1},{8,14},{9,15},{10,... | collective-permute-start | bytes 196616 | tf_op jit(solution)/shard_map/ppermute | solution.py:103
  75.1 12.3 %collective-permute-start.19 = (bf16[256,128]{1,0:T(8,128)(2,1)S(1)}, bf16[256,128]{1,0:T(8,128)(2,1)S(1)}, u32[]{:S(2)}, u32[]{:S(2)}) collective-permute-start(bf16[256,128]{1,0:T(8,128)(2,1)S(1)} %get-tuple-element.72), channel_id=1, source_target_pairs={{4,8},{5,9},{6,10},{7,11},{8,4},{9,5},{10,6},{11,7},{20,24},{21,25... | collective-permute-start | bytes 196616 | tf_op jit(solution)/shard_map/ppermute | solution.py:103
  76.1 11.3 %collective-permute-start.20 = (bf16[256,128]{1,0:T(8,128)(2,1)S(1)}, bf16[256,128]{1,0:T(8,128)(2,1)S(1)}, u32[]{:S(2)}, u32[]{:S(2)}) collective-permute-start(bf16[256,128]{1,0:T(8,128)(2,1)S(1)} %get-tuple-element.73), channel_id=1, source_target_pairs={{4,10},{5,11},{6,8},{7,9},{8,6},{9,7},{10,4},{11,5},{20,26},{21,27... | collective-permute-start | bytes 196616 | tf_op jit(solution)/shard_map/ppermute | solution.py:103
  76.8 11.2 %collective-permute-start.26 = (bf16[304,128]{1,0:T(8,128)(2,1)S(1)}, bf16[304,128]{1,0:T(8,128)(2,1)S(1)}, u32[]{:S(2)}, u32[]{:S(2)}) collective-permute-start(bf16[304,128]{1,0:T(8,128)(2,1)S(1)} %add_convert_fusion.2), channel_id=1, source_target_pairs={{0,12},{4,8},{8,4},{12,0},{1,13},{5,9},{9,5},{13,1},{2,14},{6,10},... | collective-permute-start | bytes 233480 | tf_op jit(solution)/shard_map/ppermute | solution.py:109
  78.2 12.0 %collective-permute-start.25 = (bf16[304,128]{1,0:T(8,128)(2,1)S(1)}, bf16[304,128]{1,0:T(8,128)(2,1)S(1)}, u32[]{:S(2)}, u32[]{:S(2)}) collective-permute-start(bf16[304,128]{1,0:T(8,128)(2,1)S(1)} %add_convert_fusion.2), channel_id=1, source_target_pairs={{0,8},{4,12},{8,0},{12,4},{1,9},{5,13},{9,1},{13,5},{2,10},{6,14},... | collective-permute-start | bytes 233480 | tf_op jit(solution)/shard_map/ppermute | solution.py:109
  85.4 5.2 %collective-permute-start.24 = (bf16[304,128]{1,0:T(8,128)(2,1)S(1)}, bf16[304,128]{1,0:T(8,128)(2,1)S(1)}, u32[]{:S(2)}, u32[]{:S(2)}) collective-permute-start(bf16[304,128]{1,0:T(8,128)(2,1)S(1)} %add_convert_fusion.2), channel_id=1, source_target_pairs={{0,4},{4,0},{8,12},{12,8},{1,5},{5,1},{9,13},{13,9},{2,6},{6,2},{1... | collective-permute-start | bytes 233480 | tf_op jit(solution)/shard_map/ppermute | solution.py:109
  88.0 7.3 %collective-permute-start.21 = (bf16[512,128]{1,0:T(8,128)(2,1)S(1)}, bf16[512,128]{1,0:T(8,128)(2,1)S(1)}, u32[]{:S(2)}, u32[]{:S(2)}) collective-permute-start(bf16[512,128]{1,0:T(8,128)(2,1)S(1)} %shard_map.225), channel_id=1, source_target_pairs={{0,1},{1,0},{2,3},{3,2},{4,5},{5,4},{6,7},{7,6},{8,9},{9,8},{10,11... | collective-permute-start | bytes 393224 | tf_op jit(solution)/shard_map/ppermute | solution.py:109
  90.7 4.5 %collective-permute-start.27 = (bf16[304,128]{1,0:T(8,128)(2,1)S(1)}, bf16[304,128]{1,0:T(8,128)(2,1)S(1)}, u32[]{:S(2)}, u32[]{:S(2)}) collective-permute-start(bf16[304,128]{1,0:T(8,128)(2,1)S(1)} %add_convert_fusion.1.refs_0_), channel_id=1, source_target_pairs={{0,2},{2,0},{1,3},{3,1},{4,6},{6,4},{5,7},{7,5},{8,10},{10,8},{9,1... | collective-permute-start | bytes 233480 | tf_op jit(solution)/shard_map/ppermute | solution.py:109
  95.2 1.4 %collective-permute-start.28 = (bf16[608,128]{1,0:T(8,128)(2,1)S(1)}, bf16[608,128]{1,0:T(8,128)(2,1)S(1)}, u32[]{:S(2)}, u32[]{:S(2)}) collective-permute-start(bf16[608,128]{1,0:T(8,128)(2,1)S(1)} %shard_map.228.own_ref), channel_id=1, source_target_pairs={{0,1},{1,0},{2,3},{3,2},{4,5},{5,4},{6,7},{7,6},{8,9},{9,8},{10,11... | collective-permute-start | bytes 466952 | tf_op jit(solution)/shard_map/ppermute | solution.py:109
  (16 other events, 51.0 us)

commit v2 on v1

v2 whole, which is shorter than its diff:
```python
import math

import jax
import jax.numpy as jnp
from jax import lax
from jax.experimental import pallas as pl
from jax.experimental.pallas import tpu as pltpu
from jax.sharding import PartitionSpec as P

EPS = 1e-05
BF = jnp.bfloat16
F32 = jnp.float32
AXES = ("dom", "sub", "inner")
VMEM_LIMIT = 16 * 1024 * 1024


def mm(left, right):
    return jnp.dot(left, right, preferred_element_type=F32)


def mm_tn(left, right):
    return lax.dot_general(left, right, (((0,), (0,)), ((), ())), preferred_element_type=F32)


def mm_nt(left, right):
    return lax.dot_general(left, right, (((1,), (1,)), ((), ())), preferred_element_type=F32)


def silu_pair(pre_act):
    logistic = jax.nn.sigmoid(pre_act)
    act = pre_act * logistic
    return act, logistic + act * (1.0 - logistic)


def layer_norm(output_pre):
    centred = output_pre - jnp.mean(output_pre, axis=-1, keepdims=True)
    inverse = lax.rsqrt(jnp.mean(centred * centred, axis=-1, keepdims=True) + EPS)
    return centred * inverse, inverse


def norm_backward(scaled, normed, inverse):
    return inverse * (
        scaled
        - jnp.mean(scaled, axis=-1, keepdims=True)
        - normed * jnp.mean(scaled * normed, axis=-1, keepdims=True)
    )


def hot_rows(index_row, rows):
    place = lax.broadcasted_iota(jnp.int32, (rows, index_row.shape[1]), 0)
    return jnp.where(place == index_row, 1.0, 0.0).astype(BF)


def folded_hot(index_row, rows):
    return hot_rows(jnp.where(index_row >= rows, index_row - rows, index_row), rows)


def fold(table):
    rows = table.shape[0] // 2
    return jnp.concatenate([table[:rows], table[rows:]], axis=1)


def unfold(table):
    f = table.shape[1] // 2
    return jnp.concatenate([table[:, :f], table[:, f:]], axis=0)


def gather_folded(index_row, index_col, table):
    rows, f = table.shape[0], table.shape[1] // 2
    got = mm_tn(folded_hot(index_row, rows), table)
    return jnp.where(index_col >= rows, got[:, f:], got[:, :f])


def halves(values, index_col, rows):
    upper = index_col >= rows
    zero = jnp.zeros_like(values)
    return jnp.concatenate(
        [jnp.where(upper, zero, values), jnp.where(upper, values, zero)], axis=1
    ).astype(BF)


def column(row):
    wide = jnp.broadcast_to(row, (8, row.shape[1]))
    return jnp.transpose(wide)[:, :1]


class Layout:
    def __init__(self, nodes, send):
        self.nodes, self.send = nodes, send
        self.sub = lax.axis_size("sub")
        self.dom = lax.axis_size("dom")
        across = range(1, self.sub)
        self.remote = [(2, 0), (1, 0)]
        self.remote += [(0, x) for x in across]
        self.remote += [(2, x) for x in across] + [(1, x) for x in across]
        self.halo = len(self.remote) * send

    def place(self, other):
        d, t = lax.axis_index("dom"), lax.axis_index("sub")
        slot = jnp.maximum(other - self.nodes, 0)
        layer = slot // (self.sub * self.send)
        rest = slot - layer * (self.sub * self.send)
        peer = rest // self.send
        k = rest - peer * self.send
        upper = (layer == 2).astype(jnp.int32)
        even = 1 - lax.rem(d, 2)
        x = peer ^ t
        across = self.sub - 1
        aside = jnp.where(layer == 1, 0, jnp.where(upper == even, 2, 1))
        place = jnp.where(x > 0, 2 + aside * across + x, aside)
        row = self.nodes + place * self.send + k
        return jnp.where(other < self.nodes, other, row)

    def exchange(self, arrays):
        inner = lax.axis_size("inner")
        out = []
        for (a, x), value in zip(self.remote, arrays):
            pairs = []
            for d in range(self.dom):
                other = d if a == 0 else (d ^ 1 if a == 1 else ((d + 1) ^ 1) - 1)
                if not 0 <= other < self.dom:
                    continue
                for t in range(self.sub):
                    for i in range(inner):
                        pairs.append(
                            (
                                (d * self.sub + t) * inner + i,
                                (other * self.sub + (t ^ x)) * inner + i,
                            )
                        )
            out.append(lax.ppermute(value, AXES, pairs))
        return out


def swap_axis(value, axis, mask):
    count = lax.axis_size(axis)
    return lax.ppermute(value, axis, [(j, j ^ mask) for j in range(count)])


def call(body, outs, *args, smem=(), scratch=(), flops=0):
    specs = [
        pl.BlockSpec(memory_space=pltpu.SMEM if j in smem else pltpu.VMEM)
        for j in range(len(args))
    ]
    size = sum(math.prod(a.shape) * a.dtype.itemsize for a in (*args, *outs))
    return pl.pallas_call(
        body,
        out_shape=outs,
        in_specs=specs,
        out_specs=[pl.BlockSpec(memory_space=pltpu.VMEM) for _ in outs],
        scratch_shapes=list(scratch),
        compiler_params=pltpu.CompilerParams(vmem_limit_bytes=VMEM_LIMIT),
        cost_estimate=pl.CostEstimate(flops=flops, bytes_accessed=size, transcendentals=0),
    )(*args)


def shape(rows, cols, dtype):
    return jax.ShapeDtypeStruct((rows, cols), dtype)


def border_kernel(send_ref, table_ref, out_ref):
    hot = hot_rows(send_ref[...], table_ref.shape[0])
    out_ref[...] = mm_tn(hot, table_ref[...]).astype(BF)


def live_column(count_ref, b, size):
    row = lax.broadcasted_iota(jnp.int32, (size, 1), 0) + b * size
    return jnp.where(row < count_ref[0], 1.0, 0.0)


def whole_row(ref):
    return jnp.concatenate([ref[b : b + 1, :] for b in range(ref.shape[0])], axis=1)


def per_device(
    node_state,
    edge_state,
    edge_count,
    block_start,
    edge_offset,
    edge_other,
    send_index,
    edge_entry,
    edge_middle,
    edge_outlet,
    edge_gain,
    node_entry,
    node_middle,
    node_outlet,
    node_gain,
    node_cotangent,
    edge_cotangent,
):
    nodes, feat = node_state.shape
    edges = edge_state.shape[0]
    blocks = block_start.shape[0]
    size = edges // blocks
    send = send_index.shape[0]
    lay = Layout(nodes, send)
    remote = len(lay.remote)
    own = nodes + send
    half_near, half_own, half_halo = nodes // 2, own // 2, lay.halo // 2
    f = feat

    sends = send_index.reshape(1, send)
    gain_e = edge_gain.reshape(1, f)
    gain_n = node_gain.reshape(1, f)

    (border,) = call(border_kernel, [shape(send, f, BF)], sends, node_state)
    halo = lay.exchange([border] * remote)

    def edge_local(
        off_ref, oth_ref, start_ref, node_ref, border_ref, edge_ref, entry_ref,
        near_ref, far_ref, pre_ref, place_ref, spot_ref,
    ):
        near_table = fold(node_ref[...])
        own_table = fold(jnp.concatenate([node_ref[...], border_ref[...]], axis=0))
        for b in range(blocks):
            rows = pl.ds(b * size, size)
            spot = off_ref[rows].reshape(1, size) + start_ref[b]
            place = lay.place(oth_ref[rows].reshape(1, size))
            spot_ref[b : b + 1, :] = spot
            place_ref[b : b + 1, :] = place
            near = gather_folded(spot, column(spot), near_table).astype(BF)
            near_ref[rows, :] = near
            far_ref[rows, :] = gather_folded(place, column(place), own_table).astype(BF)
            pre_ref[rows, :] = mm(edge_ref[rows, :], entry_ref[:f, :]) + mm(
                near, entry_ref[f : 2 * f, :]
            )

    near_rows, far_own, pre_own, place, spot = call(
        edge_local,
        [
            shape(edges, f, BF),
            shape(edges, f, BF),
            shape(edges, f, F32),
            shape(blocks, size, jnp.int32),
            shape(blocks, size, jnp.int32),
        ],
        edge_offset, edge_other, block_start, node_state, border, edge_state, edge_entry,
        smem=(2,),
        flops=2 * edges * f * (nodes + own + 2 * f),
    )

    def edge_forward(*refs):
        (place_ref, count_ref, edge_ref, far_own_ref, pre_ref, entry_ref, middle_ref,
         outlet_ref, gain_ref) = refs[:9]
        halo_refs = refs[9 : 9 + remote]
        (message_ref, far_ref, h1_ref, h2_ref, s1_ref, s2_ref, out_ref) = refs[
            9 + remote : 16 + remote
        ]
        slot_refs = refs[16 + remote : 16 + 2 * remote]
        table, pairs = refs[16 + 2 * remote :]
        for j in range(remote):
            table[pl.ds(j * send, send), :] = halo_refs[j][...]
        folded = fold(table[...])
        for b in range(blocks):
            rows = pl.ds(b * size, size)
            slot = place_ref[b : b + 1, :] - own
            slot_col = column(slot)
            far = gather_folded(slot, slot_col, folded)
            far = (far + far_own_ref[rows, :].astype(F32)).astype(BF)
            far_ref[rows, :] = far
            act, slope = silu_pair(pre_ref[rows, :] + mm(far, entry_ref[2 * f :, :]))
            h1 = act.astype(BF)
            h1_ref[rows, :] = h1
            s1_ref[rows, :] = slope
            act, slope = silu_pair(mm(h1, middle_ref[...]))
            h2 = act.astype(BF)
            h2_ref[rows, :] = h2
            s2_ref[rows, :] = slope
            output_pre = mm(h2, outlet_ref[...])
            out_ref[rows, :] = output_pre
            normed, _ = layer_norm(output_pre)
            live = live_column(count_ref, b, size)
            state = edge_ref[rows, :].astype(F32)
            new = (state + live * gain_ref[...] * normed).astype(BF)
            message = new.astype(F32) * live
            message_ref[rows, :] = message.astype(BF)
            pairs[rows, :] = halves(message, slot_col, half_halo)
        hot = folded_hot(whole_row(place_ref) - own, half_halo)
        sums = unfold(mm(hot, pairs[...]).astype(BF))
        for j in range(remote):
            slot_refs[j][...] = sums[j * send : (j + 1) * send]

    edge_outs = call(
        edge_forward,
        [shape(edges, f, BF)] * 4
        + [shape(edges, f, F32)] * 3
        + [shape(send, f, BF)] * remote,
        place, edge_count, edge_state, far_own, pre_own, edge_entry, edge_middle, edge_outlet,
        gain_e, *halo,
        smem=(1,),
        scratch=[pltpu.VMEM((lay.halo, f), BF), pltpu.VMEM((edges, 2 * f), BF)],
        flops=2 * edges * f * (2 * lay.halo + 3 * f),
    )
    message, far_rows, h1, h2, s1, s2, out_pre = edge_outs[:7]
    received = lay.exchange(edge_outs[7:])

    def local_sums(spot_ref, place_ref, send_ref, near_pairs, far_pairs):
        total = unfold(mm(folded_hot(whole_row(spot_ref), half_near), near_pairs[...]))
        sums = unfold(mm(folded_hot(whole_row(place_ref), half_own), far_pairs[...]))
        slot = sums[nodes:].astype(BF)
        return total + sums[:nodes] + mm(hot_rows(send_ref[...], nodes), slot)

    pair_scratch = [pltpu.VMEM((edges, 2 * f), BF), pltpu.VMEM((edges, 2 * f), BF)]

    def message_sums(
        spot_ref, place_ref, send_ref, count_ref, edge_ref, message_ref, new_ref, out_ref,
        near_pairs, far_pairs,
    ):
        for b in range(blocks):
            rows = pl.ds(b * size, size)
            message = message_ref[rows, :].astype(F32)
            live = live_column(count_ref, b, size) > 0.0
            new_ref[rows, :] = jnp.where(live, message, edge_ref[rows, :].astype(F32)).astype(BF)
            near_pairs[rows, :] = halves(message, column(spot_ref[b : b + 1, :]), half_near)
            far_pairs[rows, :] = halves(message, column(place_ref[b : b + 1, :]), half_own)
        out_ref[...] = local_sums(spot_ref, place_ref, send_ref, near_pairs, far_pairs)

    new_edges, message_part = call(
        message_sums,
        [shape(edges, f, BF), shape(nodes, f, F32)],
        spot, place, sends, edge_count, edge_state, message,
        smem=(3,),
        scratch=pair_scratch,
        flops=2 * edges * f * (nodes + own),
    )

    def join_kernel(send_ref, own_ref, *refs):
        hot = hot_rows(send_ref[...], nodes)
        total = own_ref[...]
        for ref in refs[:-1]:
            total += mm(hot, ref[...])
        refs[-1][...] = total.astype(BF)

    def join(part, arrived):
        (out,) = call(
            join_kernel, [shape(nodes, f, BF)], sends, part, *arrived,
            flops=2 * nodes * send * f * remote,
        )
        return out, swap_axis(out, "inner", 1)

    part, part_other = join(message_part, received)

    def node_kernel(
        part_ref, other_ref, node_ref, cot_ref, send_ref, entry_ref, middle_ref, outlet_ref,
        gain_ref, new_ref, pulls_ref, border_ref, direct_ref, totals_ref, h1_ref, h2_ref,
        first_ref, second_ref, og_ref, gain_grad_ref,
    ):
        totals = (part_ref[...].astype(F32) + other_ref[...].astype(F32)).astype(BF)
        totals_ref[...] = totals
        state = node_ref[...]
        act, slope1 = silu_pair(mm(state, entry_ref[:f, :]) + mm(totals, entry_ref[f:, :]))
        h1n = act.astype(BF)
        h1_ref[...] = h1n
        act, slope2 = silu_pair(mm(h1n, middle_ref[...]))
        h2n = act.astype(BF)
        h2_ref[...] = h2n
        normed, inverse = layer_norm(mm(h2n, outlet_ref[...]))
        new_ref[...] = (state.astype(F32) + gain_ref[...] * normed).astype(BF)
        up = cot_ref[...].astype(F32)
        gain_grad_ref[...] = jnp.sum(up * normed, axis=0, keepdims=True)
        og = norm_backward(up * gain_ref[...], normed, inverse).astype(BF)
        og_ref[...] = og
        second = (mm_nt(og, outlet_ref[...]) * slope2).astype(BF)
        second_ref[...] = second
        first = (mm_nt(second, middle_ref[...]) * slope1).astype(BF)
        first_ref[...] = first
        pulls = mm_nt(first, entry_ref[f:, :]).astype(BF)
        pulls_ref[...] = pulls
        border_ref[...] = mm_tn(hot_rows(send_ref[...], nodes), pulls).astype(BF)
        direct_ref[...] = up + mm_nt(first, entry_ref[:f, :])

    node_outs = call(
        node_kernel,
        [
            shape(nodes, f, BF),
            shape(nodes, f, BF),
            shape(send, f, BF),
            shape(nodes, f, F32),
        ]
        + [shape(nodes, f, BF)] * 6
        + [shape(1, f, F32)],
        part, part_other, node_state, node_cotangent, sends, node_entry, node_middle,
        node_outlet, gain_n,
        flops=2 * nodes * f * f * 8,
    )
    own_new, pulls, pull_border, direct = node_outs[:4]
    node_saved, node_gain_grad = node_outs[4:10], node_outs[10]
    pull_halo = lay.exchange([pull_border] * remote)

    def pull_local(
        spot_ref, place_ref, count_ref, pulls_ref, border_ref, cot_ref, node_ref, totals_ref,
        h1_ref, h2_ref, first_ref, second_ref, og_ref, up_ref, weight_ref,
    ):
        near_table = fold(pulls_ref[...])
        own_table = fold(jnp.concatenate([pulls_ref[...], border_ref[...]], axis=0))
        for b in range(blocks):
            rows = pl.ds(b * size, size)
            spot = spot_ref[b : b + 1, :]
            place = place_ref[b : b + 1, :]
            got = gather_folded(spot, column(spot), near_table)
            got += gather_folded(place, column(place), own_table)
            live = live_column(count_ref, b, size)
            up_ref[rows, :] = cot_ref[rows, :].astype(F32) + live * got
        first = first_ref[...]
        weight_ref[:f, :] = (0.5 * mm_tn(node_ref[...], first)).astype(BF)
        weight_ref[f : 2 * f, :] = (0.5 * mm_tn(totals_ref[...], first)).astype(BF)
        weight_ref[2 * f : 3 * f, :] = (0.5 * mm_tn(h1_ref[...], second_ref[...])).astype(BF)
        weight_ref[3 * f :, :] = (0.5 * mm_tn(h2_ref[...], og_ref[...])).astype(BF)

    up_own, node_weights = call(
        pull_local,
        [shape(edges, f, F32), shape(4 * f, f, BF)],
        spot, place, edge_count, pulls, pull_border, edge_cotangent, node_state, *node_saved,
        smem=(2,),
        flops=2 * edges * f * (nodes + own) + 8 * nodes * f * f,
    )

    subs = lax.axis_size("sub")
    doms = lax.axis_size("dom")
    inners = lax.axis_size("inner")
    unit = 16 * inners * subs
    weight_rows = -(-(9 * f + 16) // unit) * unit
    half = weight_rows // 2
    piece = half // subs
    block_total = doms * subs
    edge_scale = 1.0 / math.sqrt(edges * block_total * inners)
    node_scale = 1.0 / math.sqrt(nodes * block_total)

    def edge_backward(*refs):
        (place_ref, count_ref, up_own_ref, out_pre_ref, s1_ref, s2_ref, h1_ref, h2_ref, edge_ref,
         near_ref, far_ref, middle_ref, outlet_ref, gain_ref, node_ref, node_gain_ref) = refs[:16]
        halo_refs = refs[16 : 16 + remote]
        up_ref, first_ref, keep_ref, give_ref, table, second, output, acc = refs[16 + remote :]
        for j in range(remote):
            table[pl.ds(j * send, send), :] = halo_refs[j][...]
        folded = fold(table[...])
        gain_sum = jnp.zeros((1, f), F32)
        for b in range(blocks):
            rows = pl.ds(b * size, size)
            live = live_column(count_ref, b, size)
            slot = place_ref[b : b + 1, :] - own
            up = up_own_ref[rows, :] + live * gather_folded(slot, column(slot), folded)
            up_ref[rows, :] = up
            into = live * up
            normed, inverse = layer_norm(out_pre_ref[rows, :])
            gain_sum += jnp.sum(into * normed, axis=0, keepdims=True)
            og = norm_backward(into * gain_ref[...], normed, inverse).astype(BF)
            output[rows, :] = og
            second_b = (mm_nt(og, outlet_ref[...]) * s2_ref[rows, :]).astype(BF)
            second[rows, :] = second_b
            first_ref[rows, :] = (mm_nt(second_b, middle_ref[...]) * s1_ref[rows, :]).astype(BF)
        first = first_ref[...]
        acc[:f, :] = mm_tn(edge_ref[...], first).astype(BF)
        acc[f : 2 * f, :] = mm_tn(near_ref[...], first).astype(BF)
        acc[2 * f : 3 * f, :] = mm_tn(far_ref[...], first).astype(BF)
        acc[3 * f : 4 * f, :] = mm_tn(h1_ref[...], second[...]).astype(BF)
        acc[4 * f : 5 * f, :] = mm_tn(h2_ref[...], output[...]).astype(BF)
        acc[5 * f : 9 * f, :] = node_ref[...]
        row = lax.broadcasted_iota(jnp.int32, (weight_rows - 9 * f, f), 0)
        gains = jnp.where(row == 0, gain_sum, 0.0)
        gains = jnp.where(row == 1, node_gain_ref[...] * 0.5, gains)
        acc[9 * f :, :] = gains.astype(BF)
        me = lax.axis_index("inner")
        keep_ref[...] = acc[pl.ds(pl.multiple_of(me * half, 16), half), :]
        give_ref[...] = acc[pl.ds(pl.multiple_of((1 - me) * half, 16), half), :]

    up, first_grad, keep, give = call(
        edge_backward,
        [shape(edges, f, F32), shape(edges, f, BF), shape(half, f, BF), shape(half, f, BF)],
        place, edge_count, up_own, out_pre, s1, s2, h1, h2, edge_state, near_rows, far_rows,
        edge_middle, edge_outlet, gain_e, node_weights, node_gain_grad, *pull_halo,
        smem=(1,),
        scratch=[
            pltpu.VMEM((lay.halo, f), BF),
            pltpu.VMEM((edges, f), BF),
            pltpu.VMEM((edges, f), BF),
            pltpu.VMEM((weight_rows, f), BF),
        ],
        flops=2 * edges * f * (lay.halo + 7 * f),
    )
    got = swap_axis(give, "inner", 1)

    def far_slots(place_ref, first_ref, entry_ref, far_ref, *refs):
        slot_refs, pairs = refs[:-1], refs[-1]
        for b in range(blocks):
            rows = pl.ds(b * size, size)
            far = mm_nt(first_ref[rows, :], entry_ref[2 * f :, :])
            far_ref[rows, :] = far.astype(BF)
            pairs[rows, :] = halves(far, column(place_ref[b : b + 1, :] - own), half_halo)
        hot = folded_hot(whole_row(place_ref) - own, half_halo)
        sums = unfold(mm(hot, pairs[...]).astype(BF))
        for j in range(remote):
            slot_refs[j][...] = sums[j * send : (j + 1) * send]

    far_outs = call(
        far_slots,
        [shape(edges, f, BF)] + [shape(send, f, BF)] * remote,
        place, first_grad, edge_entry,
        scratch=[pltpu.VMEM((edges, 2 * f), BF)],
        flops=2 * edges * f * (lay.halo + f),
    )
    far_grad = far_outs[0]
    back_received = lay.exchange(far_outs[1:])

    def grad_sums(
        spot_ref, place_ref, send_ref, up_ref, first_ref, far_ref, entry_ref, adjoint_ref,
        out_ref, near_pairs, far_pairs,
    ):
        for b in range(blocks):
            rows = pl.ds(b * size, size)
            first = first_ref[rows, :]
            adjoint_ref[rows, :] = (up_ref[rows, :] + mm_nt(first, entry_ref[:f, :])).astype(BF)
            near = mm_nt(first, entry_ref[f : 2 * f, :])
            far = far_ref[rows, :].astype(F32)
            near_pairs[rows, :] = halves(near, column(spot_ref[b : b + 1, :]), half_near)
            far_pairs[rows, :] = halves(far, column(place_ref[b : b + 1, :]), half_own)
        out_ref[...] = local_sums(spot_ref, place_ref, send_ref, near_pairs, far_pairs)

    edge_adjoint, grad_part = call(
        grad_sums,
        [shape(edges, f, BF), shape(nodes, f, F32)],
        spot, place, sends, up, first_grad, far_grad, edge_entry,
        scratch=pair_scratch,
        flops=2 * edges * f * (nodes + own + 2 * f),
    )

    def split_kernel(keep_ref, got_ref, *refs):
        out_refs, acc = refs[:-1], refs[-1]
        acc[...] = (keep_ref[...].astype(F32) + got_ref[...].astype(F32)).astype(BF)
        t = lax.axis_index("sub")
        for x in range(subs):
            out_refs[x][...] = acc[pl.ds(pl.multiple_of((t ^ x) * piece, 16), piece), :]

    pieces = call(
        split_kernel,
        [shape(piece, f, BF)] * subs,
        keep, got,
        scratch=[pltpu.VMEM((half, f), BF)],
    )
    arrived = [pieces[0]] + [swap_axis(pieces[x], "sub", x) for x in range(1, subs)]

    def add_all(values):
        values = [v.astype(F32) for v in values]
        while len(values) > 1:
            values = [values[j] + values[j + 1] for j in range(0, len(values), 2)]
        return values[0]

    total = add_all(arrived)
    stride = 1
    while stride < doms:
        step = 4 if stride * 4 <= doms else 2
        sent = total.astype(BF)
        total = add_all(
            [sent] + [swap_axis(sent, "dom", stride * m) for m in range(1, step)]
        )
        stride *= step
    sent = total.astype(BF)
    own_pieces = [sent] + [swap_axis(sent, "sub", x) for x in range(1, subs)]

    def order_kernel(*refs):
        t = lax.axis_index("sub")
        for x in range(subs):
            refs[-1][pl.ds(pl.multiple_of((t ^ x) * piece, 16), piece), :] = refs[x][...]

    (own_half,) = call(order_kernel, [shape(half, f, BF)], *own_pieces)
    other_half = swap_axis(own_half, "inner", 1)

    def finish_kernel(own_ref, other_ref, edge_ref, node_ref, gain_ref, acc):
        me = lax.axis_index("inner")
        acc[pl.ds(pl.multiple_of(me * half, 16), half), :] = own_ref[...]
        acc[pl.ds(pl.multiple_of((1 - me) * half, 16), half), :] = other_ref[...]
        edge_ref[...] = acc[: 5 * f, :].astype(F32) * edge_scale
        node_ref[...] = acc[5 * f : 9 * f, :].astype(F32) * node_scale
        tail = acc[9 * f : 9 * f + 16, :].astype(F32)
        gain_ref[0:1, :] = tail[0:1, :] * edge_scale
        gain_ref[1:2, :] = tail[1:2, :] * node_scale

    edge_gradient, node_gradient, gain_gradient = call(
        finish_kernel,
        [shape(5 * f, f, F32), shape(4 * f, f, F32), shape(2, f, F32)],
        own_half, other_half,
        scratch=[pltpu.VMEM((weight_rows, f), BF)],
    )

    back, back_other = join(grad_part, back_received)
    node_adjoint = (back.astype(F32) + back_other.astype(F32) + direct).astype(BF)
    return (
        own_new,
        new_edges,
        node_adjoint,
        edge_adjoint,
        edge_gradient,
        node_gradient,
        gain_gradient,
    )


def solution(mesh):
    nodes = P(("groups", "dom", "sub"), None)
    edges = P(("groups", "dom", "sub", "inner"), None)
    slots = P(("groups", "dom", "sub", "inner"))
    return jax.shard_map(
        per_device,
        mesh=mesh,
        in_specs=(
            nodes,
            edges,
            slots,
            slots,
            slots,
            slots,
            P(("groups", "dom", "sub")),
            P(),
            P(),
            P(),
            P(),
            P(),
            P(),
            P(),
            P(),
            nodes,
            edges,
        ),
        out_specs=(
            nodes,
            edges,
            nodes,
            edges,
            P("groups", None),
            P("groups", None),
            P("groups", None),
        ),
        check_vma=False,
    )
```

time: 98.1 us -> 84.4 us (0.86)
  Pallas kernels: 29.9 us -> 21.1 us
  waiting for transfers between devices: 12.1 us -> 9.58 us
  local copies, waits for them, and re-layouts: 5.55 us -> 4.13 us
    pallas_call x14, Pallas kernels: 29.9 us -> 21.1 us  [call(): pl.pallas_call(body, out_shape=outs, in_specs=specs, out_specs=[pl.BlockS...]
    ppermute x9, starting transfers between devices: 10.4 us -> 6.39 us  [swap_axis(): return lax.ppermute(value, axis, [(j, j ^ mask) for j in range(count)])]
    ppermute x20, starting transfers between devices: 37 us -> 40.3 us  [exchange(): out.append(lax.ppermute(value, AXES, pairs))]
    ppermute x9, waiting for transfers between devices: 9.84 us -> 8.35 us  [swap_axis(): return lax.ppermute(value, axis, [(j, j ^ mask) for j in range(count)])]
    reshape x2 -> x0, local copies, waits for them, and re-layouts: 1.41 us -> none  [the longest x1 0.71 us: per_device(): other = edge_other.reshape(blocks, size)]
    ppermute x20, waiting for transfers between devices: 2.26 us -> 1.23 us  [exchange(): out.append(lax.ppermute(value, AXES, pairs))]
  transfers between devices with their start and end apart: 29 -> 29, of which waited for: 9 -> 7; matrix products, arithmetic and copies ran while one was open for 2% -> 1% of each run, Pallas kernels for 10% -> 11%
where the time goes in v2:
time: 84.4 us; the launch traced here: 84 us
  starting transfers between devices  46.7 us (55%)
  Pallas kernels  21.1 us (25%)
  waiting for transfers between devices  9.58 us (11%)
  local copies, waits for them, and re-layouts  4.13 us (5%)
  between operations  1.72 us (2%)
    ppermute x20, starting transfers between devices, exchange(): out.append(lax.ppermute(value, AXES, pairs))  40.3 us
    pallas_call x14, Pallas kernels, call(): pl.pallas_call(body, out_shape=outs, in_specs=specs, out_specs=[pl.BlockS...  21.1 us
    ppermute x9, waiting for transfers between devices, swap_axis(): return lax.ppermute(value, axis, [(j, j ^ mask) for j in range(count)])  8.35 us
    ppermute x9, starting transfers between devices, swap_axis(): return lax.ppermute(value, axis, [(j, j ^ mask) for j in range(count)])  6.39 us
    unnamed x38, local copies, waits for them, and re-layouts  4.13 us
  transfers between devices with their start and end apart: 29, of which 7 were waited for; matrix products, arithmetic and copies ran while one was open for 1% of the time, Pallas kernels for 11%

profile of v2, /device:TPU:0, one launch (start us, length us, event | category | flops | bytes accessed | tf_op | source)
XLA Modules:
  0.0 84.0 jit_solution(5514966704338109649)
XLA Ops:
  1.3 0.9 %copy-done = bf16[512,128]{1,0:T(8,128)(2,1)S(1)} copy-done((bf16[512,128]{1,0:T(8,128)(2,1)S(1)}, bf16[512,128]{1,0:T(8,128)(2,1)}, u32[]{:S(2)}) %copy-start) | copy-done | bytes 131096
  2.5 4.0 %collective-permute-start.4 = (bf16[256,128]{1,0:T(8,128)(2,1)S(1)}, bf16[256,128]{1,0:T(8,128)(2,1)S(1)}, u32[]{:S(2)}, u32[]{:S(2)}) collective-permute-start(bf16[256,128]{1,0:T(8,128)(2,1)S(1)} %shard_map.216.border_ref), channel_id=1, source_target_pairs={{0,6},{1,7},{2,4},{3,5},{4,2},{5,3},{6,0},{7,1},{8,14},{9,15},{10,... | collective-permute-start | bytes 196616 | tf_op jit(solution)/shard_map/ppermute | solution.py:131
  7.8 5.3 %collective-permute-start.1 = (bf16[256,128]{1,0:T(8,128)(2,1)S(1)}, bf16[256,128]{1,0:T(8,128)(2,1)S(1)}, u32[]{:S(2)}, u32[]{:S(2)}) collective-permute-start(bf16[256,128]{1,0:T(8,128)(2,1)S(1)} %shard_map.216.border_ref), channel_id=1, source_target_pairs={{0,4},{1,5},{2,6},{3,7},{4,0},{5,1},{6,2},{7,3},{8,12},{9,13},{10,... | collective-permute-start | bytes 196616 | tf_op jit(solution)/shard_map/ppermute | solution.py:131
  14.5 1.0 %copy-done.2 = bf16[1536,128]{1,0:T(8,128)(2,1)S(1)} copy-done((bf16[1536,128]{1,0:T(8,128)(2,1)S(1)}, bf16[1536,128]{1,0:T(8,128)(2,1)}, u32[]{:S(2)}) %copy-start.2) | copy-done | bytes 393240
  15.5 0.9 %copy-done.14 = bf16[384,128]{1,0:T(8,128)(2,1)S(1)} copy-done((bf16[384,128]{1,0:T(8,128)(2,1)S(1)}, bf16[384,128]{1,0:T(8,128)(2,1)}, u32[]{:S(2)}) %copy-start.14) | copy-done | bytes 98328
  16.4 2.3 %shard_map.217 = (bf16[1536,128]{1,0:T(8,128)(2,1)S(1)}, bf16[1536,128]{1,0:T(8,128)(2,1)S(1)}, f32[1536,128]{1,0:T(8,128)S(1)}, s32[6,256]{1,0:T(8,128)S(1)}, s32[6,256]{1,0:T(8,128)S(1)}) custom-call(s32[1536]{0:T(1024)S(1)} %copy-done.16, s32[1536]{0:T(1024)S(1)} %copy-done.17, s32[6]{0:T(128)S(1)} %copy-done.18, bf16[512,128]{1,0:T(8,128)(2,1)S(1)} %copy-done.1, ...), custom_call_target="tpu_custom_call" | custom-call | flops 603979776 | bytes 2285592 | tf_op jit(solution)/shard_map/pallas_call | solution.py:146
  19.4 4.0 %shard_map.218 = (bf16[1536,128]{1,0:T(8,128)(2,1)S(1)}, bf16[1536,128]{1,0:T(8,128)(2,1)S(1)}, bf16[1536,128]{1,0:T(8,128)(2,1)S(1)}, bf16[1536,128]{1,0:T(8,12...) custom-call(s32[6,256]{1,0:T(8,128)S(1)} %get-tuple-element.57.refs_, ...), custom_call_target="tpu_custom_call" | custom-call | flops 1157627904 | bytes 6330884 | tf_op jit(solution)/shard_map/pallas_call | solution.py:146
  24.1 4.6 %collective-permute-start.6 = (bf16[256,128]{1,0:T(8,128)(2,1)S(1)}, bf16[256,128]{1,0:T(8,128)(2,1)S(1)}, u32[]{:S(2)}, u32[]{:S(2)}) collective-permute-start(bf16[256,128]{1,0:T(8,128)(2,1)S(1)} %get-tuple-element.63), channel_id=1, source_target_pairs={{0,4},{1,5},{2,6},{3,7},{4,0},{5,1},{6,2},{7,3},{8,12},{9,13},{10,... | collective-permute-start | bytes 196616 | tf_op jit(solution)/shard_map/ppermute | solution.py:131
  29.9 2.3 %collective-permute-start.9 = (bf16[256,128]{1,0:T(8,128)(2,1)S(1)}, bf16[256,128]{1,0:T(8,128)(2,1)S(1)}, u32[]{:S(2)}, u32[]{:S(2)}) collective-permute-start(bf16[256,128]{1,0:T(8,128)(2,1)S(1)} %get-tuple-element.66), channel_id=1, source_target_pairs={{0,6},{1,7},{2,4},{3,5},{4,2},{5,3},{6,0},{7,1},{8,14},{9,15},{10,... | collective-permute-start | bytes 196616 | tf_op jit(solution)/shard_map/ppermute | solution.py:131
  32.2 1.7 %shard_map.219 = (bf16[1536,128]{1,0:T(8,128)(2,1)}, f32[512,128]{1,0:T(8,128)S(1)}) custom-call(s32[6,256]{1,0:T(8,128)S(1)} %get-tuple-element.56.spot_ref, s32[6,256]{1,0:T(8,128)S(1)} %get-tuple-element.57.refs_0_.place_ref, s32[1,256]{1,0:T(1,128)S(1)} %bitcast.4, s32[1]{0:T(128)S(6)} %copy.24.refs_1_.count_ref, bf16[1536,128]{1,0:T(8,128)(2,1)S(1)} %copy-done.3, ...), custom_call_target="tpu_custom_call" | custom-call | flops 503316480 | bytes 1455108 | tf_op jit(solution)/shard_map/pallas_call | solution.py:146
  34.0 1.2 %collective-permute-done.9.refs_4_ = bf16[256,128]{1,0:T(8,128)(2,1)S(1)} collective-permute-done((bf16[256,128]{1,0:T(8,128)(2,1)S(1)}, bf16[256,128]{1,0:T(8,128)(2,1)S(1)}, u32[]{:S(2)}, u32[]{:S(2)}) %collective-permute-start.9) | collective-permute-done | bytes 65568 | tf_op jit(solution)/shard_map/ppermute | solution.py:131
  35.8 1.3 %collective-permute-done.10.other_ref = bf16[512,128]{1,0:T(8,128)(2,1)S(1)} collective-permute-done((bf16[512,128]{1,0:T(8,128)(2,1)S(1)}, bf16[512,128]{1,0:T(8,128)(2,1)S(1)}, u32[]{:S(2)}, u32[]{:S(2)}) %collective-permute-start.10) | collective-permute-done | bytes 131104 | tf_op jit(solution)/shard_map/ppermute | solution.py:137
  37.1 1.9 %shard_map.221 = (bf16[512,128]{1,0:T(8,128)(2,1)}, bf16[512,128]{1,0:T(8,128)(2,1)S(1)}, bf16[256,128]{1,0:T(8,128)(2,1)S(1)}, f32[512,128]{1,0:T(8,128)S(1)}, ...) custom-call(bf16[512,128]{1,0:T(8,128)(2,1)S(1)} %shard_map.220.part, ...), custom_call_target="tpu_custom_call" | custom-call | flops 134217728 | bytes 2033664 | tf_op jit(solution)/shard_map/pallas_call | solution.py:146
  39.0 2.9 %collective-permute-start.15 = (bf16[256,128]{1,0:T(8,128)(2,1)S(1)}, bf16[256,128]{1,0:T(8,128)(2,1)S(1)}, u32[]{:S(2)}, u32[]{:S(2)}) collective-permute-start(bf16[256,128]{1,0:T(8,128)(2,1)S(1)} %get-tuple-element.70.border_ref), channel_id=1, source_target_pairs={{0,6},{1,7},{2,4},{3,5},{4,2},{5,3},{6,0},{7,1},{8,14},{9,15},{10,... | collective-permute-start | bytes 196616 | tf_op jit(solution)/shard_map/ppermute | solution.py:131
  42.5 0.9 %collective-permute-start.13 = (bf16[256,128]{1,0:T(8,128)(2,1)S(1)}, bf16[256,128]{1,0:T(8,128)(2,1)S(1)}, u32[]{:S(2)}, u32[]{:S(2)}) collective-permute-start(bf16[256,128]{1,0:T(8,128)(2,1)S(1)} %get-tuple-element.70.border_ref), channel_id=1, source_target_pairs={{0,2},{1,3},{2,0},{3,1},{4,6},{5,7},{6,4},{7,5},{8,10},{9,11},{10,... | collective-permute-start | bytes 196616 | tf_op jit(solution)/shard_map/ppermute | solution.py:131
  43.5 3.3 %collective-permute-start.12 = (bf16[256,128]{1,0:T(8,128)(2,1)S(1)}, bf16[256,128]{1,0:T(8,128)(2,1)S(1)}, u32[]{:S(2)}, u32[]{:S(2)}) collective-permute-start(bf16[256,128]{1,0:T(8,128)(2,1)S(1)} %get-tuple-element.70.border_ref), channel_id=1, source_target_pairs={{0,4},{1,5},{2,6},{3,7},{4,0},{5,1},{6,2},{7,3},{8,12},{9,13},{10,... | collective-permute-start | bytes 196616 | tf_op jit(solution)/shard_map/ppermute | solution.py:131
  46.7 0.8 collective-permute-start.11
  47.6 1.9 %shard_map.222 = (f32[1536,128]{1,0:T(8,128)S(1)}, bf16[512,128]{1,0:T(8,128)(2,1)S(1)}) custom-call(s32[6,256]{1,0:T(8,128)S(1)} %get-tuple-element.56.spot_ref, s32[6,256]{1,0:T(8,128)S(1)} %get-tuple-element.57.refs_0_.place_ref, s32[1]{0:T(128)S(6)} %copy.24.refs_1_.count_ref, bf16[512,128]{1,0:T(8,128)(2,1)S(1)} %get-tuple-element.69.pulls_ref, ...), custom_call_target="tpu_custom_call" | custom-call | flops 570425344 | bytes 2437124 | tf_op jit(solution)/shard_map/pallas_call | solution.py:146
  49.5 4.1 %shard_map.223 = (f32[1536,128]{1,0:T(8,128)S(1)}, bf16[1536,128]{1,0:T(8,128)(2,1)S(1)}, bf16[608,128]{1,0:T(8,128)(2,1)S(1)}, bf16[608,128]{1,0:T(8,128)(2,1)S(1)}) custom-call(s32[6,256]{1,0:T(8,128)S(1)} %get-tuple-element.57.refs_0_.place_ref, s32[1]{0:T(128)S(6)} %copy.24.refs_1_.count_ref, f32[1536,128]{1,0:T(8,128)S(1)} %get-tuple-element.77.refs_2_, ...), custom_call_target="tpu_custom_call" | custom-call | flops 855638016 | bytes 7134212 | tf_op jit(solution)/shard_map/pallas_call | solution.py:146
  53.7 1.4 %collective-permute-done.22.got_ref = bf16[608,128]{1,0:T(8,128)(2,1)S(1)} collective-permute-done((bf16[608,128]{1,0:T(8,128)(2,1)S(1)}, bf16[608,128]{1,0:T(8,128)(2,1)S(1)}, u32[]{:S(2)}, u32[]{:S(2)}) %collective-permute-start.22) | collective-permute-done | bytes 155680 | tf_op jit(solution)/shard_map/ppermute | solution.py:137
  55.8 1.0 %shard_map.224 = (bf16[1536,128]{1,0:T(8,128)(2,1)S(1)}, bf16[256,128]{1,0:T(8,128)(2,1)S(1)}, bf16[256,128]{1,0:T(8,128)(2,1)S(1)}, bf16[256,128]{1,0:T(8,128)(...) custom-call(s32[6,256]{1,0:T(8,128)S(1)} %get-tuple-element.57.refs_0_.place_ref, ...), custom_call_target="tpu_custom_call" | custom-call | flops 553648128 | bytes 1218560 | tf_op jit(solution)/shard_map/pallas_call | solution.py:146
  57.5 5.4 %collective-permute-start.17 = (bf16[256,128]{1,0:T(8,128)(2,1)S(1)}, bf16[256,128]{1,0:T(8,128)(2,1)S(1)}, u32[]{:S(2)}, u32[]{:S(2)}) collective-permute-start(bf16[256,128]{1,0:T(8,128)(2,1)S(1)} %get-tuple-element.92), channel_id=1, source_target_pairs={{0,4},{1,5},{2,6},{3,7},{4,0},{5,1},{6,2},{7,3},{8,12},{9,13},{10,... | collective-permute-start | bytes 196616 | tf_op jit(solution)/shard_map/ppermute | solution.py:131
  62.9 1.5 %collective-permute-start.18 = (bf16[256,128]{1,0:T(8,128)(2,1)S(1)}, bf16[256,128]{1,0:T(8,128)(2,1)S(1)}, u32[]{:S(2)}, u32[]{:S(2)}) collective-permute-start(bf16[256,128]{1,0:T(8,128)(2,1)S(1)} %get-tuple-element.93), channel_id=1, source_target_pairs={{0,2},{1,3},{2,0},{3,1},{4,6},{5,7},{6,4},{7,5},{8,10},{9,11},{10,... | collective-permute-start | bytes 196616 | tf_op jit(solution)/shard_map/ppermute | solution.py:131
  65.1 3.5 %collective-permute-start.20 = (bf16[256,128]{1,0:T(8,128)(2,1)S(1)}, bf16[256,128]{1,0:T(8,128)(2,1)S(1)}, u32[]{:S(2)}, u32[]{:S(2)}) collective-permute-start(bf16[256,128]{1,0:T(8,128)(2,1)S(1)} %get-tuple-element.95), channel_id=1, source_target_pairs={{0,6},{1,7},{2,4},{3,5},{4,2},{5,3},{6,0},{7,1},{8,14},{9,15},{10,... | collective-permute-start | bytes 196616 | tf_op jit(solution)/shard_map/ppermute | solution.py:131
  68.6 1.7 %collective-permute-start.26 = (bf16[304,128]{1,0:T(8,128)(2,1)S(1)}, bf16[304,128]{1,0:T(8,128)(2,1)S(1)}, u32[]{:S(2)}, u32[]{:S(2)}) collective-permute-start(bf16[304,128]{1,0:T(8,128)(2,1)S(1)} %add_convert_fusion.2), channel_id=1, source_target_pairs={{0,12},{4,8},{8,4},{12,0},{1,13},{5,9},{9,5},{13,1},{2,14},{6,10},... | collective-permute-start | bytes 233480 | tf_op jit(solution)/shard_map/ppermute | solution.py:137
  70.4 2.7 %collective-permute-start.24 = (bf16[304,128]{1,0:T(8,128)(2,1)S(1)}, bf16[304,128]{1,0:T(8,128)(2,1)S(1)}, u32[]{:S(2)}, u32[]{:S(2)}) collective-permute-start(bf16[304,128]{1,0:T(8,128)(2,1)S(1)} %add_convert_fusion.2), channel_id=1, source_target_pairs={{0,4},{4,0},{8,12},{12,8},{1,5},{5,1},{9,13},{13,9},{2,6},{6,2},{1... | collective-permute-start | bytes 233480 | tf_op jit(solution)/shard_map/ppermute | solution.py:137
  73.1 1.8 %shard_map.225 = (bf16[1536,128]{1,0:T(8,128)(2,1)}, f32[512,128]{1,0:T(8,128)S(1)}) custom-call(s32[6,256]{1,0:T(8,128)S(1)} %get-tuple-element.56.spot_ref, s32[6,256]{1,0:T(8,128)S(1)} %get-tuple-element.57.refs_0_.place_ref, s32[1,256]{1,0:T(1,128)S(1)} %bitcast.7, f32[1536,128]{1,0:T(8,128)S(1)} %get-tuple-element.87.up_ref, ...), custom_call_target="tpu_custom_call" | custom-call | flops 603979776 | bytes 2339840 | tf_op jit(solution)/shard_map/pallas_call | solution.py:146
  76.0 1.1 %collective-permute-done.25 = bf16[304,128]{1,0:T(8,128)(2,1)S(1)} collective-permute-done((bf16[304,128]{1,0:T(8,128)(2,1)S(1)}, bf16[304,128]{1,0:T(8,128)(2,1)S(1)}, u32[]{:S(2)}, u32[]{:S(2)}) %collective-permute-start.25) | collective-permute-done | bytes 77856 | tf_op jit(solution)/shard_map/ppermute | solution.py:137
  77.2 1.1 %collective-permute-start.27 = (bf16[304,128]{1,0:T(8,128)(2,1)S(1)}, bf16[304,128]{1,0:T(8,128)(2,1)S(1)}, u32[]{:S(2)}, u32[]{:S(2)}) collective-permute-start(bf16[304,128]{1,0:T(8,128)(2,1)S(1)} %add_convert_fusion.1.refs_0_), channel_id=1, source_target_pairs={{0,2},{2,0},{1,3},{3,1},{4,6},{6,4},{5,7},{7,5},{8,10},{10,8},{9,1... | collective-permute-start | bytes 233480 | tf_op jit(solution)/shard_map/ppermute | solution.py:137
  78.3 3.4 %collective-permute-done.27.refs_1_ = bf16[304,128]{1,0:T(8,128)(2,1)S(1)} collective-permute-done((bf16[304,128]{1,0:T(8,128)(2,1)S(1)}, bf16[304,128]{1,0:T(8,128)(2,1)S(1)}, u32[]{:S(2)}, u32[]{:S(2)}) %collective-permute-start.27) | collective-permute-done | bytes 77856 | tf_op jit(solution)/shard_map/ppermute | solution.py:137
  81.8 0.7 add_convert_fusion
  83.1 0.9 %shard_map.229 = (f32[640,128]{1,0:T(8,128)}, f32[512,128]{1,0:T(8,128)}, f32[2,128]{1,0:T(2,128)}) custom-call(bf16[608,128]{1,0:T(8,128)(2,1)S(1)} %shard_map.228.own_ref, bf16[608,128]{1,0:T(8,128)(2,1)S(1)} %collective-permute-done.28.other_ref), custom_call_target="tpu_custom_call" | custom-call | bytes 902144 | tf_op jit(solution)/shard_map/pallas_call | solution.py:146
  (81 shorter events, 10.6 us)
Async XLA Ops:
  2.2 12.2 %copy-start.1 = (bf16[512,128]{1,0:T(8,128)(2,1)S(1)}, bf16[512,128]{1,0:T(8,128)(2,1)}, u32[]{:S(2)}) copy-start(bf16[512,128]{1,0:T(8,128)(2,1)} %node_ref.5) | copy-start | bytes 393220
  2.2 12.2 %copy-start.16 = (s32[1536]{0:T(1024)S(1)}, s32[1536]{0:T(1024)}, u32[]{:S(2)}) copy-start(s32[1536]{0:T(1024)} %off_ref.1) | copy-start | bytes 18436
  2.2 12.2 %copy-start.17 = (s32[1536]{0:T(1024)S(1)}, s32[1536]{0:T(1024)}, u32[]{:S(2)}) copy-start(s32[1536]{0:T(1024)} %oth_ref.1) | copy-start | bytes 18436
  2.5 16.2 %collective-permute-start.4 = (bf16[256,128]{1,0:T(8,128)(2,1)S(1)}, bf16[256,128]{1,0:T(8,128)(2,1)S(1)}, u32[]{:S(2)}, u32[]{:S(2)}) collective-permute-start(bf16[256,128]{1,0:T(8,128)(2,1)S(1)} %shard_map.216.border_ref), channel_id=1, source_target_pairs={{0,6},{1,7},{2,4},{3,5},{4,2},{5,3},{6,0},{7,1},{8,14},{9,15},{10,... | collective-permute-start | bytes 196616 | tf_op jit(solution)/shard_map/ppermute | solution.py:131
  6.5 12.2 %collective-permute-start.3 = (bf16[256,128]{1,0:T(8,128)(2,1)S(1)}, bf16[256,128]{1,0:T(8,128)(2,1)S(1)}, u32[]{:S(2)}, u32[]{:S(2)}) collective-permute-start(bf16[256,128]{1,0:T(8,128)(2,1)S(1)} %shard_map.216.border_ref), channel_id=1, source_target_pairs={{4,10},{5,11},{6,8},{7,9},{8,6},{9,7},{10,4},{11,5},{20,26},{21,27... | collective-permute-start | bytes 196616 | tf_op jit(solution)/shard_map/ppermute | solution.py:131
  7.2 11.6 %collective-permute-start.2 = (bf16[256,128]{1,0:T(8,128)(2,1)S(1)}, bf16[256,128]{1,0:T(8,128)(2,1)S(1)}, u32[]{:S(2)}, u32[]{:S(2)}) collective-permute-start(bf16[256,128]{1,0:T(8,128)(2,1)S(1)} %shard_map.216.border_ref), channel_id=1, source_target_pairs={{0,2},{1,3},{2,0},{3,1},{4,6},{5,7},{6,4},{7,5},{8,10},{9,11},{10,... | collective-permute-start | bytes 196616 | tf_op jit(solution)/shard_map/ppermute | solution.py:131
  7.8 11.0 %collective-permute-start.1 = (bf16[256,128]{1,0:T(8,128)(2,1)S(1)}, bf16[256,128]{1,0:T(8,128)(2,1)S(1)}, u32[]{:S(2)}, u32[]{:S(2)}) collective-permute-start(bf16[256,128]{1,0:T(8,128)(2,1)S(1)} %shard_map.216.border_ref), channel_id=1, source_target_pairs={{0,4},{1,5},{2,6},{3,7},{4,0},{5,1},{6,2},{7,3},{8,12},{9,13},{10,... | collective-permute-start | bytes 196616 | tf_op jit(solution)/shard_map/ppermute | solution.py:131
  13.1 5.6 %collective-permute-start = (bf16[256,128]{1,0:T(8,128)(2,1)S(1)}, bf16[256,128]{1,0:T(8,128)(2,1)S(1)}, u32[]{:S(2)}, u32[]{:S(2)}) collective-permute-start(bf16[256,128]{1,0:T(8,128)(2,1)S(1)} %shard_map.216.border_ref), channel_id=1, source_target_pairs={{4,8},{5,9},{6,10},{7,11},{8,4},{9,5},{10,6},{11,7},{20,24},{21,25... | collective-permute-start | bytes 196616 | tf_op jit(solution)/shard_map/ppermute | solution.py:131
  23.5 10.5 %collective-permute-start.5 = (bf16[256,128]{1,0:T(8,128)(2,1)S(1)}, bf16[256,128]{1,0:T(8,128)(2,1)S(1)}, u32[]{:S(2)}, u32[]{:S(2)}) collective-permute-start(bf16[256,128]{1,0:T(8,128)(2,1)S(1)} %get-tuple-element.62), channel_id=1, source_target_pairs={{4,8},{5,9},{6,10},{7,11},{8,4},{9,5},{10,6},{11,7},{20,24},{21,25... | collective-permute-start | bytes 196616 | tf_op jit(solution)/shard_map/ppermute | solution.py:131
  24.1 9.8 %collective-permute-start.6 = (bf16[256,128]{1,0:T(8,128)(2,1)S(1)}, bf16[256,128]{1,0:T(8,128)(2,1)S(1)}, u32[]{:S(2)}, u32[]{:S(2)}) collective-permute-start(bf16[256,128]{1,0:T(8,128)(2,1)S(1)} %get-tuple-element.63), channel_id=1, source_target_pairs={{0,4},{1,5},{2,6},{3,7},{4,0},{5,1},{6,2},{7,3},{8,12},{9,13},{10,... | collective-permute-start | bytes 196616 | tf_op jit(solution)/shard_map/ppermute | solution.py:131
  28.7 5.2 %collective-permute-start.7 = (bf16[256,128]{1,0:T(8,128)(2,1)S(1)}, bf16[256,128]{1,0:T(8,128)(2,1)S(1)}, u32[]{:S(2)}, u32[]{:S(2)}) collective-permute-start(bf16[256,128]{1,0:T(8,128)(2,1)S(1)} %get-tuple-element.64), channel_id=1, source_target_pairs={{0,2},{1,3},{2,0},{3,1},{4,6},{5,7},{6,4},{7,5},{8,10},{9,11},{10,... | collective-permute-start | bytes 196616 | tf_op jit(solution)/shard_map/ppermute | solution.py:131
  29.3 4.7 %collective-permute-start.8 = (bf16[256,128]{1,0:T(8,128)(2,1)S(1)}, bf16[256,128]{1,0:T(8,128)(2,1)S(1)}, u32[]{:S(2)}, u32[]{:S(2)}) collective-permute-start(bf16[256,128]{1,0:T(8,128)(2,1)S(1)} %get-tuple-element.65), channel_id=1, source_target_pairs={{4,10},{5,11},{6,8},{7,9},{8,6},{9,7},{10,4},{11,5},{20,26},{21,27... | collective-permute-start | bytes 196616 | tf_op jit(solution)/shard_map/ppermute | solution.py:131
  29.9 5.2 %collective-permute-start.9 = (bf16[256,128]{1,0:T(8,128)(2,1)S(1)}, bf16[256,128]{1,0:T(8,128)(2,1)S(1)}, u32[]{:S(2)}, u32[]{:S(2)}) collective-permute-start(bf16[256,128]{1,0:T(8,128)(2,1)S(1)} %get-tuple-element.66), channel_id=1, source_target_pairs={{0,6},{1,7},{2,4},{3,5},{4,2},{5,3},{6,0},{7,1},{8,14},{9,15},{10,... | collective-permute-start | bytes 196616 | tf_op jit(solution)/shard_map/ppermute | solution.py:131
  35.7 1.4 %collective-permute-start.10 = (bf16[512,128]{1,0:T(8,128)(2,1)S(1)}, bf16[512,128]{1,0:T(8,128)(2,1)S(1)}, u32[]{:S(2)}, u32[]{:S(2)}) collective-permute-start(bf16[512,128]{1,0:T(8,128)(2,1)S(1)} %shard_map.220.part_ref), channel_id=1, source_target_pairs={{0,1},{1,0},{2,3},{3,2},{4,5},{5,4},{6,7},{7,6},{8,9},{9,8},{10,11... | collective-permute-start | bytes 393224 | tf_op jit(solution)/shard_map/ppermute | solution.py:137
  39.0 10.5 %collective-permute-start.15 = (bf16[256,128]{1,0:T(8,128)(2,1)S(1)}, bf16[256,128]{1,0:T(8,128)(2,1)S(1)}, u32[]{:S(2)}, u32[]{:S(2)}) collective-permute-start(bf16[256,128]{1,0:T(8,128)(2,1)S(1)} %get-tuple-element.70.border_ref), channel_id=1, source_target_pairs={{0,6},{1,7},{2,4},{3,5},{4,2},{5,3},{6,0},{7,1},{8,14},{9,15},{10,... | collective-permute-start | bytes 196616 | tf_op jit(solution)/shard_map/ppermute | solution.py:131
  41.9 7.6 %collective-permute-start.14 = (bf16[256,128]{1,0:T(8,128)(2,1)S(1)}, bf16[256,128]{1,0:T(8,128)(2,1)S(1)}, u32[]{:S(2)}, u32[]{:S(2)}) collective-permute-start(bf16[256,128]{1,0:T(8,128)(2,1)S(1)} %get-tuple-element.70.border_ref), channel_id=1, source_target_pairs={{4,10},{5,11},{6,8},{7,9},{8,6},{9,7},{10,4},{11,5},{20,26},{21,27... | collective-permute-start | bytes 196616 | tf_op jit(solution)/shard_map/ppermute | solution.py:131
  42.5 7.0 %collective-permute-start.13 = (bf16[256,128]{1,0:T(8,128)(2,1)S(1)}, bf16[256,128]{1,0:T(8,128)(2,1)S(1)}, u32[]{:S(2)}, u32[]{:S(2)}) collective-permute-start(bf16[256,128]{1,0:T(8,128)(2,1)S(1)} %get-tuple-element.70.border_ref), channel_id=1, source_target_pairs={{0,2},{1,3},{2,0},{3,1},{4,6},{5,7},{6,4},{7,5},{8,10},{9,11},{10,... | collective-permute-start | bytes 196616 | tf_op jit(solution)/shard_map/ppermute | solution.py:131
  43.5 6.1 %collective-permute-start.12 = (bf16[256,128]{1,0:T(8,128)(2,1)S(1)}, bf16[256,128]{1,0:T(8,128)(2,1)S(1)}, u32[]{:S(2)}, u32[]{:S(2)}) collective-permute-start(bf16[256,128]{1,0:T(8,128)(2,1)S(1)} %get-tuple-element.70.border_ref), channel_id=1, source_target_pairs={{0,4},{1,5},{2,6},{3,7},{4,0},{5,1},{6,2},{7,3},{8,12},{9,13},{10,... | collective-permute-start | bytes 196616 | tf_op jit(solution)/shard_map/ppermute | solution.py:131
  46.7 2.8 %collective-permute-start.11 = (bf16[256,128]{1,0:T(8,128)(2,1)S(1)}, bf16[256,128]{1,0:T(8,128)(2,1)S(1)}, u32[]{:S(2)}, u32[]{:S(2)}) collective-permute-start(bf16[256,128]{1,0:T(8,128)(2,1)S(1)} %get-tuple-element.70.border_ref), channel_id=1, source_target_pairs={{4,8},{5,9},{6,10},{7,11},{8,4},{9,5},{10,6},{11,7},{20,24},{21,25... | collective-permute-start | bytes 196616 | tf_op jit(solution)/shard_map/ppermute | solution.py:131
  53.7 1.4 %collective-permute-start.22 = (bf16[608,128]{1,0:T(8,128)(2,1)S(1)}, bf16[608,128]{1,0:T(8,128)(2,1)S(1)}, u32[]{:S(2)}, u32[]{:S(2)}) collective-permute-start(bf16[608,128]{1,0:T(8,128)(2,1)S(1)} %get-tuple-element.99), channel_id=1, source_target_pairs={{0,1},{1,0},{2,3},{3,2},{4,5},{5,4},{6,7},{7,6},{8,9},{9,8},{10,11... | collective-permute-start | bytes 466952 | tf_op jit(solution)/shard_map/ppermute | solution.py:137
  55.2 9.9 %collective-permute-start.23 = (bf16[304,128]{1,0:T(8,128)(2,1)S(1)}, bf16[304,128]{1,0:T(8,128)(2,1)S(1)}, u32[]{:S(2)}, u32[]{:S(2)}) collective-permute-start(bf16[304,128]{1,0:T(8,128)(2,1)S(1)} %get-tuple-element.101), channel_id=1, source_target_pairs={{0,2},{2,0},{1,3},{3,1},{4,6},{6,4},{5,7},{7,5},{8,10},{10,8},{9,1... | collective-permute-start | bytes 233480 | tf_op jit(solution)/shard_map/ppermute | solution.py:137
  56.8 11.8 %collective-permute-start.16 = (bf16[256,128]{1,0:T(8,128)(2,1)S(1)}, bf16[256,128]{1,0:T(8,128)(2,1)S(1)}, u32[]{:S(2)}, u32[]{:S(2)}) collective-permute-start(bf16[256,128]{1,0:T(8,128)(2,1)S(1)} %get-tuple-element.91), channel_id=1, source_target_pairs={{4,8},{5,9},{6,10},{7,11},{8,4},{9,5},{10,6},{11,7},{20,24},{21,25... | collective-permute-start | bytes 196616 | tf_op jit(solution)/shard_map/ppermute | solution.py:131
  57.5 12.9 %collective-permute-start.17 = (bf16[256,128]{1,0:T(8,128)(2,1)S(1)}, bf16[256,128]{1,0:T(8,128)(2,1)S(1)}, u32[]{:S(2)}, u32[]{:S(2)}) collective-permute-start(bf16[256,128]{1,0:T(8,128)(2,1)S(1)} %get-tuple-element.92), channel_id=1, source_target_pairs={{0,4},{1,5},{2,6},{3,7},{4,0},{5,1},{6,2},{7,3},{8,12},{9,13},{10,... | collective-permute-start | bytes 196616 | tf_op jit(solution)/shard_map/ppermute | solution.py:131
  62.9 7.5 %collective-permute-start.18 = (bf16[256,128]{1,0:T(8,128)(2,1)S(1)}, bf16[256,128]{1,0:T(8,128)(2,1)S(1)}, u32[]{:S(2)}, u32[]{:S(2)}) collective-permute-start(bf16[256,128]{1,0:T(8,128)(2,1)S(1)} %get-tuple-element.93), channel_id=1, source_target_pairs={{0,2},{1,3},{2,0},{3,1},{4,6},{5,7},{6,4},{7,5},{8,10},{9,11},{10,... | collective-permute-start | bytes 196616 | tf_op jit(solution)/shard_map/ppermute | solution.py:131
  64.4 10.6 %collective-permute-start.19 = (bf16[256,128]{1,0:T(8,128)(2,1)S(1)}, bf16[256,128]{1,0:T(8,128)(2,1)S(1)}, u32[]{:S(2)}, u32[]{:S(2)}) collective-permute-start(bf16[256,128]{1,0:T(8,128)(2,1)S(1)} %get-tuple-element.94), channel_id=1, source_target_pairs={{4,10},{5,11},{6,8},{7,9},{8,6},{9,7},{10,4},{11,5},{20,26},{21,27... | collective-permute-start | bytes 196616 | tf_op jit(solution)/shard_map/ppermute | solution.py:131
  65.1 9.9 %collective-permute-start.20 = (bf16[256,128]{1,0:T(8,128)(2,1)S(1)}, bf16[256,128]{1,0:T(8,128)(2,1)S(1)}, u32[]{:S(2)}, u32[]{:S(2)}) collective-permute-start(bf16[256,128]{1,0:T(8,128)(2,1)S(1)} %get-tuple-element.95), channel_id=1, source_target_pairs={{0,6},{1,7},{2,4},{3,5},{4,2},{5,3},{6,0},{7,1},{8,14},{9,15},{10,... | collective-permute-start | bytes 196616 | tf_op jit(solution)/shard_map/ppermute | solution.py:131
  68.6 7.3 %collective-permute-start.26 = (bf16[304,128]{1,0:T(8,128)(2,1)S(1)}, bf16[304,128]{1,0:T(8,128)(2,1)S(1)}, u32[]{:S(2)}, u32[]{:S(2)}) collective-permute-start(bf16[304,128]{1,0:T(8,128)(2,1)S(1)} %add_convert_fusion.2), channel_id=1, source_target_pairs={{0,12},{4,8},{8,4},{12,0},{1,13},{5,9},{9,5},{13,1},{2,14},{6,10},... | collective-permute-start | bytes 233480 | tf_op jit(solution)/shard_map/ppermute | solution.py:137
  70.4 6.8 %collective-permute-start.25 = (bf16[304,128]{1,0:T(8,128)(2,1)S(1)}, bf16[304,128]{1,0:T(8,128)(2,1)S(1)}, u32[]{:S(2)}, u32[]{:S(2)}) collective-permute-start(bf16[304,128]{1,0:T(8,128)(2,1)S(1)} %add_convert_fusion.2), channel_id=1, source_target_pairs={{0,8},{4,12},{8,0},{12,4},{1,9},{5,13},{9,1},{13,5},{2,10},{6,14},... | collective-permute-start | bytes 233480 | tf_op jit(solution)/shard_map/ppermute | solution.py:137
  70.4 6.8 %collective-permute-start.24 = (bf16[304,128]{1,0:T(8,128)(2,1)S(1)}, bf16[304,128]{1,0:T(8,128)(2,1)S(1)}, u32[]{:S(2)}, u32[]{:S(2)}) collective-permute-start(bf16[304,128]{1,0:T(8,128)(2,1)S(1)} %add_convert_fusion.2), channel_id=1, source_target_pairs={{0,4},{4,0},{8,12},{12,8},{1,5},{5,1},{9,13},{13,9},{2,6},{6,2},{1... | collective-permute-start | bytes 233480 | tf_op jit(solution)/shard_map/ppermute | solution.py:137
  75.5 6.3 %collective-permute-start.21 = (bf16[512,128]{1,0:T(8,128)(2,1)S(1)}, bf16[512,128]{1,0:T(8,128)(2,1)S(1)}, u32[]{:S(2)}, u32[]{:S(2)}) collective-permute-start(bf16[512,128]{1,0:T(8,128)(2,1)S(1)} %shard_map.226), channel_id=1, source_target_pairs={{0,1},{1,0},{2,3},{3,2},{4,5},{5,4},{6,7},{7,6},{8,9},{9,8},{10,11... | collective-permute-start | bytes 393224 | tf_op jit(solution)/shard_map/ppermute | solution.py:137
  77.2 4.5 %collective-permute-start.27 = (bf16[304,128]{1,0:T(8,128)(2,1)S(1)}, bf16[304,128]{1,0:T(8,128)(2,1)S(1)}, u32[]{:S(2)}, u32[]{:S(2)}) collective-permute-start(bf16[304,128]{1,0:T(8,128)(2,1)S(1)} %add_convert_fusion.1.refs_0_), channel_id=1, source_target_pairs={{0,2},{2,0},{1,3},{3,1},{4,6},{6,4},{5,7},{7,5},{8,10},{10,8},{9,1... | collective-permute-start | bytes 233480 | tf_op jit(solution)/shard_map/ppermute | solution.py:137
  81.7 1.4 %collective-permute-start.28 = (bf16[608,128]{1,0:T(8,128)(2,1)S(1)}, bf16[608,128]{1,0:T(8,128)(2,1)S(1)}, u32[]{:S(2)}, u32[]{:S(2)}) collective-permute-start(bf16[608,128]{1,0:T(8,128)(2,1)S(1)} %shard_map.228.own_ref), channel_id=1, source_target_pairs={{0,1},{1,0},{2,3},{3,2},{4,5},{5,4},{6,7},{7,6},{8,9},{9,8},{10,11... | collective-permute-start | bytes 466952 | tf_op jit(solution)/shard_map/ppermute | solution.py:137
  (16 other events, 47.1 us)

commit v3 on v2

--- a/solution.py
+++ b/solution.py
@@ -89,14 +89,10 @@
         self.nodes, self.send = nodes, send
         self.sub = lax.axis_size("sub")
         self.dom = lax.axis_size("dom")
-        across = range(1, self.sub)
-        self.remote = [(2, 0), (1, 0)]
-        self.remote += [(0, x) for x in across]
-        self.remote += [(2, x) for x in across] + [(1, x) for x in across]
-        self.halo = len(self.remote) * send
+        self.halo = (3 * self.sub - 1) * send
 
     def place(self, other):
-        d, t = lax.axis_index("dom"), lax.axis_index("sub")
+        d, t, core = (lax.axis_index(name) for name in AXES)
         slot = jnp.maximum(other - self.nodes, 0)
         layer = slot // (self.sub * self.send)
         rest = slot - layer * (self.sub * self.send)
@@ -105,31 +101,55 @@
         upper = (layer == 2).astype(jnp.int32)
         even = 1 - lax.rem(d, 2)
         x = peer ^ t
-        across = self.sub - 1
-        aside = jnp.where(layer == 1, 0, jnp.where(upper == even, 2, 1))
-        place = jnp.where(x > 0, 2 + aside * across + x, aside)
-        row = self.nodes + place * self.send + k
+        side = jnp.where(upper == even, 0, 1)
+        mine = side == ((core + x) & 1)
+        group = jnp.where(mine, 1 + x, 2 * self.sub + x)
+        group = jnp.where(layer == 1, jnp.where(x > 0, self.sub + x, 0), group)
+        row = self.nodes + group * self.send + k
         return jnp.where(other < self.nodes, other, row)
 
-    def exchange(self, arrays):
+    def permute(self, value, x, across):
         inner = lax.axis_size("inner")
-        out = []
-        for (a, x), value in zip(self.remote, arrays):
-            pairs = []
-            for d in range(self.dom):
-                other = d if a == 0 else (d ^ 1 if a == 1 else ((d + 1) ^ 1) - 1)
-                if not 0 <= other < self.dom:
-                    continue
-                for t in range(self.sub):
-                    for i in range(inner):
-                        pairs.append(
-                            (
-                                (d * self.sub + t) * inner + i,
-                                (other * self.sub + (t ^ x)) * inner + i,
-                            )
-                        )
-            out.append(lax.ppermute(value, AXES, pairs))
-        return out
+        pairs = []
+        for d in range(self.dom):
+            for t in range(self.sub):
+                for i in range(inner):
+                    other = d if not across else (((d + 1) ^ 1) - 1 if (i + x) & 1 else d ^ 1)
+                    if 0 <= other < self.dom:
+                        source = (d * self.sub + t) * inner + i
+                        pairs.append((source, (other * self.sub + (t ^ x)) * inner + i))
+        return lax.ppermute(value, AXES, pairs)
+
+    def fetch(self, border):
+        mine = [self.permute(border, x, True) for x in range(self.sub)]
+        own = [self.permute(border, x, False) for x in range(1, self.sub)]
+        return mine + own + [swap_axis(value, "inner", 1) for value in mine]
+
+    def give_back(self, mine, own, theirs):
+        got = swap_axis(theirs, "inner", 1)
+        send = self.send
+
+        def add_kernel(mine_ref, got_ref, *outs):
+            total = (mine_ref[...] + got_ref[...].astype(F32)).astype(BF)
+            for x, out in enumerate(outs):
+                out[...] = total[x * send : (x + 1) * send]
+
+        rows = [shape(send, mine.shape[1], BF)] * self.sub
+        sums = call(add_kernel, rows, mine, got)
+        arrived = [self.permute(value, x, True) for x, value in enumerate(sums)]
+        return arrived + [self.permute(value, x + 1, False) for x, value in enumerate(own)]
+
+    def slot_shapes(self, f):
+        block = self.sub * self.send
+        own = [shape(self.send, f, BF)] * (self.sub - 1)
+        return [shape(block, f, F32)] + own + [shape(block, f, BF)]
+
+    def store_slots(self, sums, refs):
+        block, send = self.sub * self.send, self.send
+        refs[0][...] = sums[:block]
+        for j in range(self.sub - 1):
+            refs[1 + j][...] = sums[block + j * send : block + (j + 1) * send].astype(BF)
+        refs[-1][...] = sums[self.halo - block :].astype(BF)
 
 
 def swap_axis(value, axis, mask):
@@ -137,21 +157,29 @@
     return lax.ppermute(value, axis, [(j, j ^ mask) for j in range(count)])
 
 
-def call(body, outs, *args, smem=(), scratch=(), flops=0):
-    specs = [
-        pl.BlockSpec(memory_space=pltpu.SMEM if j in smem else pltpu.VMEM)
-        for j in range(len(args))
-    ]
+def call(body, outs, *args, smem=(), hbm=(), scratch=(), flops=0, after=()):
+    first, passed = len(args), len(after)
+    specs = []
+    for j in range(first):
+        space = pltpu.SMEM if j in smem else pltpu.HBM if j in hbm else pltpu.VMEM
+        specs.append(pl.BlockSpec(memory_space=space))
+    anywhere = [pl.BlockSpec(memory_space=pl.ANY)] * passed
     size = sum(math.prod(a.shape) * a.dtype.itemsize for a in (*args, *outs))
+
+    def inner(*refs):
+        body(*refs[:first], *refs[first + passed : first + passed + len(outs)],
+             *refs[first + 2 * passed + len(outs) :])
+
     return pl.pallas_call(
-        body,
-        out_shape=outs,
-        in_specs=specs,
-        out_specs=[pl.BlockSpec(memory_space=pltpu.VMEM) for _ in outs],
+        inner,
+        out_shape=list(outs) + [jax.ShapeDtypeStruct(a.shape, a.dtype) for a in after],
+        in_specs=specs + anywhere,
+        out_specs=[pl.BlockSpec(memory_space=pltpu.VMEM) for _ in outs] + anywhere,
         scratch_shapes=list(scratch),
+        input_output_aliases={first + j: len(outs) + j for j in range(passed)},
         compiler_params=pltpu.CompilerParams(vmem_limit_bytes=VMEM_LIMIT),
         cost_estimate=pl.CostEstimate(flops=flops, bytes_accessed=size, transcendentals=0),
-    )(*args)
+    )(*args, *after)
 
 
 def shape(rows, cols, dtype):
@@ -197,7 +225,8 @@
     size = edges // blocks
     send = send_index.shape[0]
     lay = Layout(nodes, send)
-    remote = len(lay.remote)
+    remote = 3 * lay.sub - 1
+    outward = lay.sub + 1
     own = nodes + send
     half_near, half_own, half_halo = nodes // 2, own // 2, lay.halo // 2
     f = feat
@@ -207,11 +236,10 @@
     gain_n = node_gain.reshape(1, f)
 
     (border,) = call(border_kernel, [shape(send, f, BF)], sends, node_state)
-    halo = lay.exchange([border] * remote)
+    halo = lay.fetch(border)
 
     def edge_local(
-        off_ref, oth_ref, start_ref, node_ref, border_ref, edge_ref, entry_ref,
-        near_ref, far_ref, pre_ref, place_ref, spot_ref,
+        off_ref, oth_ref, start_ref, node_ref, border_ref, near_ref, far_ref, place_ref, spot_ref
     ):
         near_table = fold(node_ref[...])
         own_table = fold(jnp.concatenate([node_ref[...], border_ref[...]], axis=0))
@@ -221,36 +249,31 @@
             place = lay.place(oth_ref[rows].reshape(1, size))
             spot_ref[b : b + 1, :] = spot
             place_ref[b : b + 1, :] = place
-            near = gather_folded(spot, column(spot), near_table).astype(BF)
-            near_ref[rows, :] = near
+            near_ref[rows, :] = gather_folded(spot, column(spot), near_table).astype(BF)
             far_ref[rows, :] = gather_folded(place, column(place), own_table).astype(BF)
-            pre_ref[rows, :] = mm(edge_ref[rows, :], entry_ref[:f, :]) + mm(
-                near, entry_ref[f : 2 * f, :]
-            )
-
-    near_rows, far_own, pre_own, place, spot = call(
+
+    near_rows, far_own, place, spot = call(
         edge_local,
         [
             shape(edges, f, BF),
             shape(edges, f, BF),
-            shape(edges, f, F32),
             shape(blocks, size, jnp.int32),
             shape(blocks, size, jnp.int32),
         ],
-        edge_offset, edge_other, block_start, node_state, border, edge_state, edge_entry,
+        edge_offset, edge_other, block_start, node_state, border,
         smem=(2,),
-        flops=2 * edges * f * (nodes + own + 2 * f),
+        flops=2 * edges * f * (nodes + own),
     )
 
     def edge_forward(*refs):
-        (place_ref, count_ref, edge_ref, far_own_ref, pre_ref, entry_ref, middle_ref,
+        (place_ref, count_ref, edge_ref, far_own_ref, near_ref, entry_ref, middle_ref,
          outlet_ref, gain_ref) = refs[:9]
         halo_refs = refs[9 : 9 + remote]
         (message_ref, far_ref, h1_ref, h2_ref, s1_ref, s2_ref, out_ref) = refs[
             9 + remote : 16 + remote
         ]
-        slot_refs = refs[16 + remote : 16 + 2 * remote]
-        table, pairs = refs[16 + 2 * remote :]
+        slot_refs = refs[16 + remote : 16 + remote + outward]
+        table, pairs = refs[16 + remote + outward :]
         for j in range(remote):
             table[pl.ds(j * send, send), :] = halo_refs[j][...]
         folded = fold(table[...])
@@ -261,7 +284,8 @@
             far = gather_folded(slot, slot_col, folded)
             far = (far + far_own_ref[rows, :].astype(F32)).astype(BF)
             far_ref[rows, :] = far
-            act, slope = silu_pair(pre_ref[rows, :] + mm(far, entry_ref[2 * f :, :]))
+            inputs = jnp.concatenate([edge_ref[rows, :], near_ref[rows, :], far], axis=1)
+            act, slope = silu_pair(mm(inputs, entry_ref[...]))
             h1 = act.astype(BF)
             h1_ref[rows, :] = h1
             s1_ref[rows, :] = slope
@@ -279,23 +303,21 @@
             message_ref[rows, :] = message.astype(BF)
             pairs[rows, :] = halves(message, slot_col, half_halo)
         hot = folded_hot(whole_row(place_ref) - own, half_halo)
-        sums = unfold(mm(hot, pairs[...]).astype(BF))
-        for j in range(remote):
-            slot_refs[j][...] = sums[j * send : (j + 1) * send]
+        lay.store_slots(unfold(mm(hot, pairs[...])), slot_refs)
 
     edge_outs = call(
         edge_forward,
         [shape(edges, f, BF)] * 4
         + [shape(edges, f, F32)] * 3
-        + [shape(send, f, BF)] * remote,
-        place, edge_count, edge_state, far_own, pre_own, edge_entry, edge_middle, edge_outlet,
+        + lay.slot_shapes(f),
+        place, edge_count, edge_state, far_own, near_rows, edge_entry, edge_middle, edge_outlet,
         gain_e, *halo,
         smem=(1,),
         scratch=[pltpu.VMEM((lay.halo, f), BF), pltpu.VMEM((edges, 2 * f), BF)],
-        flops=2 * edges * f * (2 * lay.halo + 3 * f),
+        flops=2 * edges * f * (2 * lay.halo + 5 * f),
     )
     message, far_rows, h1, h2, s1, s2, out_pre = edge_outs[:7]
-    received = lay.exchange(edge_outs[7:])
+    received = lay.give_back(edge_outs[7], edge_outs[8:-1], edge_outs[-1])
 
     def local_sums(spot_ref, place_ref, send_ref, near_pairs, far_pairs):
         total = unfold(mm(folded_hot(whole_row(spot_ref), half_near), near_pairs[...]))
@@ -337,7 +359,7 @@
     def join(part, arrived):
         (out,) = call(
             join_kernel, [shape(nodes, f, BF)], sends, part, *arrived,
-            flops=2 * nodes * send * f * remote,
+            flops=2 * nodes * send * f * len(arrived),
         )
         return out, swap_axis(out, "inner", 1)
 
@@ -388,7 +410,7 @@
     )
     own_new, pulls, pull_border, direct = node_outs[:4]
     node_saved, node_gain_grad = node_outs[4:10], node_outs[10]
-    pull_halo = lay.exchange([pull_border] * remote)
+    pull_halo = lay.fetch(pull_border)
 
     def pull_local(
         spot_ref, place_ref, count_ref, pulls_ref, border_ref, cot_ref, node_ref, totals_ref,
@@ -491,19 +513,53 @@
             far_ref[rows, :] = far.astype(BF)
             pairs[rows, :] = halves(far, column(place_ref[b : b + 1, :] - own), half_halo)
         hot = folded_hot(whole_row(place_ref) - own, half_halo)
-        sums = unfold(mm(hot, pairs[...]).astype(BF))
-        for j in range(remote):
-            slot_refs[j][...] = sums[j * send : (j + 1) * send]
+        lay.store_slots(unfold(mm(hot, pairs[...])), slot_refs)
 
     far_outs = call(
         far_slots,
-        [shape(edges, f, BF)] + [shape(send, f, BF)] * remote,
+        [shape(edges, f, BF)] + lay.slot_shapes(f),
         place, first_grad, edge_entry,
         scratch=[pltpu.VMEM((edges, 2 * f), BF)],
         flops=2 * edges * f * (lay.halo + f),
     )
     far_grad = far_outs[0]
-    back_received = lay.exchange(far_outs[1:])
+    back = lay.give_back(far_outs[1], far_outs[2:-1], far_outs[-1])
+
+    def split_kernel(keep_ref, got_ref, *refs):
+        out_refs, acc = refs[:-1], refs[-1]
+        acc[...] = (keep_ref[...].astype(F32) + got_ref[...].astype(F32)).astype(BF)
+        t = lax.axis_index("sub")
+        for x in range(subs):
+            out_refs[x][...] = acc[pl.ds(pl.multiple_of((t ^ x) * piece, 16), piece), :]
+
+    split = call(
+        split_kernel,
+        [shape(piece, f, BF)] * subs,
+        keep, got,
+        scratch=[pltpu.VMEM((half, f), BF)],
+    )
+    arrived = [split[0]] + [swap_axis(split[x], "sub", x) for x in range(1, subs)]
+
+    def add_kernel(*refs):
+        values = [ref[...].astype(F32) for ref in refs[:-1]]
+        while len(values) > 1:
+            values = [values[j] + values[j + 1] for j in range(0, len(values), 2)]
+        refs[-1][...] = values[0].astype(BF)
+
+    def add_all(values, after=()):
+        out = call(add_kernel, [shape(piece, f, BF)], *values, after=after)
+        return out[0], out[1:]
+
+    total, _ = add_all(arrived)
+    stride = 1
+    while stride < doms:
+        partner = swap_axis(total, "dom", stride)
+        if stride == 1:
+            total, (far_grad,) = add_all([total, partner], [far_grad])
+        else:
+            total, _ = add_all([total, partner])
+        stride *= 2
+    own_pieces = [total] + [swap_axis(total, "sub", x) for x in range(1, subs)]
 
     def grad_sums(
         spot_ref, place_ref, send_ref, up_ref, first_ref, far_ref, entry_ref, adjoint_ref,
@@ -527,39 +583,6 @@
         flops=2 * edges * f * (nodes + own + 2 * f),
     )
 
-    def split_kernel(keep_ref, got_ref, *refs):
-        out_refs, acc = refs[:-1], refs[-1]
-        acc[...] = (keep_ref[...].astype(F32) + got_ref[...].astype(F32)).astype(BF)
-        t = lax.axis_index("sub")
-        for x in range(subs):
-            out_refs[x][...] = acc[pl.ds(pl.multiple_of((t ^ x) * piece, 16), piece), :]
-
-    pieces = call(
-        split_kernel,
-        [shape(piece, f, BF)] * subs,
-        keep, got,
-        scratch=[pltpu.VMEM((half, f), BF)],
-    )
-    arrived = [pieces[0]] + [swap_axis(pieces[x], "sub", x) for x in range(1, subs)]
-
-    def add_all(values):
-        values = [v.astype(F32) for v in values]
-        while len(values) > 1:
-            values = [values[j] + values[j + 1] for j in range(0, len(values), 2)]
-        return values[0]
-
-    total = add_all(arrived)
-    stride = 1
-    while stride < doms:
-        step = 4 if stride * 4 <= doms else 2
-        sent = total.astype(BF)
-        total = add_all(
-            [sent] + [swap_axis(sent, "dom", stride * m) for m in range(1, step)]
-        )
-        stride *= step
-    sent = total.astype(BF)
-    own_pieces = [sent] + [swap_axis(sent, "sub", x) for x in range(1, subs)]
-
     def order_kernel(*refs):
         t = lax.axis_index("sub")
         for x in range(subs):
@@ -585,8 +608,8 @@
         scratch=[pltpu.VMEM((weight_rows, f), BF)],
     )
 
-    back, back_other = join(grad_part, back_received)
-    node_adjoint = (back.astype(F32) + back_other.astype(F32) + direct).astype(BF)
+    back_part, back_other = join(grad_part, back)
+    node_adjoint = (back_part.astype(F32) + back_other.astype(F32) + direct).astype(BF)
     return (
         own_new,
         new_edges,

time: 84.4 us -> 79.3 us (0.940)
  starting transfers between devices: 46.7 us -> 39.5 us
  waiting for transfers between devices: 9.58 us -> 13.8 us
  local copies, waits for them, and re-layouts: 4.13 us -> 2.27 us
    ppermute x20 -> x12, starting transfers between devices: 40.3 us -> 28 us  [permute(): return lax.ppermute(value, AXES, pairs)]
    ppermute x9 -> x14, starting transfers between devices: 6.39 us -> 11.5 us  [swap_axis(): return lax.ppermute(value, axis, [(j, j ^ mask) for j in range(count)])]
    ppermute x20 -> x12, waiting for transfers between devices: 1.23 us -> 3.39 us  [permute(): return lax.ppermute(value, AXES, pairs)]
    ppermute x9 -> x14, waiting for transfers between devices: 8.35 us -> 10.5 us  [swap_axis(): return lax.ppermute(value, axis, [(j, j ^ mask) for j in range(count)])]
    unnamed x38 -> x34, local copies, waits for them, and re-layouts: 4.13 us -> 2.27 us
    pallas_call x14 -> x19, Pallas kernels: 21.1 us -> 20.9 us  [call(): pl.pallas_call(inner, out_shape=list(outs) + [jax.ShapeDtypeStruct(a.shap...]
  transfers between devices with their start and end apart: 29 -> 26, of which waited for: 7 -> 10; matrix products, arithmetic and copies ran while one was open for 1% -> 1% of each run, Pallas kernels for 11% -> 12%
where the time goes in v3:
time: 79.3 us; the launch traced here: 78.9 us
  starting transfers between devices  39.5 us (50%)
  Pallas kernels  20.9 us (26%)
  waiting for transfers between devices  13.8 us (17%)
  local copies, waits for them, and re-layouts  2.27 us (3%)
  between operations  1.69 us (2%)
    ppermute x12, starting transfers between devices, permute(): return lax.ppermute(value, AXES, pairs)  28 us
    pallas_call x19, Pallas kernels, call(): pl.pallas_call(inner, out_shape=list(outs) + [jax.ShapeDtypeStruct(a.shap...  20.9 us
    ppermute x14, starting transfers between devices, swap_axis(): return lax.ppermute(value, axis, [(j, j ^ mask) for j in range(count)])  11.5 us
    ppermute x14, waiting for transfers between devices, swap_axis(): return lax.ppermute(value, axis, [(j, j ^ mask) for j in range(count)])  10.5 us
    ppermute x12, waiting for transfers between devices, permute(): return lax.ppermute(value, AXES, pairs)  3.39 us
    unnamed x34, local copies, waits for them, and re-layouts  2.27 us
  transfers between devices with their start and end apart: 26, of which 10 were waited for; matrix products, arithmetic and copies ran while one was open for 1% of the time, Pallas kernels for 12%

profile of v3, /device:TPU:0, one launch (start us, length us, event | category | flops | bytes accessed | tf_op | source)
XLA Modules:
  0.0 78.9 jit_solution(3904238734719120561)
XLA Ops:
  0.6 0.7 copy-done.9
  1.3 0.9 %copy-done = bf16[512,128]{1,0:T(8,128)(2,1)S(1)} copy-done((bf16[512,128]{1,0:T(8,128)(2,1)S(1)}, bf16[512,128]{1,0:T(8,128)(2,1)}, u32[]{:S(2)}) %copy-start) | copy-done | bytes 131096
  2.5 0.7 collective-permute-start.1
  3.2 8.7 %collective-permute-start = (bf16[256,128]{1,0:T(8,128)(2,1)S(1)}, bf16[256,128]{1,0:T(8,128)(2,1)S(1)}, u32[]{:S(2)}, u32[]{:S(2)}) collective-permute-start(bf16[256,128]{1,0:T(8,128)(2,1)S(1)} %shard_map.216.refs_4_), channel_id=1, source_target_pairs={{0,4},{2,6},{4,0},{5,9},{6,2},{7,11},{8,12},{9,5},{10,14},{11,7},{... | collective-permute-start | bytes 196616 | tf_op jit(solution)/shard_map/ppermute | solution.py:121
  12.5 1.6 %collective-permute-done.refs_9_ = bf16[256,128]{1,0:T(8,128)(2,1)S(1)} collective-permute-done((bf16[256,128]{1,0:T(8,128)(2,1)S(1)}, bf16[256,128]{1,0:T(8,128)(2,1)S(1)}, u32[]{:S(2)}, u32[]{:S(2)}) %collective-permute-start) | collective-permute-done | bytes 65568 | tf_op jit(solution)/shard_map/ppermute | solution.py:121
  14.8 2.2 %shard_map.217 = (bf16[1536,128]{1,0:T(8,128)(2,1)S(1)}, bf16[1536,128]{1,0:T(8,128)(2,1)S(1)}, s32[6,256]{1,0:T(8,128)S(1)}, s32[6,256]{1,0:T(8,128)S(1)}) custom-call(s32[1536]{0:T(1024)S(1)} %copy-done.14, s32[1536]{0:T(1024)S(1)} %copy-done.15, s32[6]{0:T(128)S(1)} %copy-done.16, bf16[512,128]{1,0:T(8,128)(2,1)S(1)} %copy-done.1, ...), custom_call_target="tpu_custom_call" | custom-call | flops 503316480 | bytes 1007640 | tf_op jit(solution)/shard_map/pallas_call | solution.py:173
  17.8 4.1 %shard_map.218 = (bf16[1536,128]{1,0:T(8,128)(2,1)S(1)}, bf16[1536,128]{1,0:T(8,128)(2,1)S(1)}, bf16[1536,128]{1,0:T(8,128)(2,1)S(1)}, bf16[1536,128]{1,0:T(8,12...) custom-call(s32[6,256]{1,0:T(8,128)S(1)} %get-tuple-element.58.refs_, ...), custom_call_target="tpu_custom_call" | custom-call | flops 1258291200 | bytes 6068740 | tf_op jit(solution)/shard_map/pallas_call | solution.py:173
  23.5 3.9 %collective-permute-start.6 = (bf16[256,128]{1,0:T(8,128)(2,1)S(1)}, bf16[256,128]{1,0:T(8,128)(2,1)S(1)}, u32[]{:S(2)}, u32[]{:S(2)}) collective-permute-start(bf16[256,128]{1,0:T(8,128)(2,1)S(1)} %get-tuple-element.65), channel_id=1, source_target_pairs={{0,4},{2,6},{4,0},{5,9},{6,2},{7,11},{8,12},{9,5},{10,14},{11,7},{... | collective-permute-start | bytes 196616 | tf_op jit(solution)/shard_map/ppermute | solution.py:121
  27.4 0.7 collective-permute-start.7
  28.1 1.7 %shard_map.219 = (bf16[1536,128]{1,0:T(8,128)(2,1)}, f32[512,128]{1,0:T(8,128)S(1)}) custom-call(s32[6,256]{1,0:T(8,128)S(1)} %get-tuple-element.57.refs_0_, s32[6,256]{1,0:T(8,128)S(1)} %get-tuple-element.58.refs_0_.refs_1_, s32[1,256]{1,0:T(1,128)S(1)} %bitcast.4, s32[1]{0:T(128)S(6)} %copy.26.refs_1_.refs_3_.refs_2_, bf16[1536,128]{1,0:T(8,128)(2,1)S(1)} %copy-done.2, ...), custom_call_target="tpu_custom_call" | custom-call | flops 503316480 | bytes 1455108 | tf_op jit(solution)/shard_map/pallas_call | solution.py:173
  30.3 1.5 %collective-permute-start.9 = (bf16[512,128]{1,0:T(8,128)(2,1)S(1)}, bf16[512,128]{1,0:T(8,128)(2,1)S(1)}, u32[]{:S(2)}, u32[]{:S(2)}) collective-permute-start(bf16[512,128]{1,0:T(8,128)(2,1)S(1)} %shard_map.221.refs_0_), channel_id=1, source_target_pairs={{0,1},{1,0},{2,3},{3,2},{4,5},{5,4},{6,7},{7,6},{8,9},{9,8},{10,11... | collective-permute-start | bytes 393224 | tf_op jit(solution)/shard_map/ppermute | solution.py:157
  31.8 1.0 %collective-permute-done.9.refs_1_ = bf16[512,128]{1,0:T(8,128)(2,1)S(1)} collective-permute-done((bf16[512,128]{1,0:T(8,128)(2,1)S(1)}, bf16[512,128]{1,0:T(8,128)(2,1)S(1)}, u32[]{:S(2)}, u32[]{:S(2)}) %collective-permute-start.9) | collective-permute-done | bytes 131104 | tf_op jit(solution)/shard_map/ppermute | solution.py:157
  32.8 1.9 %shard_map.222 = (bf16[512,128]{1,0:T(8,128)(2,1)}, bf16[512,128]{1,0:T(8,128)(2,1)S(1)}, bf16[256,128]{1,0:T(8,128)(2,1)S(1)}, f32[512,128]{1,0:T(8,128)S(1)}, ...) custom-call(bf16[512,128]{1,0:T(8,128)(2,1)S(1)} %shard_map.221.refs, ...), custom_call_target="tpu_custom_call" | custom-call | flops 134217728 | bytes 2033664 | tf_op jit(solution)/shard_map/pallas_call | solution.py:173
  34.7 0.7 collective-permute-start.11
  35.3 8.3 %collective-permute-start.10 = (bf16[256,128]{1,0:T(8,128)(2,1)S(1)}, bf16[256,128]{1,0:T(8,128)(2,1)S(1)}, u32[]{:S(2)}, u32[]{:S(2)}) collective-permute-start(bf16[256,128]{1,0:T(8,128)(2,1)S(1)} %get-tuple-element.71.refs_4_), channel_id=1, source_target_pairs={{0,4},{2,6},{4,0},{5,9},{6,2},{7,11},{8,12},{9,5},{10,14},{11,7},{... | collective-permute-start | bytes 196616 | tf_op jit(solution)/shard_map/ppermute | solution.py:121
  43.7 0.7 collective-permute-start.12
  44.4 1.4 %collective-permute-done.10.refs_16_ = bf16[256,128]{1,0:T(8,128)(2,1)S(1)} collective-permute-done((bf16[256,128]{1,0:T(8,128)(2,1)S(1)}, bf16[256,128]{1,0:T(8,128)(2,1)S(1)}, u32[]{:S(2)}, u32[]{:S(2)}) %collective-permute-start.10) | collective-permute-done | bytes 65568 | tf_op jit(solution)/shard_map/ppermute | solution.py:121
  45.7 1.9 %shard_map.223 = (f32[1536,128]{1,0:T(8,128)S(1)}, bf16[512,128]{1,0:T(8,128)(2,1)S(1)}) custom-call(s32[6,256]{1,0:T(8,128)S(1)} %get-tuple-element.57.refs_0_, s32[6,256]{1,0:T(8,128)S(1)} %get-tuple-element.58.refs_0_.refs_1_, s32[1]{0:T(128)S(6)} %copy.26.refs_1_.refs_3_.refs_2_, bf16[512,128]{1,0:T(8,128)(2,1)S(1)} %get-tuple-element.70.refs_3_, ...), custom_call_target="tpu_custom_call" | custom-call | flops 570425344 | bytes 2437124 | tf_op jit(solution)/shard_map/pallas_call | solution.py:173
  48.0 4.1 %shard_map.224 = (f32[1536,128]{1,0:T(8,128)S(1)}, bf16[1536,128]{1,0:T(8,128)(2,1)S(1)}, bf16[608,128]{1,0:T(8,128)(2,1)S(1)}, bf16[608,128]{1,0:T(8,128)(2,1)S(1)}) custom-call(s32[6,256]{1,0:T(8,128)S(1)} %get-tuple-element.58.refs_0_.refs_1_, s32[1]{0:T(128)S(6)} %copy.26.refs_1_.refs_3_.refs_2_, f32[1536,128]{1,0:T(8,128)S(1)} %get-tuple-element.78.refs_2_, ...), custom_call_target="tpu_custom_call" | custom-call | flops 855638016 | bytes 7134212 | tf_op jit(solution)/shard_map/pallas_call | solution.py:173
  52.3 1.2 %collective-permute-done.15.refs_1_ = bf16[608,128]{1,0:T(8,128)(2,1)S(1)} collective-permute-done((bf16[608,128]{1,0:T(8,128)(2,1)S(1)}, bf16[608,128]{1,0:T(8,128)(2,1)S(1)}, u32[]{:S(2)}, u32[]{:S(2)}) %collective-permute-start.15) | collective-permute-done | bytes 155680 | tf_op jit(solution)/shard_map/ppermute | solution.py:157
  53.6 0.7 collective-permute-start.16
  54.3 1.0 %shard_map.227 = (bf16[1536,128]{1,0:T(8,128)(2,1)S(1)}, f32[512,128]{1,0:T(8,128)S(1)}, bf16[256,128]{1,0:T(8,128)(2,1)S(1)}, bf16[512,128]{1,0:T(8,128)(2,1)S(1)}) custom-call(s32[6,256]{1,0:T(8,128)S(1)} %get-tuple-element.58.refs_0_.refs_1_, bf16[1536,128]{1,0:T(8,128)(2,1)S(1)} %get-tuple-element.88.refs_1_.refs_4_, bf16[384,128]{1,0:T(8,128)(2,1)S(1)} %copy-done.13), custom_call_target="tpu_custom_call" | custom-call | flops 553648128 | bytes 1349632 | tf_op jit(solution)/shard_map/pallas_call | solution.py:173
  55.4 2.7 %collective-permute-done.16.refs_1_ = bf16[304,128]{1,0:T(8,128)(2,1)S(1)} collective-permute-done((bf16[304,128]{1,0:T(8,128)(2,1)S(1)}, bf16[304,128]{1,0:T(8,128)(2,1)S(1)}, u32[]{:S(2)}, u32[]{:S(2)}) %collective-permute-start.16) | collective-permute-done | bytes 77856 | tf_op jit(solution)/shard_map/ppermute | solution.py:157
  58.1 2.1 %collective-permute-start.17 = (bf16[304,128]{1,0:T(8,128)(2,1)S(1)}, bf16[304,128]{1,0:T(8,128)(2,1)S(1)}, u32[]{:S(2)}, u32[]{:S(2)}) collective-permute-start(bf16[304,128]{1,0:T(8,128)(2,1)S(1)} %shard_map.226.refs_0_), channel_id=1, source_target_pairs={{0,4},{4,0},{8,12},{12,8},{1,5},{5,1},{9,13},{13,9},{2,6},{6,2},{1... | collective-permute-start | bytes 233480 | tf_op jit(solution)/shard_map/ppermute | solution.py:157
  60.9 2.0 %collective-permute-start.19 = (bf16[256,128]{1,0:T(8,128)(2,1)S(1)}, bf16[256,128]{1,0:T(8,128)(2,1)S(1)}, u32[]{:S(2)}, u32[]{:S(2)}) collective-permute-start(bf16[256,128]{1,0:T(8,128)(2,1)S(1)} %get-tuple-element.98), channel_id=1, source_target_pairs={{0,4},{2,6},{4,0},{5,9},{6,2},{7,11},{8,12},{9,5},{10,14},{11,7},{... | collective-permute-start | bytes 196616 | tf_op jit(solution)/shard_map/ppermute | solution.py:121
  62.9 0.7 collective-permute-start.20
  63.6 5.6 %collective-permute-start.23 = (bf16[304,128]{1,0:T(8,128)(2,1)S(1)}, bf16[304,128]{1,0:T(8,128)(2,1)S(1)}, u32[]{:S(2)}, u32[]{:S(2)}) collective-permute-start(bf16[304,128]{1,0:T(8,128)(2,1)S(1)} %get-tuple-element.103.refs_0_), channel_id=1, source_target_pairs={{0,8},{4,12},{8,0},{12,4},{1,9},{5,13},{9,1},{13,5},{2,10},{6,14},... | collective-permute-start | bytes 233480 | tf_op jit(solution)/shard_map/ppermute | solution.py:157
  69.1 1.8 %shard_map.229 = (bf16[1536,128]{1,0:T(8,128)(2,1)}, f32[512,128]{1,0:T(8,128)S(1)}) custom-call(s32[6,256]{1,0:T(8,128)S(1)} %get-tuple-element.57.refs_0_, s32[6,256]{1,0:T(8,128)S(1)} %get-tuple-element.58.refs_0_.refs_1_, s32[1,256]{1,0:T(1,128)S(1)} %bitcast.7, f32[1536,128]{1,0:T(8,128)S(1)} %get-tuple-element.87.refs_3_, ...), custom_call_target="tpu_custom_call" | custom-call | flops 603979776 | bytes 2339840 | tf_op jit(solution)/shard_map/pallas_call | solution.py:173
  72.1 0.7 collective-permute-start.24
  72.8 3.8 %collective-permute-done.24.refs_1_ = bf16[304,128]{1,0:T(8,128)(2,1)S(1)} collective-permute-done((bf16[304,128]{1,0:T(8,128)(2,1)S(1)}, bf16[304,128]{1,0:T(8,128)(2,1)S(1)}, u32[]{:S(2)}, u32[]{:S(2)}) %collective-permute-start.24) | collective-permute-done | bytes 77856 | tf_op jit(solution)/shard_map/ppermute | solution.py:157
  76.7 0.7 add_convert_fusion
  78.0 0.9 %shard_map.234 = (f32[640,128]{1,0:T(8,128)}, f32[512,128]{1,0:T(8,128)}, f32[2,128]{1,0:T(2,128)}) custom-call(bf16[608,128]{1,0:T(8,128)(2,1)S(1)} %shard_map.233.refs_0_, bf16[608,128]{1,0:T(8,128)(2,1)S(1)} %collective-permute-done.25.refs_1_), custom_call_target="tpu_custom_call" | custom-call | bytes 902144 | tf_op jit(solution)/shard_map/pallas_call | solution.py:173
  (74 shorter events, 6.8 us)
Async XLA Ops:
  2.2 12.5 %copy-start.1 = (bf16[512,128]{1,0:T(8,128)(2,1)S(1)}, bf16[512,128]{1,0:T(8,128)(2,1)}, u32[]{:S(2)}) copy-start(bf16[512,128]{1,0:T(8,128)(2,1)} %refs_6_.6) | copy-start | bytes 393220
  2.2 12.6 %copy-start.14 = (s32[1536]{0:T(1024)S(1)}, s32[1536]{0:T(1024)}, u32[]{:S(2)}) copy-start(s32[1536]{0:T(1024)} %refs_0_.1) | copy-start | bytes 18436
  2.2 12.6 %copy-start.15 = (s32[1536]{0:T(1024)S(1)}, s32[1536]{0:T(1024)}, u32[]{:S(2)}) copy-start(s32[1536]{0:T(1024)} %refs_1_.5) | copy-start | bytes 18436
  2.5 12.3 %copy-start.16 = (s32[6]{0:T(128)S(1)}, s32[6]{0:T(128)}, u32[]{:S(2)}) copy-start(s32[6]{0:T(128)} %refs_2_.5) | copy-start | bytes 76
  2.5 10.0 %collective-permute-start.1 = (bf16[256,128]{1,0:T(8,128)(2,1)S(1)}, bf16[256,128]{1,0:T(8,128)(2,1)S(1)}, u32[]{:S(2)}, u32[]{:S(2)}) collective-permute-start(bf16[256,128]{1,0:T(8,128)(2,1)S(1)} %shard_map.216.refs_4_), channel_id=1, source_target_pairs={{1,7},{3,5},{4,10},{5,3},{6,8},{7,1},{8,6},{9,15},{10,4},{11,13},{... | collective-permute-start | bytes 196616 | tf_op jit(solution)/shard_map/ppermute | solution.py:121
  3.2 10.9 %collective-permute-start = (bf16[256,128]{1,0:T(8,128)(2,1)S(1)}, bf16[256,128]{1,0:T(8,128)(2,1)S(1)}, u32[]{:S(2)}, u32[]{:S(2)}) collective-permute-start(bf16[256,128]{1,0:T(8,128)(2,1)S(1)} %shard_map.216.refs_4_), channel_id=1, source_target_pairs={{0,4},{2,6},{4,0},{5,9},{6,2},{7,11},{8,12},{9,5},{10,14},{11,7},{... | collective-permute-start | bytes 196616 | tf_op jit(solution)/shard_map/ppermute | solution.py:121
  11.9 5.2 %collective-permute-start.2 = (bf16[256,128]{1,0:T(8,128)(2,1)S(1)}, bf16[256,128]{1,0:T(8,128)(2,1)S(1)}, u32[]{:S(2)}, u32[]{:S(2)}) collective-permute-start(bf16[256,128]{1,0:T(8,128)(2,1)S(1)} %shard_map.216.refs_4_), channel_id=1, source_target_pairs={{0,2},{1,3},{2,0},{3,1},{4,6},{5,7},{6,4},{7,5},{8,10},{9,11},{10,... | collective-permute-start | bytes 196616 | tf_op jit(solution)/shard_map/ppermute | solution.py:121
  12.5 4.6 %collective-permute-start.4 = (bf16[256,128]{1,0:T(8,128)(2,1)S(1)}, bf16[256,128]{1,0:T(8,128)(2,1)S(1)}, u32[]{:S(2)}, u32[]{:S(2)}) collective-permute-start(bf16[256,128]{1,0:T(8,128)(2,1)S(1)} %collective-permute-done.1.refs_10_), channel_id=1, source_target_pairs={{0,1},{1,0},{2,3},{3,2},{4,5},{5,4},{6,7},{7,6},{8,9},{9,8},{10,11... | collective-permute-start | bytes 196616 | tf_op jit(solution)/shard_map/ppermute | solution.py:157
  14.1 3.0 %collective-permute-start.3 = (bf16[256,128]{1,0:T(8,128)(2,1)S(1)}, bf16[256,128]{1,0:T(8,128)(2,1)S(1)}, u32[]{:S(2)}, u32[]{:S(2)}) collective-permute-start(bf16[256,128]{1,0:T(8,128)(2,1)S(1)} %collective-permute-done.refs_9_), channel_id=1, source_target_pairs={{0,1},{1,0},{2,3},{3,2},{4,5},{5,4},{6,7},{7,6},{8,9},{9,8},{10,11... | collective-permute-start | bytes 196616 | tf_op jit(solution)/shard_map/ppermute | solution.py:157
  21.9 1.6 %collective-permute-start.5 = (bf16[512,128]{1,0:T(8,128)(2,1)S(1)}, bf16[512,128]{1,0:T(8,128)(2,1)S(1)}, u32[]{:S(2)}, u32[]{:S(2)}) collective-permute-start(bf16[512,128]{1,0:T(8,128)(2,1)S(1)} %get-tuple-element.64), channel_id=1, source_target_pairs={{0,1},{1,0},{2,3},{3,2},{4,5},{5,4},{6,7},{7,6},{8,9},{9,8},{10,11... | collective-permute-start | bytes 393224 | tf_op jit(solution)/shard_map/ppermute | solution.py:157
  22.5 7.3 %collective-permute-start.8 = (bf16[256,128]{1,0:T(8,128)(2,1)S(1)}, bf16[256,128]{1,0:T(8,128)(2,1)S(1)}, u32[]{:S(2)}, u32[]{:S(2)}) collective-permute-start(bf16[256,128]{1,0:T(8,128)(2,1)S(1)} %get-tuple-element.67), channel_id=1, source_target_pairs={{0,2},{1,3},{2,0},{3,1},{4,6},{5,7},{6,4},{7,5},{8,10},{9,11},{10,... | collective-permute-start | bytes 196616 | tf_op jit(solution)/shard_map/ppermute | solution.py:121
  23.5 6.3 %collective-permute-start.6 = (bf16[256,128]{1,0:T(8,128)(2,1)S(1)}, bf16[256,128]{1,0:T(8,128)(2,1)S(1)}, u32[]{:S(2)}, u32[]{:S(2)}) collective-permute-start(bf16[256,128]{1,0:T(8,128)(2,1)S(1)} %get-tuple-element.65), channel_id=1, source_target_pairs={{0,4},{2,6},{4,0},{5,9},{6,2},{7,11},{8,12},{9,5},{10,14},{11,7},{... | collective-permute-start | bytes 196616 | tf_op jit(solution)/shard_map/ppermute | solution.py:121
  27.4 2.4 %collective-permute-start.7 = (bf16[256,128]{1,0:T(8,128)(2,1)S(1)}, bf16[256,128]{1,0:T(8,128)(2,1)S(1)}, u32[]{:S(2)}, u32[]{:S(2)}) collective-permute-start(bf16[256,128]{1,0:T(8,128)(2,1)S(1)} %get-tuple-element.66), channel_id=1, source_target_pairs={{1,7},{3,5},{4,10},{5,3},{6,8},{7,1},{8,6},{9,15},{10,4},{11,13},{... | collective-permute-start | bytes 196616 | tf_op jit(solution)/shard_map/ppermute | solution.py:121
  29.8 3.0 %copy-start.3 = (bf16[512,128]{1,0:T(8,128)(2,1)S(1)}, bf16[512,128]{1,0:T(8,128)(2,1)}, u32[]{:S(2)}) copy-start(bf16[512,128]{1,0:T(8,128)(2,1)} %refs_3_.4) | copy-start | bytes 393220
  30.3 15.5 %copy-start.12 = (bf16[1536,128]{1,0:T(8,128)(2,1)S(1)}, bf16[1536,128]{1,0:T(8,128)(2,1)}, u32[]{:S(2)}) copy-start(bf16[1536,128]{1,0:T(8,128)(2,1)} %refs_5_.5) | copy-start | bytes 1179652
  30.3 2.5 %collective-permute-start.9 = (bf16[512,128]{1,0:T(8,128)(2,1)S(1)}, bf16[512,128]{1,0:T(8,128)(2,1)S(1)}, u32[]{:S(2)}, u32[]{:S(2)}) collective-permute-start(bf16[512,128]{1,0:T(8,128)(2,1)S(1)} %shard_map.221.refs_0_), channel_id=1, source_target_pairs={{0,1},{1,0},{2,3},{3,2},{4,5},{5,4},{6,7},{7,6},{8,9},{9,8},{10,11... | collective-permute-start | bytes 393224 | tf_op jit(solution)/shard_map/ppermute | solution.py:157
  34.7 9.7 %collective-permute-start.11 = (bf16[256,128]{1,0:T(8,128)(2,1)S(1)}, bf16[256,128]{1,0:T(8,128)(2,1)S(1)}, u32[]{:S(2)}, u32[]{:S(2)}) collective-permute-start(bf16[256,128]{1,0:T(8,128)(2,1)S(1)} %get-tuple-element.71.refs_4_), channel_id=1, source_target_pairs={{1,7},{3,5},{4,10},{5,3},{6,8},{7,1},{8,6},{9,15},{10,4},{11,13},{... | collective-permute-start | bytes 196616 | tf_op jit(solution)/shard_map/ppermute | solution.py:121
  35.3 10.4 %collective-permute-start.10 = (bf16[256,128]{1,0:T(8,128)(2,1)S(1)}, bf16[256,128]{1,0:T(8,128)(2,1)S(1)}, u32[]{:S(2)}, u32[]{:S(2)}) collective-permute-start(bf16[256,128]{1,0:T(8,128)(2,1)S(1)} %get-tuple-element.71.refs_4_), channel_id=1, source_target_pairs={{0,4},{2,6},{4,0},{5,9},{6,2},{7,11},{8,12},{9,5},{10,14},{11,7},{... | collective-permute-start | bytes 196616 | tf_op jit(solution)/shard_map/ppermute | solution.py:121
  43.7 4.3 %collective-permute-start.12 = (bf16[256,128]{1,0:T(8,128)(2,1)S(1)}, bf16[256,128]{1,0:T(8,128)(2,1)S(1)}, u32[]{:S(2)}, u32[]{:S(2)}) collective-permute-start(bf16[256,128]{1,0:T(8,128)(2,1)S(1)} %get-tuple-element.71.refs_4_), channel_id=1, source_target_pairs={{0,2},{1,3},{2,0},{3,1},{4,6},{5,7},{6,4},{7,5},{8,10},{9,11},{10,... | collective-permute-start | bytes 196616 | tf_op jit(solution)/shard_map/ppermute | solution.py:121
  44.4 3.7 %collective-permute-start.14 = (bf16[256,128]{1,0:T(8,128)(2,1)S(1)}, bf16[256,128]{1,0:T(8,128)(2,1)S(1)}, u32[]{:S(2)}, u32[]{:S(2)}) collective-permute-start(bf16[256,128]{1,0:T(8,128)(2,1)S(1)} %collective-permute-done.11.refs_17_), channel_id=1, source_target_pairs={{0,1},{1,0},{2,3},{3,2},{4,5},{5,4},{6,7},{7,6},{8,9},{9,8},{10,11... | collective-permute-start | bytes 196616 | tf_op jit(solution)/shard_map/ppermute | solution.py:157
  45.7 2.3 %collective-permute-start.13 = (bf16[256,128]{1,0:T(8,128)(2,1)S(1)}, bf16[256,128]{1,0:T(8,128)(2,1)S(1)}, u32[]{:S(2)}, u32[]{:S(2)}) collective-permute-start(bf16[256,128]{1,0:T(8,128)(2,1)S(1)} %collective-permute-done.10.refs_16_), channel_id=1, source_target_pairs={{0,1},{1,0},{2,3},{3,2},{4,5},{5,4},{6,7},{7,6},{8,9},{9,8},{10,11... | collective-permute-start | bytes 196616 | tf_op jit(solution)/shard_map/ppermute | solution.py:157
  52.1 1.4 %collective-permute-start.15 = (bf16[608,128]{1,0:T(8,128)(2,1)S(1)}, bf16[608,128]{1,0:T(8,128)(2,1)S(1)}, u32[]{:S(2)}, u32[]{:S(2)}) collective-permute-start(bf16[608,128]{1,0:T(8,128)(2,1)S(1)} %get-tuple-element.90), channel_id=1, source_target_pairs={{0,1},{1,0},{2,3},{3,2},{4,5},{5,4},{6,7},{7,6},{8,9},{9,8},{10,11... | collective-permute-start | bytes 466952 | tf_op jit(solution)/shard_map/ppermute | solution.py:157
  53.6 4.5 %collective-permute-start.16 = (bf16[304,128]{1,0:T(8,128)(2,1)S(1)}, bf16[304,128]{1,0:T(8,128)(2,1)S(1)}, u32[]{:S(2)}, u32[]{:S(2)}) collective-permute-start(bf16[304,128]{1,0:T(8,128)(2,1)S(1)} %get-tuple-element.92), channel_id=1, source_target_pairs={{0,2},{2,0},{1,3},{3,1},{4,6},{6,4},{5,7},{7,5},{8,10},{10,8},{9,1... | collective-permute-start | bytes 233480 | tf_op jit(solution)/shard_map/ppermute | solution.py:157
  55.4 5.5 %collective-permute-start.18 = (bf16[512,128]{1,0:T(8,128)(2,1)S(1)}, bf16[512,128]{1,0:T(8,128)(2,1)S(1)}, u32[]{:S(2)}, u32[]{:S(2)}) collective-permute-start(bf16[512,128]{1,0:T(8,128)(2,1)S(1)} %get-tuple-element.97), channel_id=1, source_target_pairs={{0,1},{1,0},{2,3},{3,2},{4,5},{5,4},{6,7},{7,6},{8,9},{9,8},{10,11... | collective-permute-start | bytes 393224 | tf_op jit(solution)/shard_map/ppermute | solution.py:157
  58.1 5.4 %collective-permute-start.17 = (bf16[304,128]{1,0:T(8,128)(2,1)S(1)}, bf16[304,128]{1,0:T(8,128)(2,1)S(1)}, u32[]{:S(2)}, u32[]{:S(2)}) collective-permute-start(bf16[304,128]{1,0:T(8,128)(2,1)S(1)} %shard_map.226.refs_0_), channel_id=1, source_target_pairs={{0,4},{4,0},{8,12},{12,8},{1,5},{5,1},{9,13},{13,9},{2,6},{6,2},{1... | collective-permute-start | bytes 233480 | tf_op jit(solution)/shard_map/ppermute | solution.py:157
  60.2 10.8 %collective-permute-start.21 = (bf16[256,128]{1,0:T(8,128)(2,1)S(1)}, bf16[256,128]{1,0:T(8,128)(2,1)S(1)}, u32[]{:S(2)}, u32[]{:S(2)}) collective-permute-start(bf16[256,128]{1,0:T(8,128)(2,1)S(1)} %get-tuple-element.100), channel_id=1, source_target_pairs={{0,2},{1,3},{2,0},{3,1},{4,6},{5,7},{6,4},{7,5},{8,10},{9,11},{10,... | collective-permute-start | bytes 196616 | tf_op jit(solution)/shard_map/ppermute | solution.py:121
  60.9 10.1 %collective-permute-start.19 = (bf16[256,128]{1,0:T(8,128)(2,1)S(1)}, bf16[256,128]{1,0:T(8,128)(2,1)S(1)}, u32[]{:S(2)}, u32[]{:S(2)}) collective-permute-start(bf16[256,128]{1,0:T(8,128)(2,1)S(1)} %get-tuple-element.98), channel_id=1, source_target_pairs={{0,4},{2,6},{4,0},{5,9},{6,2},{7,11},{8,12},{9,5},{10,14},{11,7},{... | collective-permute-start | bytes 196616 | tf_op jit(solution)/shard_map/ppermute | solution.py:121
  62.9 8.1 %collective-permute-start.20 = (bf16[256,128]{1,0:T(8,128)(2,1)S(1)}, bf16[256,128]{1,0:T(8,128)(2,1)S(1)}, u32[]{:S(2)}, u32[]{:S(2)}) collective-permute-start(bf16[256,128]{1,0:T(8,128)(2,1)S(1)} %get-tuple-element.99), channel_id=1, source_target_pairs={{1,7},{3,5},{4,10},{5,3},{6,8},{7,1},{8,6},{9,15},{10,4},{11,13},{... | collective-permute-start | bytes 196616 | tf_op jit(solution)/shard_map/ppermute | solution.py:121
  63.6 8.5 %collective-permute-start.23 = (bf16[304,128]{1,0:T(8,128)(2,1)S(1)}, bf16[304,128]{1,0:T(8,128)(2,1)S(1)}, u32[]{:S(2)}, u32[]{:S(2)}) collective-permute-start(bf16[304,128]{1,0:T(8,128)(2,1)S(1)} %get-tuple-element.103.refs_0_), channel_id=1, source_target_pairs={{0,8},{4,12},{8,0},{12,4},{1,9},{5,13},{9,1},{13,5},{2,10},{6,14},... | collective-permute-start | bytes 233480 | tf_op jit(solution)/shard_map/ppermute | solution.py:157
  71.4 5.3 %collective-permute-start.22 = (bf16[512,128]{1,0:T(8,128)(2,1)S(1)}, bf16[512,128]{1,0:T(8,128)(2,1)S(1)}, u32[]{:S(2)}, u32[]{:S(2)}) collective-permute-start(bf16[512,128]{1,0:T(8,128)(2,1)S(1)} %shard_map.231), channel_id=1, source_target_pairs={{0,1},{1,0},{2,3},{3,2},{4,5},{5,4},{6,7},{7,6},{8,9},{9,8},{10,11... | collective-permute-start | bytes 393224 | tf_op jit(solution)/shard_map/ppermute | solution.py:157
  72.1 4.5 %collective-permute-start.24 = (bf16[304,128]{1,0:T(8,128)(2,1)S(1)}, bf16[304,128]{1,0:T(8,128)(2,1)S(1)}, u32[]{:S(2)}, u32[]{:S(2)}) collective-permute-start(bf16[304,128]{1,0:T(8,128)(2,1)S(1)} %shard_map.232.refs_0_), channel_id=1, source_target_pairs={{0,2},{2,0},{1,3},{3,1},{4,6},{6,4},{5,7},{7,5},{8,10},{10,8},{9,1... | collective-permute-start | bytes 233480 | tf_op jit(solution)/shard_map/ppermute | solution.py:157
  76.6 1.4 %collective-permute-start.25 = (bf16[608,128]{1,0:T(8,128)(2,1)S(1)}, bf16[608,128]{1,0:T(8,128)(2,1)S(1)}, u32[]{:S(2)}, u32[]{:S(2)}) collective-permute-start(bf16[608,128]{1,0:T(8,128)(2,1)S(1)} %shard_map.233.refs_0_), channel_id=1, source_target_pairs={{0,1},{1,0},{2,3},{3,2},{4,5},{5,4},{6,7},{7,6},{8,9},{9,8},{10,11... | collective-permute-start | bytes 466952 | tf_op jit(solution)/shard_map/ppermute | solution.py:157
  (11 other events, 23.0 us)

commit v4 on v3

--- a/solution.py
+++ b/solution.py
@@ -11,6 +11,7 @@
 BF = jnp.bfloat16
 F32 = jnp.float32
 AXES = ("dom", "sub", "inner")
+BACK_ORDER = (1, 0, 2)
 VMEM_LIMIT = 16 * 1024 * 1024
 
 
@@ -101,29 +102,36 @@
         upper = (layer == 2).astype(jnp.int32)
         even = 1 - lax.rem(d, 2)
         x = peer ^ t
-        side = jnp.where(upper == even, 0, 1)
-        mine = side == ((core + x) & 1)
-        group = jnp.where(mine, 1 + x, 2 * self.sub + x)
+        pair = x >> 1
+        near = upper == even
+        mine = near == ((x & 1) == core)
+        group = jnp.where(near, self.sub // 2 + pair, pair)
+        group += jnp.where(mine, 1, 2 * self.sub)
         group = jnp.where(layer == 1, jnp.where(x > 0, self.sub + x, 0), group)
         row = self.nodes + group * self.send + k
         return jnp.where(other < self.nodes, other, row)
 
-    def permute(self, value, x, across):
+    def permute(self, value, layer, x):
         inner = lax.axis_size("inner")
         pairs = []
         for d in range(self.dom):
+            other = (d, d ^ 1, ((d + 1) ^ 1) - 1)[layer]
+            if not 0 <= other < self.dom:
+                continue
             for t in range(self.sub):
                 for i in range(inner):
-                    other = d if not across else (((d + 1) ^ 1) - 1 if (i + x) & 1 else d ^ 1)
-                    if 0 <= other < self.dom:
-                        source = (d * self.sub + t) * inner + i
-                        pairs.append((source, (other * self.sub + (t ^ x)) * inner + i))
+                    source = (d * self.sub + t) * inner + i
+                    pairs.append((source, (other * self.sub + (t ^ x[i])) * inner + i))
         return lax.ppermute(value, AXES, pairs)
 
+    def swaps(self):
+        pairs = range(0, self.sub, 2)
+        steps = [(2, (x + 1, x)) for x in pairs] + [(1, (x, x + 1)) for x in pairs]
+        return steps + [(0, (x, x)) for x in range(1, self.sub)]
+
     def fetch(self, border):
-        mine = [self.permute(border, x, True) for x in range(self.sub)]
-        own = [self.permute(border, x, False) for x in range(1, self.sub)]
-        return mine + own + [swap_axis(value, "inner", 1) for value in mine]
+        got = [self.permute(border, layer, x) for layer, x in self.swaps()]
+        return got + [swap_axis(value, "inner", 1) for value in got[: self.sub]]
 
     def give_back(self, mine, own, theirs):
         got = swap_axis(theirs, "inner", 1)
@@ -136,8 +144,12 @@
 
         rows = [shape(send, mine.shape[1], BF)] * self.sub
         sums = call(add_kernel, rows, mine, got)
-        arrived = [self.permute(value, x, True) for x, value in enumerate(sums)]
-        return arrived + [self.permute(value, x + 1, False) for x, value in enumerate(own)]
+        arrived = {}
+        order = BACK_ORDER if self.sub == 2 else range(len(self.swaps()))
+        for j in order:
+            value = (*sums, *own)[j]
+            arrived[j] = self.permute(value, *self.swaps()[j])
+        return list(arrived.values())
 
     def slot_shapes(self, f):
         block = self.sub * self.send

time: 79.3 us -> 71.9 us (0.907)
  starting transfers between devices: 39.5 us -> 33.2 us
  waiting for transfers between devices: 13.8 us -> 12.9 us
    ppermute x12, starting transfers between devices: 28 us -> 20.6 us  [permute(): return lax.ppermute(value, AXES, pairs)]
    ppermute x12, waiting for transfers between devices: 3.39 us -> 1.71 us  [permute(): return lax.ppermute(value, AXES, pairs)]
    ppermute x14, starting transfers between devices: 11.5 us -> 12.6 us  [swap_axis(): return lax.ppermute(value, axis, [(j, j ^ mask) for j in range(count)])]
  transfers between devices with their start and end apart: 26 -> 26, of which waited for: 10 -> 11; matrix products, arithmetic and copies ran while one was open for 1% -> 1% of each run, Pallas kernels for 12% -> 13%
where the time goes in v4:
time: 71.9 us; the launch traced here: 71.7 us
  starting transfers between devices  33.2 us (46%)
  Pallas kernels  20.9 us (29%)
  waiting for transfers between devices  12.9 us (18%)
  local copies, waits for them, and re-layouts  2.26 us (3%)
  between operations  1.65 us (2%)
    pallas_call x19, Pallas kernels, call(): pl.pallas_call(inner, out_shape=list(outs) + [jax.ShapeDtypeStruct(a.shap...  20.9 us
    ppermute x12, starting transfers between devices, permute(): return lax.ppermute(value, AXES, pairs)  20.6 us
    ppermute x14, starting transfers between devices, swap_axis(): return lax.ppermute(value, axis, [(j, j ^ mask) for j in range(count)])  12.6 us
    ppermute x14, waiting for transfers between devices, swap_axis(): return lax.ppermute(value, axis, [(j, j ^ mask) for j in range(count)])  11.2 us
    unnamed x34, local copies, waits for them, and re-layouts  2.26 us
    ppermute x12, waiting for transfers between devices, permute(): return lax.ppermute(value, AXES, pairs)  1.71 us
  transfers between devices with their start and end apart: 26, of which 11 were waited for; matrix products, arithmetic and copies ran while one was open for 1% of the time, Pallas kernels for 13%

profile of v4, /device:TPU:0, one launch (start us, length us, event | category | flops | bytes accessed | tf_op | source)
XLA Modules:
  0.0 71.7 jit_solution(15647118224811763648)
XLA Ops:
  0.6 0.7 copy-done.9
  1.3 0.9 %copy-done = bf16[512,128]{1,0:T(8,128)(2,1)S(1)} copy-done((bf16[512,128]{1,0:T(8,128)(2,1)S(1)}, bf16[512,128]{1,0:T(8,128)(2,1)}, u32[]{:S(2)}) %copy-start) | copy-done | bytes 131096
  2.5 3.1 %collective-permute-start.1 = (bf16[256,128]{1,0:T(8,128)(2,1)S(1)}, bf16[256,128]{1,0:T(8,128)(2,1)S(1)}, u32[]{:S(2)}, u32[]{:S(2)}) collective-permute-start(bf16[256,128]{1,0:T(8,128)(2,1)S(1)} %shard_map.216.refs_4_), channel_id=1, source_target_pairs={{0,4},{1,7},{2,6},{3,5},{4,0},{5,3},{6,2},{7,1},{8,12},{9,15},{10,... | collective-permute-start | bytes 196616 | tf_op jit(solution)/shard_map/ppermute | solution.py:125
  5.6 0.7 collective-permute-start
  6.3 1.6 %collective-permute-start.2 = (bf16[256,128]{1,0:T(8,128)(2,1)S(1)}, bf16[256,128]{1,0:T(8,128)(2,1)S(1)}, u32[]{:S(2)}, u32[]{:S(2)}) collective-permute-start(bf16[256,128]{1,0:T(8,128)(2,1)S(1)} %shard_map.216.refs_4_), channel_id=1, source_target_pairs={{0,2},{1,3},{2,0},{3,1},{4,6},{5,7},{6,4},{7,5},{8,10},{9,11},{10,... | collective-permute-start | bytes 196616 | tf_op jit(solution)/shard_map/ppermute | solution.py:125
  9.6 2.2 %shard_map.217 = (bf16[1536,128]{1,0:T(8,128)(2,1)S(1)}, bf16[1536,128]{1,0:T(8,128)(2,1)S(1)}, s32[6,256]{1,0:T(8,128)S(1)}, s32[6,256]{1,0:T(8,128)S(1)}) custom-call(s32[1536]{0:T(1024)S(1)} %copy-done.14, s32[1536]{0:T(1024)S(1)} %copy-done.15, s32[6]{0:T(128)S(1)} %copy-done.16, bf16[512,128]{1,0:T(8,128)(2,1)S(1)} %copy-done.1, ...), custom_call_target="tpu_custom_call" | custom-call | flops 503316480 | bytes 1007640 | tf_op jit(solution)/shard_map/pallas_call | solution.py:185
  12.5 4.1 %shard_map.218 = (bf16[1536,128]{1,0:T(8,128)(2,1)S(1)}, bf16[1536,128]{1,0:T(8,128)(2,1)S(1)}, bf16[1536,128]{1,0:T(8,128)(2,1)S(1)}, bf16[1536,128]{1,0:T(8,12...) custom-call(s32[6,256]{1,0:T(8,128)S(1)} %get-tuple-element.58.refs_, ...), custom_call_target="tpu_custom_call" | custom-call | flops 1258291200 | bytes 6068740 | tf_op jit(solution)/shard_map/pallas_call | solution.py:185
  16.7 1.5 %collective-permute-start.8 = (bf16[256,128]{1,0:T(8,128)(2,1)S(1)}, bf16[256,128]{1,0:T(8,128)(2,1)S(1)}, u32[]{:S(2)}, u32[]{:S(2)}) collective-permute-start(bf16[256,128]{1,0:T(8,128)(2,1)S(1)} %get-tuple-element.67), channel_id=1, source_target_pairs={{0,2},{1,3},{2,0},{3,1},{4,6},{5,7},{6,4},{7,5},{8,10},{9,11},{10,... | collective-permute-start | bytes 196616 | tf_op jit(solution)/shard_map/ppermute | solution.py:125
  18.3 5.2 %collective-permute-start.6 = (bf16[256,128]{1,0:T(8,128)(2,1)S(1)}, bf16[256,128]{1,0:T(8,128)(2,1)S(1)}, u32[]{:S(2)}, u32[]{:S(2)}) collective-permute-start(bf16[256,128]{1,0:T(8,128)(2,1)S(1)} %get-tuple-element.65), channel_id=1, source_target_pairs={{0,4},{1,7},{2,6},{3,5},{4,0},{5,3},{6,2},{7,1},{8,12},{9,15},{10,... | collective-permute-start | bytes 196616 | tf_op jit(solution)/shard_map/ppermute | solution.py:125
  24.1 1.7 %shard_map.219 = (bf16[1536,128]{1,0:T(8,128)(2,1)}, f32[512,128]{1,0:T(8,128)S(1)}) custom-call(s32[6,256]{1,0:T(8,128)S(1)} %get-tuple-element.57.refs_0_, s32[6,256]{1,0:T(8,128)S(1)} %get-tuple-element.58.refs_0_.refs_1_, s32[1,256]{1,0:T(1,128)S(1)} %bitcast.4, s32[1]{0:T(128)S(6)} %copy.26.refs_1_.refs_3_.refs_2_, bf16[1536,128]{1,0:T(8,128)(2,1)S(1)} %copy-done.2, ...), custom_call_target="tpu_custom_call" | custom-call | flops 503316480 | bytes 1455108 | tf_op jit(solution)/shard_map/pallas_call | solution.py:185
  26.8 1.0 %collective-permute-done.9.refs_1_ = bf16[512,128]{1,0:T(8,128)(2,1)S(1)} collective-permute-done((bf16[512,128]{1,0:T(8,128)(2,1)S(1)}, bf16[512,128]{1,0:T(8,128)(2,1)S(1)}, u32[]{:S(2)}, u32[]{:S(2)}) %collective-permute-start.9) | collective-permute-done | bytes 131104 | tf_op jit(solution)/shard_map/ppermute | solution.py:169
  27.8 1.9 %shard_map.222 = (bf16[512,128]{1,0:T(8,128)(2,1)}, bf16[512,128]{1,0:T(8,128)(2,1)S(1)}, bf16[256,128]{1,0:T(8,128)(2,1)S(1)}, f32[512,128]{1,0:T(8,128)S(1)}, ...) custom-call(bf16[512,128]{1,0:T(8,128)(2,1)S(1)} %shard_map.221.refs, ...), custom_call_target="tpu_custom_call" | custom-call | flops 134217728 | bytes 2033664 | tf_op jit(solution)/shard_map/pallas_call | solution.py:185
  29.7 4.7 %collective-permute-start.11 = (bf16[256,128]{1,0:T(8,128)(2,1)S(1)}, bf16[256,128]{1,0:T(8,128)(2,1)S(1)}, u32[]{:S(2)}, u32[]{:S(2)}) collective-permute-start(bf16[256,128]{1,0:T(8,128)(2,1)S(1)} %get-tuple-element.71.refs_4_), channel_id=1, source_target_pairs={{0,4},{1,7},{2,6},{3,5},{4,0},{5,3},{6,2},{7,1},{8,12},{9,15},{10,... | collective-permute-start | bytes 196616 | tf_op jit(solution)/shard_map/ppermute | solution.py:125
  34.4 0.8 %collective-permute-start.10 = (bf16[256,128]{1,0:T(8,128)(2,1)S(1)}, bf16[256,128]{1,0:T(8,128)(2,1)S(1)}, u32[]{:S(2)}, u32[]{:S(2)}) collective-permute-start(bf16[256,128]{1,0:T(8,128)(2,1)S(1)} %get-tuple-element.71.refs_4_), channel_id=1, source_target_pairs={{4,10},{5,9},{6,8},{7,11},{8,6},{9,5},{10,4},{11,7},{20,26},{21,25... | collective-permute-start | bytes 196616 | tf_op jit(solution)/shard_map/ppermute | solution.py:125
  35.3 0.8 %collective-permute-start.12 = (bf16[256,128]{1,0:T(8,128)(2,1)S(1)}, bf16[256,128]{1,0:T(8,128)(2,1)S(1)}, u32[]{:S(2)}, u32[]{:S(2)}) collective-permute-start(bf16[256,128]{1,0:T(8,128)(2,1)S(1)} %get-tuple-element.71.refs_4_), channel_id=1, source_target_pairs={{0,2},{1,3},{2,0},{3,1},{4,6},{5,7},{6,4},{7,5},{8,10},{9,11},{10,... | collective-permute-start | bytes 196616 | tf_op jit(solution)/shard_map/ppermute | solution.py:125
  36.1 0.7 %collective-permute-done.11.refs_17_ = bf16[256,128]{1,0:T(8,128)(2,1)S(1)} collective-permute-done((bf16[256,128]{1,0:T(8,128)(2,1)S(1)}, bf16[256,128]{1,0:T(8,128)(2,1)S(1)}, u32[]{:S(2)}, u32[]{:S(2)}) %collective-permute-start.11) | collective-permute-done | bytes 65568 | tf_op jit(solution)/shard_map/ppermute | solution.py:125
  37.4 1.9 %shard_map.223 = (f32[1536,128]{1,0:T(8,128)S(1)}, bf16[512,128]{1,0:T(8,128)(2,1)S(1)}) custom-call(s32[6,256]{1,0:T(8,128)S(1)} %get-tuple-element.57.refs_0_, s32[6,256]{1,0:T(8,128)S(1)} %get-tuple-element.58.refs_0_.refs_1_, s32[1]{0:T(128)S(6)} %copy.26.refs_1_.refs_3_.refs_2_, bf16[512,128]{1,0:T(8,128)(2,1)S(1)} %get-tuple-element.70.refs_3_, ...), custom_call_target="tpu_custom_call" | custom-call | flops 570425344 | bytes 2437124 | tf_op jit(solution)/shard_map/pallas_call | solution.py:185
  39.6 4.1 %shard_map.224 = (f32[1536,128]{1,0:T(8,128)S(1)}, bf16[1536,128]{1,0:T(8,128)(2,1)S(1)}, bf16[608,128]{1,0:T(8,128)(2,1)S(1)}, bf16[608,128]{1,0:T(8,128)(2,1)S(1)}) custom-call(s32[6,256]{1,0:T(8,128)S(1)} %get-tuple-element.58.refs_0_.refs_1_, s32[1]{0:T(128)S(6)} %copy.26.refs_1_.refs_3_.refs_2_, f32[1536,128]{1,0:T(8,128)S(1)} %get-tuple-element.78.refs_2_, ...), custom_call_target="tpu_custom_call" | custom-call | flops 855638016 | bytes 7134212 | tf_op jit(solution)/shard_map/pallas_call | solution.py:185
  43.8 1.4 %collective-permute-done.15.refs_1_ = bf16[608,128]{1,0:T(8,128)(2,1)S(1)} collective-permute-done((bf16[608,128]{1,0:T(8,128)(2,1)S(1)}, bf16[608,128]{1,0:T(8,128)(2,1)S(1)}, u32[]{:S(2)}, u32[]{:S(2)}) %collective-permute-start.15) | collective-permute-done | bytes 155680 | tf_op jit(solution)/shard_map/ppermute | solution.py:169
  45.2 1.1 %collective-permute-start.16 = (bf16[304,128]{1,0:T(8,128)(2,1)S(1)}, bf16[304,128]{1,0:T(8,128)(2,1)S(1)}, u32[]{:S(2)}, u32[]{:S(2)}) collective-permute-start(bf16[304,128]{1,0:T(8,128)(2,1)S(1)} %get-tuple-element.92), channel_id=1, source_target_pairs={{0,2},{2,0},{1,3},{3,1},{4,6},{6,4},{5,7},{7,5},{8,10},{10,8},{9,1... | collective-permute-start | bytes 233480 | tf_op jit(solution)/shard_map/ppermute | solution.py:169
  46.4 1.0 %shard_map.227 = (bf16[1536,128]{1,0:T(8,128)(2,1)S(1)}, f32[512,128]{1,0:T(8,128)S(1)}, bf16[256,128]{1,0:T(8,128)(2,1)S(1)}, bf16[512,128]{1,0:T(8,128)(2,1)S(1)}) custom-call(s32[6,256]{1,0:T(8,128)S(1)} %get-tuple-element.58.refs_0_.refs_1_, bf16[1536,128]{1,0:T(8,128)(2,1)S(1)} %get-tuple-element.88.refs_1_.refs_4_, bf16[384,128]{1,0:T(8,128)(2,1)S(1)} %copy-done.13), custom_call_target="tpu_custom_call" | custom-call | flops 553648128 | bytes 1349632 | tf_op jit(solution)/shard_map/pallas_call | solution.py:185
  47.5 2.2 %collective-permute-done.16.refs_1_ = bf16[304,128]{1,0:T(8,128)(2,1)S(1)} collective-permute-done((bf16[304,128]{1,0:T(8,128)(2,1)S(1)}, bf16[304,128]{1,0:T(8,128)(2,1)S(1)}, u32[]{:S(2)}, u32[]{:S(2)}) %collective-permute-start.16) | collective-permute-done | bytes 77856 | tf_op jit(solution)/shard_map/ppermute | solution.py:169
  49.7 4.3 %collective-permute-start.17 = (bf16[304,128]{1,0:T(8,128)(2,1)S(1)}, bf16[304,128]{1,0:T(8,128)(2,1)S(1)}, u32[]{:S(2)}, u32[]{:S(2)}) collective-permute-start(bf16[304,128]{1,0:T(8,128)(2,1)S(1)} %shard_map.226.refs_0_), channel_id=1, source_target_pairs={{0,4},{4,0},{8,12},{12,8},{1,5},{5,1},{9,13},{13,9},{2,6},{6,2},{1... | collective-permute-start | bytes 233480 | tf_op jit(solution)/shard_map/ppermute | solution.py:169
  54.0 0.8 %collective-permute-start.21 = (bf16[256,128]{1,0:T(8,128)(2,1)S(1)}, bf16[256,128]{1,0:T(8,128)(2,1)S(1)}, u32[]{:S(2)}, u32[]{:S(2)}) collective-permute-start(bf16[256,128]{1,0:T(8,128)(2,1)S(1)} %get-tuple-element.100), channel_id=1, source_target_pairs={{0,2},{1,3},{2,0},{3,1},{4,6},{5,7},{6,4},{7,5},{8,10},{9,11},{10,... | collective-permute-start | bytes 196616 | tf_op jit(solution)/shard_map/ppermute | solution.py:125
  55.6 0.9 %collective-permute-done.17.refs_1_ = bf16[304,128]{1,0:T(8,128)(2,1)S(1)} collective-permute-done((bf16[304,128]{1,0:T(8,128)(2,1)S(1)}, bf16[304,128]{1,0:T(8,128)(2,1)S(1)}, u32[]{:S(2)}, u32[]{:S(2)}) %collective-permute-start.17) | collective-permute-done | bytes 77856 | tf_op jit(solution)/shard_map/ppermute | solution.py:169
  56.6 4.5 %collective-permute-start.23 = (bf16[304,128]{1,0:T(8,128)(2,1)S(1)}, bf16[304,128]{1,0:T(8,128)(2,1)S(1)}, u32[]{:S(2)}, u32[]{:S(2)}) collective-permute-start(bf16[304,128]{1,0:T(8,128)(2,1)S(1)} %get-tuple-element.103.refs_0_), channel_id=1, source_target_pairs={{0,8},{4,12},{8,0},{12,4},{1,9},{5,13},{9,1},{13,5},{2,10},{6,14},... | collective-permute-start | bytes 233480 | tf_op jit(solution)/shard_map/ppermute | solution.py:169
  61.1 1.8 %shard_map.229 = (bf16[1536,128]{1,0:T(8,128)(2,1)}, f32[512,128]{1,0:T(8,128)S(1)}) custom-call(s32[6,256]{1,0:T(8,128)S(1)} %get-tuple-element.57.refs_0_, s32[6,256]{1,0:T(8,128)S(1)} %get-tuple-element.58.refs_0_.refs_1_, s32[1,256]{1,0:T(1,128)S(1)} %bitcast.7, f32[1536,128]{1,0:T(8,128)S(1)} %get-tuple-element.87.refs_3_, ...), custom_call_target="tpu_custom_call" | custom-call | flops 603979776 | bytes 2339840 | tf_op jit(solution)/shard_map/pallas_call | solution.py:185
  63.4 1.5 %collective-permute-done.23.refs_1_ = bf16[304,128]{1,0:T(8,128)(2,1)S(1)} collective-permute-done((bf16[304,128]{1,0:T(8,128)(2,1)S(1)}, bf16[304,128]{1,0:T(8,128)(2,1)S(1)}, u32[]{:S(2)}, u32[]{:S(2)}) %collective-permute-start.23) | collective-permute-done | bytes 77856 | tf_op jit(solution)/shard_map/ppermute | solution.py:169
  64.9 0.9 %collective-permute-start.24 = (bf16[304,128]{1,0:T(8,128)(2,1)S(1)}, bf16[304,128]{1,0:T(8,128)(2,1)S(1)}, u32[]{:S(2)}, u32[]{:S(2)}) collective-permute-start(bf16[304,128]{1,0:T(8,128)(2,1)S(1)} %shard_map.232.refs_0_), channel_id=1, source_target_pairs={{0,2},{2,0},{1,3},{3,1},{4,6},{6,4},{5,7},{7,5},{8,10},{10,8},{9,1... | collective-permute-start | bytes 233480 | tf_op jit(solution)/shard_map/ppermute | solution.py:169
  65.7 3.6 %collective-permute-done.24.refs_1_ = bf16[304,128]{1,0:T(8,128)(2,1)S(1)} collective-permute-done((bf16[304,128]{1,0:T(8,128)(2,1)S(1)}, bf16[304,128]{1,0:T(8,128)(2,1)S(1)}, u32[]{:S(2)}, u32[]{:S(2)}) %collective-permute-start.24) | collective-permute-done | bytes 77856 | tf_op jit(solution)/shard_map/ppermute | solution.py:169
  69.4 0.7 add_convert_fusion
  70.8 0.9 %shard_map.234 = (f32[640,128]{1,0:T(8,128)}, f32[512,128]{1,0:T(8,128)}, f32[2,128]{1,0:T(2,128)}) custom-call(bf16[608,128]{1,0:T(8,128)(2,1)S(1)} %shard_map.233.refs_0_, bf16[608,128]{1,0:T(8,128)(2,1)S(1)} %collective-permute-done.25.refs_1_), custom_call_target="tpu_custom_call" | custom-call | bytes 902144 | tf_op jit(solution)/shard_map/pallas_call | solution.py:185
  (74 shorter events, 6.9 us)
Async XLA Ops:
  2.2 7.3 %copy-start.1 = (bf16[512,128]{1,0:T(8,128)(2,1)S(1)}, bf16[512,128]{1,0:T(8,128)(2,1)}, u32[]{:S(2)}) copy-start(bf16[512,128]{1,0:T(8,128)(2,1)} %refs_6_.6) | copy-start | bytes 393220
  2.2 7.3 %copy-start.14 = (s32[1536]{0:T(1024)S(1)}, s32[1536]{0:T(1024)}, u32[]{:S(2)}) copy-start(s32[1536]{0:T(1024)} %refs_0_.1) | copy-start | bytes 18436
  2.2 7.3 %copy-start.15 = (s32[1536]{0:T(1024)S(1)}, s32[1536]{0:T(1024)}, u32[]{:S(2)}) copy-start(s32[1536]{0:T(1024)} %refs_1_.5) | copy-start | bytes 18436
  2.5 7.0 %copy-start.16 = (s32[6]{0:T(128)S(1)}, s32[6]{0:T(128)}, u32[]{:S(2)}) copy-start(s32[6]{0:T(128)} %refs_2_.5) | copy-start | bytes 76
  2.5 5.8 %collective-permute-start.1 = (bf16[256,128]{1,0:T(8,128)(2,1)S(1)}, bf16[256,128]{1,0:T(8,128)(2,1)S(1)}, u32[]{:S(2)}, u32[]{:S(2)}) collective-permute-start(bf16[256,128]{1,0:T(8,128)(2,1)S(1)} %shard_map.216.refs_4_), channel_id=1, source_target_pairs={{0,4},{1,7},{2,6},{3,5},{4,0},{5,3},{6,2},{7,1},{8,12},{9,15},{10,... | collective-permute-start | bytes 196616 | tf_op jit(solution)/shard_map/ppermute | solution.py:125
  5.6 2.7 %collective-permute-start = (bf16[256,128]{1,0:T(8,128)(2,1)S(1)}, bf16[256,128]{1,0:T(8,128)(2,1)S(1)}, u32[]{:S(2)}, u32[]{:S(2)}) collective-permute-start(bf16[256,128]{1,0:T(8,128)(2,1)S(1)} %shard_map.216.refs_4_), channel_id=1, source_target_pairs={{4,10},{5,9},{6,8},{7,11},{8,6},{9,5},{10,4},{11,7},{20,26},{21,25... | collective-permute-start | bytes 196616 | tf_op jit(solution)/shard_map/ppermute | solution.py:125
  6.3 5.6 %collective-permute-start.2 = (bf16[256,128]{1,0:T(8,128)(2,1)S(1)}, bf16[256,128]{1,0:T(8,128)(2,1)S(1)}, u32[]{:S(2)}, u32[]{:S(2)}) collective-permute-start(bf16[256,128]{1,0:T(8,128)(2,1)S(1)} %shard_map.216.refs_4_), channel_id=1, source_target_pairs={{0,2},{1,3},{2,0},{3,1},{4,6},{5,7},{6,4},{7,5},{8,10},{9,11},{10,... | collective-permute-start | bytes 196616 | tf_op jit(solution)/shard_map/ppermute | solution.py:125
  8.3 3.5 %collective-permute-start.4 = (bf16[256,128]{1,0:T(8,128)(2,1)S(1)}, bf16[256,128]{1,0:T(8,128)(2,1)S(1)}, u32[]{:S(2)}, u32[]{:S(2)}) collective-permute-start(bf16[256,128]{1,0:T(8,128)(2,1)S(1)} %collective-permute-done.1.refs_10_), channel_id=1, source_target_pairs={{0,1},{1,0},{2,3},{3,2},{4,5},{5,4},{6,7},{7,6},{8,9},{9,8},{10,11... | collective-permute-start | bytes 196616 | tf_op jit(solution)/shard_map/ppermute | solution.py:169
  8.3 3.5 %collective-permute-start.3 = (bf16[256,128]{1,0:T(8,128)(2,1)S(1)}, bf16[256,128]{1,0:T(8,128)(2,1)S(1)}, u32[]{:S(2)}, u32[]{:S(2)}) collective-permute-start(bf16[256,128]{1,0:T(8,128)(2,1)S(1)} %collective-permute-done.refs_9_), channel_id=1, source_target_pairs={{0,1},{1,0},{2,3},{3,2},{4,5},{5,4},{6,7},{7,6},{8,9},{9,8},{10,11... | collective-permute-start | bytes 196616 | tf_op jit(solution)/shard_map/ppermute | solution.py:169
  9.5 2.3 %copy-start.2 = (bf16[1536,128]{1,0:T(8,128)(2,1)S(1)}, bf16[1536,128]{1,0:T(8,128)(2,1)}, u32[]{:S(2)}) copy-start(bf16[1536,128]{1,0:T(8,128)(2,1)} %refs_8_.1) | copy-start | bytes 1179652
  16.6 1.6 %collective-permute-start.5 = (bf16[512,128]{1,0:T(8,128)(2,1)S(1)}, bf16[512,128]{1,0:T(8,128)(2,1)S(1)}, u32[]{:S(2)}, u32[]{:S(2)}) collective-permute-start(bf16[512,128]{1,0:T(8,128)(2,1)S(1)} %get-tuple-element.64), channel_id=1, source_target_pairs={{0,1},{1,0},{2,3},{3,2},{4,5},{5,4},{6,7},{7,6},{8,9},{9,8},{10,11... | collective-permute-start | bytes 393224 | tf_op jit(solution)/shard_map/ppermute | solution.py:169
  16.7 9.1 %collective-permute-start.8 = (bf16[256,128]{1,0:T(8,128)(2,1)S(1)}, bf16[256,128]{1,0:T(8,128)(2,1)S(1)}, u32[]{:S(2)}, u32[]{:S(2)}) collective-permute-start(bf16[256,128]{1,0:T(8,128)(2,1)S(1)} %get-tuple-element.67), channel_id=1, source_target_pairs={{0,2},{1,3},{2,0},{3,1},{4,6},{5,7},{6,4},{7,5},{8,10},{9,11},{10,... | collective-permute-start | bytes 196616 | tf_op jit(solution)/shard_map/ppermute | solution.py:125
  18.3 7.6 %collective-permute-start.6 = (bf16[256,128]{1,0:T(8,128)(2,1)S(1)}, bf16[256,128]{1,0:T(8,128)(2,1)S(1)}, u32[]{:S(2)}, u32[]{:S(2)}) collective-permute-start(bf16[256,128]{1,0:T(8,128)(2,1)S(1)} %get-tuple-element.65), channel_id=1, source_target_pairs={{0,4},{1,7},{2,6},{3,5},{4,0},{5,3},{6,2},{7,1},{8,12},{9,15},{10,... | collective-permute-start | bytes 196616 | tf_op jit(solution)/shard_map/ppermute | solution.py:125
  23.4 2.5 %collective-permute-start.7 = (bf16[256,128]{1,0:T(8,128)(2,1)S(1)}, bf16[256,128]{1,0:T(8,128)(2,1)S(1)}, u32[]{:S(2)}, u32[]{:S(2)}) collective-permute-start(bf16[256,128]{1,0:T(8,128)(2,1)S(1)} %get-tuple-element.66), channel_id=1, source_target_pairs={{4,10},{5,9},{6,8},{7,11},{8,6},{9,5},{10,4},{11,7},{20,26},{21,25... | collective-permute-start | bytes 196616 | tf_op jit(solution)/shard_map/ppermute | solution.py:125
  26.3 11.0 %copy-start.12 = (bf16[1536,128]{1,0:T(8,128)(2,1)S(1)}, bf16[1536,128]{1,0:T(8,128)(2,1)}, u32[]{:S(2)}) copy-start(bf16[1536,128]{1,0:T(8,128)(2,1)} %refs_5_.5) | copy-start | bytes 1179652
  26.3 1.5 %collective-permute-start.9 = (bf16[512,128]{1,0:T(8,128)(2,1)S(1)}, bf16[512,128]{1,0:T(8,128)(2,1)S(1)}, u32[]{:S(2)}, u32[]{:S(2)}) collective-permute-start(bf16[512,128]{1,0:T(8,128)(2,1)S(1)} %shard_map.221.refs_0_), channel_id=1, source_target_pairs={{0,1},{1,0},{2,3},{3,2},{4,5},{5,4},{6,7},{7,6},{8,9},{9,8},{10,11... | collective-permute-start | bytes 393224 | tf_op jit(solution)/shard_map/ppermute | solution.py:169
  29.7 7.1 %collective-permute-start.11 = (bf16[256,128]{1,0:T(8,128)(2,1)S(1)}, bf16[256,128]{1,0:T(8,128)(2,1)S(1)}, u32[]{:S(2)}, u32[]{:S(2)}) collective-permute-start(bf16[256,128]{1,0:T(8,128)(2,1)S(1)} %get-tuple-element.71.refs_4_), channel_id=1, source_target_pairs={{0,4},{1,7},{2,6},{3,5},{4,0},{5,3},{6,2},{7,1},{8,12},{9,15},{10,... | collective-permute-start | bytes 196616 | tf_op jit(solution)/shard_map/ppermute | solution.py:125
  34.4 2.4 %collective-permute-start.10 = (bf16[256,128]{1,0:T(8,128)(2,1)S(1)}, bf16[256,128]{1,0:T(8,128)(2,1)S(1)}, u32[]{:S(2)}, u32[]{:S(2)}) collective-permute-start(bf16[256,128]{1,0:T(8,128)(2,1)S(1)} %get-tuple-element.71.refs_4_), channel_id=1, source_target_pairs={{4,10},{5,9},{6,8},{7,11},{8,6},{9,5},{10,4},{11,7},{20,26},{21,25... | collective-permute-start | bytes 196616 | tf_op jit(solution)/shard_map/ppermute | solution.py:125
  35.3 4.3 %collective-permute-start.12 = (bf16[256,128]{1,0:T(8,128)(2,1)S(1)}, bf16[256,128]{1,0:T(8,128)(2,1)S(1)}, u32[]{:S(2)}, u32[]{:S(2)}) collective-permute-start(bf16[256,128]{1,0:T(8,128)(2,1)S(1)} %get-tuple-element.71.refs_4_), channel_id=1, source_target_pairs={{0,2},{1,3},{2,0},{3,1},{4,6},{5,7},{6,4},{7,5},{8,10},{9,11},{10,... | collective-permute-start | bytes 196616 | tf_op jit(solution)/shard_map/ppermute | solution.py:125
  36.8 2.8 %collective-permute-start.14 = (bf16[256,128]{1,0:T(8,128)(2,1)S(1)}, bf16[256,128]{1,0:T(8,128)(2,1)S(1)}, u32[]{:S(2)}, u32[]{:S(2)}) collective-permute-start(bf16[256,128]{1,0:T(8,128)(2,1)S(1)} %collective-permute-done.11.refs_17_), channel_id=1, source_target_pairs={{0,1},{1,0},{2,3},{3,2},{4,5},{5,4},{6,7},{7,6},{8,9},{9,8},{10,11... | collective-permute-start | bytes 196616 | tf_op jit(solution)/shard_map/ppermute | solution.py:169
  36.8 2.8 %collective-permute-start.13 = (bf16[256,128]{1,0:T(8,128)(2,1)S(1)}, bf16[256,128]{1,0:T(8,128)(2,1)S(1)}, u32[]{:S(2)}, u32[]{:S(2)}) collective-permute-start(bf16[256,128]{1,0:T(8,128)(2,1)S(1)} %collective-permute-done.10.refs_16_), channel_id=1, source_target_pairs={{0,1},{1,0},{2,3},{3,2},{4,5},{5,4},{6,7},{7,6},{8,9},{9,8},{10,11... | collective-permute-start | bytes 196616 | tf_op jit(solution)/shard_map/ppermute | solution.py:169
  43.7 1.4 %collective-permute-start.15 = (bf16[608,128]{1,0:T(8,128)(2,1)S(1)}, bf16[608,128]{1,0:T(8,128)(2,1)S(1)}, u32[]{:S(2)}, u32[]{:S(2)}) collective-permute-start(bf16[608,128]{1,0:T(8,128)(2,1)S(1)} %get-tuple-element.90), channel_id=1, source_target_pairs={{0,1},{1,0},{2,3},{3,2},{4,5},{5,4},{6,7},{7,6},{8,9},{9,8},{10,11... | collective-permute-start | bytes 466952 | tf_op jit(solution)/shard_map/ppermute | solution.py:169
  45.2 4.5 %collective-permute-start.16 = (bf16[304,128]{1,0:T(8,128)(2,1)S(1)}, bf16[304,128]{1,0:T(8,128)(2,1)S(1)}, u32[]{:S(2)}, u32[]{:S(2)}) collective-permute-start(bf16[304,128]{1,0:T(8,128)(2,1)S(1)} %get-tuple-element.92), channel_id=1, source_target_pairs={{0,2},{2,0},{1,3},{3,1},{4,6},{6,4},{5,7},{7,5},{8,10},{10,8},{9,1... | collective-permute-start | bytes 233480 | tf_op jit(solution)/shard_map/ppermute | solution.py:169
  47.4 7.4 %collective-permute-start.18 = (bf16[512,128]{1,0:T(8,128)(2,1)S(1)}, bf16[512,128]{1,0:T(8,128)(2,1)S(1)}, u32[]{:S(2)}, u32[]{:S(2)}) collective-permute-start(bf16[512,128]{1,0:T(8,128)(2,1)S(1)} %get-tuple-element.97), channel_id=1, source_target_pairs={{0,1},{1,0},{2,3},{3,2},{4,5},{5,4},{6,7},{7,6},{8,9},{9,8},{10,11... | collective-permute-start | bytes 393224 | tf_op jit(solution)/shard_map/ppermute | solution.py:169
  49.7 6.8 %collective-permute-start.17 = (bf16[304,128]{1,0:T(8,128)(2,1)S(1)}, bf16[304,128]{1,0:T(8,128)(2,1)S(1)}, u32[]{:S(2)}, u32[]{:S(2)}) collective-permute-start(bf16[304,128]{1,0:T(8,128)(2,1)S(1)} %shard_map.226.refs_0_), channel_id=1, source_target_pairs={{0,4},{4,0},{8,12},{12,8},{1,5},{5,1},{9,13},{13,9},{2,6},{6,2},{1... | collective-permute-start | bytes 233480 | tf_op jit(solution)/shard_map/ppermute | solution.py:169
  54.0 8.9 %collective-permute-start.21 = (bf16[256,128]{1,0:T(8,128)(2,1)S(1)}, bf16[256,128]{1,0:T(8,128)(2,1)S(1)}, u32[]{:S(2)}, u32[]{:S(2)}) collective-permute-start(bf16[256,128]{1,0:T(8,128)(2,1)S(1)} %get-tuple-element.100), channel_id=1, source_target_pairs={{0,2},{1,3},{2,0},{3,1},{4,6},{5,7},{6,4},{7,5},{8,10},{9,11},{10,... | collective-permute-start | bytes 196616 | tf_op jit(solution)/shard_map/ppermute | solution.py:125
  54.8 8.1 %collective-permute-start.19 = (bf16[256,128]{1,0:T(8,128)(2,1)S(1)}, bf16[256,128]{1,0:T(8,128)(2,1)S(1)}, u32[]{:S(2)}, u32[]{:S(2)}) collective-permute-start(bf16[256,128]{1,0:T(8,128)(2,1)S(1)} %get-tuple-element.98), channel_id=1, source_target_pairs={{0,4},{1,7},{2,6},{3,5},{4,0},{5,3},{6,2},{7,1},{8,12},{9,15},{10,... | collective-permute-start | bytes 196616 | tf_op jit(solution)/shard_map/ppermute | solution.py:125
  55.0 7.9 %collective-permute-start.20 = (bf16[256,128]{1,0:T(8,128)(2,1)S(1)}, bf16[256,128]{1,0:T(8,128)(2,1)S(1)}, u32[]{:S(2)}, u32[]{:S(2)}) collective-permute-start(bf16[256,128]{1,0:T(8,128)(2,1)S(1)} %get-tuple-element.99), channel_id=1, source_target_pairs={{4,10},{5,9},{6,8},{7,11},{8,6},{9,5},{10,4},{11,7},{20,26},{21,25... | collective-permute-start | bytes 196616 | tf_op jit(solution)/shard_map/ppermute | solution.py:125
  56.6 8.3 %collective-permute-start.23 = (bf16[304,128]{1,0:T(8,128)(2,1)S(1)}, bf16[304,128]{1,0:T(8,128)(2,1)S(1)}, u32[]{:S(2)}, u32[]{:S(2)}) collective-permute-start(bf16[304,128]{1,0:T(8,128)(2,1)S(1)} %get-tuple-element.103.refs_0_), channel_id=1, source_target_pairs={{0,8},{4,12},{8,0},{12,4},{1,9},{5,13},{9,1},{13,5},{2,10},{6,14},... | collective-permute-start | bytes 233480 | tf_op jit(solution)/shard_map/ppermute | solution.py:169
  63.3 6.1 %collective-permute-start.22 = (bf16[512,128]{1,0:T(8,128)(2,1)S(1)}, bf16[512,128]{1,0:T(8,128)(2,1)S(1)}, u32[]{:S(2)}, u32[]{:S(2)}) collective-permute-start(bf16[512,128]{1,0:T(8,128)(2,1)S(1)} %shard_map.231), channel_id=1, source_target_pairs={{0,1},{1,0},{2,3},{3,2},{4,5},{5,4},{6,7},{7,6},{8,9},{9,8},{10,11... | collective-permute-start | bytes 393224 | tf_op jit(solution)/shard_map/ppermute | solution.py:169
  64.9 4.5 %collective-permute-start.24 = (bf16[304,128]{1,0:T(8,128)(2,1)S(1)}, bf16[304,128]{1,0:T(8,128)(2,1)S(1)}, u32[]{:S(2)}, u32[]{:S(2)}) collective-permute-start(bf16[304,128]{1,0:T(8,128)(2,1)S(1)} %shard_map.232.refs_0_), channel_id=1, source_target_pairs={{0,2},{2,0},{1,3},{3,1},{4,6},{6,4},{5,7},{7,5},{8,10},{10,8},{9,1... | collective-permute-start | bytes 233480 | tf_op jit(solution)/shard_map/ppermute | solution.py:169
  69.3 1.4 %collective-permute-start.25 = (bf16[608,128]{1,0:T(8,128)(2,1)S(1)}, bf16[608,128]{1,0:T(8,128)(2,1)S(1)}, u32[]{:S(2)}, u32[]{:S(2)}) collective-permute-start(bf16[608,128]{1,0:T(8,128)(2,1)S(1)} %shard_map.233.refs_0_), channel_id=1, source_target_pairs={{0,1},{1,0},{2,3},{3,2},{4,5},{5,4},{6,7},{7,6},{8,9},{9,8},{10,11... | collective-permute-start | bytes 466952 | tf_op jit(solution)/shard_map/ppermute | solution.py:169
  (11 other events, 18.3 us)

commit v5 on v4

--- a/solution.py
+++ b/solution.py
@@ -130,8 +130,10 @@
         return steps + [(0, (x, x)) for x in range(1, self.sub)]
 
     def fetch(self, border):
-        got = [self.permute(border, layer, x) for layer, x in self.swaps()]
-        return got + [swap_axis(value, "inner", 1) for value in got[: self.sub]]
+        return [self.permute(border, layer, x) for layer, x in self.swaps()]
+
+    def fetch_theirs(self, got):
+        return [swap_axis(value, "inner", 1) for value in got[: self.sub]]
 
     def give_back(self, mine, own, theirs):
         got = swap_axis(theirs, "inner", 1)
@@ -250,31 +252,45 @@
     (border,) = call(border_kernel, [shape(send, f, BF)], sends, node_state)
     halo = lay.fetch(border)
 
-    def edge_local(
-        off_ref, oth_ref, start_ref, node_ref, border_ref, near_ref, far_ref, place_ref, spot_ref
+    def edge_near(
+        off_ref, oth_ref, start_ref, node_ref, gain_ref, near_ref, place_ref, spot_ref,
+        gain_out_ref,
     ):
-        near_table = fold(node_ref[...])
-        own_table = fold(jnp.concatenate([node_ref[...], border_ref[...]], axis=0))
+        gain_out_ref[...] = gain_ref[...]
+        table = fold(node_ref[...])
         for b in range(blocks):
             rows = pl.ds(b * size, size)
             spot = off_ref[rows].reshape(1, size) + start_ref[b]
-            place = lay.place(oth_ref[rows].reshape(1, size))
             spot_ref[b : b + 1, :] = spot
-            place_ref[b : b + 1, :] = place
-            near_ref[rows, :] = gather_folded(spot, column(spot), near_table).astype(BF)
-            far_ref[rows, :] = gather_folded(place, column(place), own_table).astype(BF)
-
-    near_rows, far_own, place, spot = call(
-        edge_local,
+            place_ref[b : b + 1, :] = lay.place(oth_ref[rows].reshape(1, size))
+            near_ref[rows, :] = gather_folded(spot, column(spot), table).astype(BF)
+
+    near_rows, place, spot, gain_e = call(
+        edge_near,
         [
-            shape(edges, f, BF),
             shape(edges, f, BF),
             shape(blocks, size, jnp.int32),
             shape(blocks, size, jnp.int32),
+            shape(1, f, F32),
         ],
-        edge_offset, edge_other, block_start, node_state, border,
+        edge_offset, edge_other, block_start, node_state, gain_e,
         smem=(2,),
-        flops=2 * edges * f * (nodes + own),
+        flops=2 * edges * f * nodes,
+    )
+    halo += lay.fetch_theirs(halo)
+
+    def edge_far(place_ref, node_ref, border_ref, far_ref):
+        table = fold(jnp.concatenate([node_ref[...], border_ref[...]], axis=0))
+        for b in range(blocks):
+            place = place_ref[b : b + 1, :]
+            got = gather_folded(place, column(place), table)
+            far_ref[pl.ds(b * size, size), :] = got.astype(BF)
+
+    (far_own,) = call(
+        edge_far,
+        [shape(edges, f, BF)],
+        place, node_state, border,
+        flops=20 * edges * f * own,
     )
 
     def edge_forward(*refs):
@@ -379,8 +395,8 @@
 
     def node_kernel(
         part_ref, other_ref, node_ref, cot_ref, send_ref, entry_ref, middle_ref, outlet_ref,
-        gain_ref, new_ref, pulls_ref, border_ref, direct_ref, totals_ref, h1_ref, h2_ref,
-        first_ref, second_ref, og_ref, gain_grad_ref,
+        gain_ref, new_ref, pulls_ref, border_ref, totals_ref, h1_ref, h2_ref, first_ref,
+        second_ref, og_ref, gain_grad_ref,
     ):
         totals = (part_ref[...].astype(F32) + other_ref[...].astype(F32)).astype(BF)
         totals_ref[...] = totals
@@ -404,7 +420,6 @@
         pulls = mm_nt(first, entry_ref[f:, :]).astype(BF)
         pulls_ref[...] = pulls
         border_ref[...] = mm_tn(hot_rows(send_ref[...], nodes), pulls).astype(BF)
-        direct_ref[...] = up + mm_nt(first, entry_ref[:f, :])
 
     node_outs = call(
         node_kernel,
@@ -412,7 +427,6 @@
             shape(nodes, f, BF),
             shape(nodes, f, BF),
             shape(send, f, BF),
-            shape(nodes, f, F32),
         ]
         + [shape(nodes, f, BF)] * 6
         + [shape(1, f, F32)],
@@ -420,36 +434,54 @@
         node_outlet, gain_n,
         flops=2 * nodes * f * f * 8,
     )
-    own_new, pulls, pull_border, direct = node_outs[:4]
-    node_saved, node_gain_grad = node_outs[4:10], node_outs[10]
+    new_rows, pulls, pull_border = node_outs[:3]
+    node_saved, node_gain_grad = node_outs[3:9], node_outs[9]
     pull_halo = lay.fetch(pull_border)
 
-    def pull_local(
-        spot_ref, place_ref, count_ref, pulls_ref, border_ref, cot_ref, node_ref, totals_ref,
-        h1_ref, h2_ref, first_ref, second_ref, og_ref, up_ref, weight_ref,
+    def pull_near(
+        spot_ref, pulls_ref, node_ref, totals_ref, h1_ref, h2_ref, first_ref, second_ref, og_ref,
+        new_ref, got_ref, weight_ref, own_new_ref,
     ):
-        near_table = fold(pulls_ref[...])
-        own_table = fold(jnp.concatenate([pulls_ref[...], border_ref[...]], axis=0))
-        for b in range(blocks):
-            rows = pl.ds(b * size, size)
+        table = fold(pulls_ref[...])
+        for b in range(blocks):
             spot = spot_ref[b : b + 1, :]
-            place = place_ref[b : b + 1, :]
-            got = gather_folded(spot, column(spot), near_table)
-            got += gather_folded(place, column(place), own_table)
-            live = live_column(count_ref, b, size)
-            up_ref[rows, :] = cot_ref[rows, :].astype(F32) + live * got
+            got = gather_folded(spot, column(spot), table)
+            got_ref[pl.ds(b * size, size), :] = got.astype(BF)
         first = first_ref[...]
         weight_ref[:f, :] = (0.5 * mm_tn(node_ref[...], first)).astype(BF)
         weight_ref[f : 2 * f, :] = (0.5 * mm_tn(totals_ref[...], first)).astype(BF)
         weight_ref[2 * f : 3 * f, :] = (0.5 * mm_tn(h1_ref[...], second_ref[...])).astype(BF)
         weight_ref[3 * f :, :] = (0.5 * mm_tn(h2_ref[...], og_ref[...])).astype(BF)
-
-    up_own, node_weights = call(
-        pull_local,
-        [shape(edges, f, F32), shape(4 * f, f, BF)],
-        spot, place, edge_count, pulls, pull_border, edge_cotangent, node_state, *node_saved,
-        smem=(2,),
-        flops=2 * edges * f * (nodes + own) + 8 * nodes * f * f,
+        own_new_ref[...] = new_ref[...]
+
+    got_near, node_weights, own_new = call(
+        pull_near,
+        [shape(edges, f, BF), shape(4 * f, f, BF), shape(nodes, f, BF)],
+        spot, pulls, node_state, *node_saved, new_rows,
+        flops=2 * edges * f * nodes + 8 * nodes * f * f,
+    )
+    pull_halo += lay.fetch_theirs(pull_halo)
+
+    def pull_far(
+        place_ref, count_ref, got_ref, pulls_ref, border_ref, cot_ref, first_ref, node_cot_ref,
+        entry_ref, up_ref, direct_ref,
+    ):
+        table = fold(jnp.concatenate([pulls_ref[...], border_ref[...]], axis=0))
+        for b in range(blocks):
+            rows = pl.ds(b * size, size)
+            place = place_ref[b : b + 1, :]
+            got = got_ref[rows, :].astype(F32) + gather_folded(place, column(place), table)
+            live = live_column(count_ref, b, size)
+            up_ref[rows, :] = cot_ref[rows, :].astype(F32) + live * got
+        direct_ref[...] = node_cot_ref[...].astype(F32) + mm_nt(first_ref[...], entry_ref[:f, :])
+
+    up_own, direct = call(
+        pull_far,
+        [shape(edges, f, F32), shape(nodes, f, F32)],
+        place, edge_count, got_near, pulls, pull_border, edge_cotangent, node_saved[3],
+        node_cotangent, node_entry,
+        smem=(1,),
+        flops=20 * edges * f * own,
     )
 
     subs = lax.axis_size("sub")

time: 71.9 us -> 69.2 us (0.962)
  waiting for transfers between devices: 12.9 us -> 11.4 us
  starting transfers between devices: 33.2 us -> 32.2 us
    ppermute x12, waiting for transfers between devices: 1.71 us -> 0.09 us  [permute(): return lax.ppermute(value, AXES, pairs)]
    ppermute x12, starting transfers between devices: 20.6 us -> 19.8 us  [permute(): return lax.ppermute(value, AXES, pairs)]
    pallas_call x19 -> x21, Pallas kernels: 20.9 us -> 21.4 us  [call(): pl.pallas_call(inner, out_shape=list(outs) + [jax.ShapeDtypeStruct(a.shap...]
  transfers between devices with their start and end apart: 26 -> 26, of which waited for: 11 -> 8; matrix products, arithmetic and copies ran while one was open for 1% -> 1% of each run, Pallas kernels for 13% -> 15%
where the time goes in v5:
time: 69.2 us; the launch traced here: 69 us
  starting transfers between devices  32.2 us (47%)
  Pallas kernels  21.4 us (31%)
  waiting for transfers between devices  11.4 us (16%)
  local copies, waits for them, and re-layouts  1.64 us (2%)
  between operations  1.63 us (2%)
  other arithmetic  0.7 us (1%)
    pallas_call x21, Pallas kernels, call(): pl.pallas_call(inner, out_shape=list(outs) + [jax.ShapeDtypeStruct(a.shap...  21.4 us
    ppermute x12, starting transfers between devices, permute(): return lax.ppermute(value, AXES, pairs)  19.8 us
    ppermute x14, starting transfers between devices, swap_axis(): return lax.ppermute(value, axis, [(j, j ^ mask) for j in range(count)])  12.4 us
    ppermute x14, waiting for transfers between devices, swap_axis(): return lax.ppermute(value, axis, [(j, j ^ mask) for j in range(count)])  11.3 us
    unnamed x34, local copies, waits for them, and re-layouts  1.64 us
  transfers between devices with their start and end apart: 26, of which 8 were waited for; matrix products, arithmetic and copies ran while one was open for 1% of the time, Pallas kernels for 15%

profile of v5, /device:TPU:0, one launch (start us, length us, event | category | flops | bytes accessed | tf_op | source)
XLA Modules:
  0.0 69.0 jit_solution(12921977110544946699)
XLA Ops:
  0.6 0.7 copy-done.9
  1.3 0.9 %copy-done = bf16[512,128]{1,0:T(8,128)(2,1)S(1)} copy-done((bf16[512,128]{1,0:T(8,128)(2,1)S(1)}, bf16[512,128]{1,0:T(8,128)(2,1)}, u32[]{:S(2)}) %copy-start) | copy-done | bytes 131096
  2.5 3.1 %collective-permute-start.1 = (bf16[256,128]{1,0:T(8,128)(2,1)S(1)}, bf16[256,128]{1,0:T(8,128)(2,1)S(1)}, u32[]{:S(2)}, u32[]{:S(2)}) collective-permute-start(bf16[256,128]{1,0:T(8,128)(2,1)S(1)} %shard_map.217.refs_2_), channel_id=1, source_target_pairs={{0,4},{1,7},{2,6},{3,5},{4,0},{5,3},{6,2},{7,1},{8,12},{9,15},{10,... | collective-permute-start | bytes 196616 | tf_op jit(solution)/shard_map/ppermute | solution.py:125
  6.3 1.6 %collective-permute-start.2 = (bf16[256,128]{1,0:T(8,128)(2,1)S(1)}, bf16[256,128]{1,0:T(8,128)(2,1)S(1)}, u32[]{:S(2)}, u32[]{:S(2)}) collective-permute-start(bf16[256,128]{1,0:T(8,128)(2,1)S(1)} %shard_map.217.refs_2_), channel_id=1, source_target_pairs={{0,2},{1,3},{2,0},{3,1},{4,6},{5,7},{6,4},{7,5},{8,10},{9,11},{10,... | collective-permute-start | bytes 196616 | tf_op jit(solution)/shard_map/ppermute | solution.py:125
  7.9 1.5 %shard_map.216 = (bf16[1536,128]{1,0:T(8,128)(2,1)S(1)}, s32[6,256]{1,0:T(8,128)S(1)}, s32[6,256]{1,0:T(8,128)S(1)}, f32[1,128]{1,0:T(1,128)S(1)}) custom-call(s32[1536]{0:T(1024)S(1)} %copy-done.13, s32[1536]{0:T(1024)S(1)} %copy-done.14, s32[6]{0:T(128)S(1)} %copy-done.15, bf16[512,128]{1,0:T(8,128)(2,1)S(1)} %copy-done.1, f32[1,128]{1,0:T(1,128)S(1)} %bitcast.10), custom_call_target="tpu_custom_call" | custom-call | flops 201326592 | bytes 549912 | tf_op jit(solution)/shard_map/pallas_call | solution.py:187
  9.9 1.0 %shard_map.218.refs_3_ = bf16[1536,128]{1,0:T(8,128)(2,1)S(1)} custom-call(s32[6,256]{1,0:T(8,128)S(1)} %get-tuple-element.60.refs_0_.refs_1_, bf16[512,128]{1,0:T(8,128)(2,1)S(1)} %copy-done.1, bf16[256,128]{1,0:T(8,128)(2,1)S(1)} %shard_map.217.refs_2_), custom_call_target="tpu_custom_call" | custom-call | flops 3019898880 | bytes 595968 | tf_op jit(solution)/shard_map/pallas_call | solution.py:187
  11.6 4.1 %shard_map.219 = (bf16[1536,128]{1,0:T(8,128)(2,1)S(1)}, bf16[1536,128]{1,0:T(8,128)(2,1)S(1)}, bf16[1536,128]{1,0:T(8,128)(2,1)S(1)}, bf16[1536,128]{1,0:T(8,12...) custom-call(s32[6,256]{1,0:T(8,128)S(1)} %get-tuple-element.60.refs_, ...), custom_call_target="tpu_custom_call" | custom-call | flops 1258291200 | bytes 6068740 | tf_op jit(solution)/shard_map/pallas_call | solution.py:187
  15.9 0.7 collective-permute-start.8
  17.2 4.7 %collective-permute-start.6 = (bf16[256,128]{1,0:T(8,128)(2,1)S(1)}, bf16[256,128]{1,0:T(8,128)(2,1)S(1)}, u32[]{:S(2)}, u32[]{:S(2)}) collective-permute-start(bf16[256,128]{1,0:T(8,128)(2,1)S(1)} %get-tuple-element.67), channel_id=1, source_target_pairs={{0,4},{1,7},{2,6},{3,5},{4,0},{5,3},{6,2},{7,1},{8,12},{9,15},{10,... | collective-permute-start | bytes 196616 | tf_op jit(solution)/shard_map/ppermute | solution.py:125
  22.5 1.7 %shard_map.220 = (bf16[1536,128]{1,0:T(8,128)(2,1)}, f32[512,128]{1,0:T(8,128)S(1)}) custom-call(s32[6,256]{1,0:T(8,128)S(1)} %get-tuple-element.59.refs_0_, s32[6,256]{1,0:T(8,128)S(1)} %get-tuple-element.60.refs_0_.refs_1_, s32[1,256]{1,0:T(1,128)S(1)} %bitcast.4, s32[1]{0:T(128)S(6)} %copy.26.refs_1_.refs_3_, bf16[1536,128]{1,0:T(8,128)(2,1)S(1)} %copy-done.2, ...), custom_call_target="tpu_custom_call" | custom-call | flops 503316480 | bytes 1455108 | tf_op jit(solution)/shard_map/pallas_call | solution.py:187
  25.3 1.0 %collective-permute-done.9.refs_1_ = bf16[512,128]{1,0:T(8,128)(2,1)S(1)} collective-permute-done((bf16[512,128]{1,0:T(8,128)(2,1)S(1)}, bf16[512,128]{1,0:T(8,128)(2,1)S(1)}, u32[]{:S(2)}, u32[]{:S(2)}) %collective-permute-start.9) | collective-permute-done | bytes 131104 | tf_op jit(solution)/shard_map/ppermute | solution.py:171
  26.3 1.3 %shard_map.223 = (bf16[512,128]{1,0:T(8,128)(2,1)S(1)}, bf16[512,128]{1,0:T(8,128)(2,1)S(1)}, bf16[256,128]{1,0:T(8,128)(2,1)S(1)}, bf16[512,128]{1,0:T(8,128)(2...) custom-call(bf16[512,128]{1,0:T(8,128)(2,1)S(1)} %shard_map.222.refs, ...), custom_call_target="tpu_custom_call" | custom-call | flops 134217728 | bytes 1771520 | tf_op jit(solution)/shard_map/pallas_call | solution.py:187
  27.6 4.5 %collective-permute-start.11 = (bf16[256,128]{1,0:T(8,128)(2,1)S(1)}, bf16[256,128]{1,0:T(8,128)(2,1)S(1)}, u32[]{:S(2)}, u32[]{:S(2)}) collective-permute-start(bf16[256,128]{1,0:T(8,128)(2,1)S(1)} %get-tuple-element.81.refs_4_), channel_id=1, source_target_pairs={{0,4},{1,7},{2,6},{3,5},{4,0},{5,3},{6,2},{7,1},{8,12},{9,15},{10,... | collective-permute-start | bytes 196616 | tf_op jit(solution)/shard_map/ppermute | solution.py:125
  32.2 0.8 %collective-permute-start.10 = (bf16[256,128]{1,0:T(8,128)(2,1)S(1)}, bf16[256,128]{1,0:T(8,128)(2,1)S(1)}, u32[]{:S(2)}, u32[]{:S(2)}) collective-permute-start(bf16[256,128]{1,0:T(8,128)(2,1)S(1)} %get-tuple-element.81.refs_4_), channel_id=1, source_target_pairs={{4,10},{5,9},{6,8},{7,11},{8,6},{9,5},{10,4},{11,7},{20,26},{21,25... | collective-permute-start | bytes 196616 | tf_op jit(solution)/shard_map/ppermute | solution.py:125
  33.0 1.3 %collective-permute-start.12 = (bf16[256,128]{1,0:T(8,128)(2,1)S(1)}, bf16[256,128]{1,0:T(8,128)(2,1)S(1)}, u32[]{:S(2)}, u32[]{:S(2)}) collective-permute-start(bf16[256,128]{1,0:T(8,128)(2,1)S(1)} %get-tuple-element.81.refs_4_), channel_id=1, source_target_pairs={{0,2},{1,3},{2,0},{3,1},{4,6},{5,7},{6,4},{7,5},{8,10},{9,11},{10,... | collective-permute-start | bytes 196616 | tf_op jit(solution)/shard_map/ppermute | solution.py:125
  34.3 1.6 %shard_map.224 = (bf16[1536,128]{1,0:T(8,128)(2,1)S(1)}, bf16[512,128]{1,0:T(8,128)(2,1)S(1)}, bf16[512,128]{1,0:T(8,128)(2,1)}) custom-call(s32[6,256]{1,0:T(8,128)S(1)} %get-tuple-element.59.refs_0_, bf16[512,128]{1,0:T(8,128)(2,1)S(1)} %get-tuple-element.70.refs_1_.refs_3_, bf16[512,128]{1,0:T(8,128)(2,1)S(1)} %copy-done.1, ...), custom_call_target="tpu_custom_call" | custom-call | flops 268435456 | bytes 1841152 | tf_op jit(solution)/shard_map/pallas_call | solution.py:187
  36.5 1.1 %shard_map.225 = (f32[1536,128]{1,0:T(8,128)S(1)}, f32[512,128]{1,0:T(8,128)S(1)}) custom-call(s32[6,256]{1,0:T(8,128)S(1)} %get-tuple-element.60.refs_0_.refs_1_, s32[1]{0:T(128)S(6)} %copy.26.refs_1_.refs_3_, bf16[1536,128]{1,0:T(8,128)(2,1)S(1)} %get-tuple-element.80.refs_2_, bf16[512,128]{1,0:T(8,128)(2,1)S(1)} %get-tuple-element.70.refs_1_.refs_3_, ...), custom_call_target="tpu_custom_call" | custom-call | flops 3019898880 | bytes 2365444 | tf_op jit(solution)/shard_map/pallas_call | solution.py:187
  37.7 4.1 %shard_map.226 = (f32[1536,128]{1,0:T(8,128)S(1)}, bf16[1536,128]{1,0:T(8,128)(2,1)S(1)}, bf16[608,128]{1,0:T(8,128)(2,1)S(1)}, bf16[608,128]{1,0:T(8,128)(2,1)S(1)}) custom-call(s32[6,256]{1,0:T(8,128)S(1)} %get-tuple-element.60.refs_0_.refs_1_, s32[1]{0:T(128)S(6)} %copy.26.refs_1_.refs_3_, f32[1536,128]{1,0:T(8,128)S(1)} %get-tuple-element.82.refs_2_, ...), custom_call_target="tpu_custom_call" | custom-call | flops 855638016 | bytes 7134212 | tf_op jit(solution)/shard_map/pallas_call | solution.py:187
  41.9 1.3 %collective-permute-done.15.refs_1_ = bf16[608,128]{1,0:T(8,128)(2,1)S(1)} collective-permute-done((bf16[608,128]{1,0:T(8,128)(2,1)S(1)}, bf16[608,128]{1,0:T(8,128)(2,1)S(1)}, u32[]{:S(2)}, u32[]{:S(2)}) %collective-permute-start.15) | collective-permute-done | bytes 155680 | tf_op jit(solution)/shard_map/ppermute | solution.py:171
  43.3 1.0 %collective-permute-start.16 = (bf16[304,128]{1,0:T(8,128)(2,1)S(1)}, bf16[304,128]{1,0:T(8,128)(2,1)S(1)}, u32[]{:S(2)}, u32[]{:S(2)}) collective-permute-start(bf16[304,128]{1,0:T(8,128)(2,1)S(1)} %get-tuple-element.96), channel_id=1, source_target_pairs={{0,2},{2,0},{1,3},{3,1},{4,6},{6,4},{5,7},{7,5},{8,10},{10,8},{9,1... | collective-permute-start | bytes 233480 | tf_op jit(solution)/shard_map/ppermute | solution.py:171
  44.3 1.0 %shard_map.229 = (bf16[1536,128]{1,0:T(8,128)(2,1)S(1)}, f32[512,128]{1,0:T(8,128)S(1)}, bf16[256,128]{1,0:T(8,128)(2,1)S(1)}, bf16[512,128]{1,0:T(8,128)(2,1)S(1)}) custom-call(s32[6,256]{1,0:T(8,128)S(1)} %get-tuple-element.60.refs_0_.refs_1_, bf16[1536,128]{1,0:T(8,128)(2,1)S(1)} %get-tuple-element.92.refs_1_.refs_4_, bf16[384,128]{1,0:T(8,128)(2,1)S(1)} %copy-done.12), custom_call_target="tpu_custom_call" | custom-call | flops 553648128 | bytes 1349632 | tf_op jit(solution)/shard_map/pallas_call | solution.py:187
  45.4 2.3 %collective-permute-done.16.refs_1_ = bf16[304,128]{1,0:T(8,128)(2,1)S(1)} collective-permute-done((bf16[304,128]{1,0:T(8,128)(2,1)S(1)}, bf16[304,128]{1,0:T(8,128)(2,1)S(1)}, u32[]{:S(2)}, u32[]{:S(2)}) %collective-permute-start.16) | collective-permute-done | bytes 77856 | tf_op jit(solution)/shard_map/ppermute | solution.py:171
  47.8 3.5 %collective-permute-start.17 = (bf16[304,128]{1,0:T(8,128)(2,1)S(1)}, bf16[304,128]{1,0:T(8,128)(2,1)S(1)}, u32[]{:S(2)}, u32[]{:S(2)}) collective-permute-start(bf16[304,128]{1,0:T(8,128)(2,1)S(1)} %shard_map.228.refs_0_), channel_id=1, source_target_pairs={{0,4},{4,0},{8,12},{12,8},{1,5},{5,1},{9,13},{13,9},{2,6},{6,2},{1... | collective-permute-start | bytes 233480 | tf_op jit(solution)/shard_map/ppermute | solution.py:171
  51.3 1.0 %collective-permute-start.21 = (bf16[256,128]{1,0:T(8,128)(2,1)S(1)}, bf16[256,128]{1,0:T(8,128)(2,1)S(1)}, u32[]{:S(2)}, u32[]{:S(2)}) collective-permute-start(bf16[256,128]{1,0:T(8,128)(2,1)S(1)} %get-tuple-element.104), channel_id=1, source_target_pairs={{0,2},{1,3},{2,0},{3,1},{4,6},{5,7},{6,4},{7,5},{8,10},{9,11},{10,... | collective-permute-start | bytes 196616 | tf_op jit(solution)/shard_map/ppermute | solution.py:125
  53.7 4.7 %collective-permute-start.23 = (bf16[304,128]{1,0:T(8,128)(2,1)S(1)}, bf16[304,128]{1,0:T(8,128)(2,1)S(1)}, u32[]{:S(2)}, u32[]{:S(2)}) collective-permute-start(bf16[304,128]{1,0:T(8,128)(2,1)S(1)} %get-tuple-element.107.refs_0_), channel_id=1, source_target_pairs={{0,8},{4,12},{8,0},{12,4},{1,9},{5,13},{9,1},{13,5},{2,10},{6,14},... | collective-permute-start | bytes 233480 | tf_op jit(solution)/shard_map/ppermute | solution.py:171
  58.4 1.8 %shard_map.231 = (bf16[1536,128]{1,0:T(8,128)(2,1)}, f32[512,128]{1,0:T(8,128)S(1)}) custom-call(s32[6,256]{1,0:T(8,128)S(1)} %get-tuple-element.59.refs_0_, s32[6,256]{1,0:T(8,128)S(1)} %get-tuple-element.60.refs_0_.refs_1_, s32[1,256]{1,0:T(1,128)S(1)} %bitcast.7, f32[1536,128]{1,0:T(8,128)S(1)} %get-tuple-element.91.refs_3_, ...), custom_call_target="tpu_custom_call" | custom-call | flops 603979776 | bytes 2339840 | tf_op jit(solution)/shard_map/pallas_call | solution.py:187
  60.7 1.5 %collective-permute-done.23.refs_1_ = bf16[304,128]{1,0:T(8,128)(2,1)S(1)} collective-permute-done((bf16[304,128]{1,0:T(8,128)(2,1)S(1)}, bf16[304,128]{1,0:T(8,128)(2,1)S(1)}, u32[]{:S(2)}, u32[]{:S(2)}) %collective-permute-start.23) | collective-permute-done | bytes 77856 | tf_op jit(solution)/shard_map/ppermute | solution.py:171
  62.2 1.1 %collective-permute-start.24 = (bf16[304,128]{1,0:T(8,128)(2,1)S(1)}, bf16[304,128]{1,0:T(8,128)(2,1)S(1)}, u32[]{:S(2)}, u32[]{:S(2)}) collective-permute-start(bf16[304,128]{1,0:T(8,128)(2,1)S(1)} %shard_map.234.refs_0_), channel_id=1, source_target_pairs={{0,2},{2,0},{1,3},{3,1},{4,6},{6,4},{5,7},{7,5},{8,10},{10,8},{9,1... | collective-permute-start | bytes 233480 | tf_op jit(solution)/shard_map/ppermute | solution.py:171
  63.2 3.4 %collective-permute-done.24.refs_1_ = bf16[304,128]{1,0:T(8,128)(2,1)S(1)} collective-permute-done((bf16[304,128]{1,0:T(8,128)(2,1)S(1)}, bf16[304,128]{1,0:T(8,128)(2,1)S(1)}, u32[]{:S(2)}, u32[]{:S(2)}) %collective-permute-start.24) | collective-permute-done | bytes 77856 | tf_op jit(solution)/shard_map/ppermute | solution.py:171
  66.7 0.7 %add_convert_fusion = bf16[512,128]{1,0:T(8,128)(2,1)} fusion(f32[512,128]{1,0:T(8,128)S(1)} %get-tuple-element.105, bf16[512,128]{1,0:T(8,128)(2,1)S(1)} %collective-permute-done.22, bf16[512,128]{1,0:T(8,128)(2,1)S(1)} %shard_map.233), kind=kLoop, calls=%fused_computation | loop fusion | flops 327680 | bytes 655360 | tf_op jit(solution)/shard_map/convert_element_type | solution.py:656
  67.4 0.7 collective-permute-done.25.refs_1_
  68.1 0.9 %shard_map.236 = (f32[640,128]{1,0:T(8,128)}, f32[512,128]{1,0:T(8,128)}, f32[2,128]{1,0:T(2,128)}) custom-call(bf16[608,128]{1,0:T(8,128)(2,1)S(1)} %shard_map.235.refs_0_, bf16[608,128]{1,0:T(8,128)(2,1)S(1)} %collective-permute-done.25.refs_1_), custom_call_target="tpu_custom_call" | custom-call | bytes 902144 | tf_op jit(solution)/shard_map/pallas_call | solution.py:187
  (76 shorter events, 6.8 us)
Async XLA Ops:
  2.2 5.6 %copy-start.1 = (bf16[512,128]{1,0:T(8,128)(2,1)S(1)}, bf16[512,128]{1,0:T(8,128)(2,1)}, u32[]{:S(2)}) copy-start(bf16[512,128]{1,0:T(8,128)(2,1)} %refs_2_.8) | copy-start | bytes 393220
  2.2 5.6 %copy-start.13 = (s32[1536]{0:T(1024)S(1)}, s32[1536]{0:T(1024)}, u32[]{:S(2)}) copy-start(s32[1536]{0:T(1024)} %refs_0_.1) | copy-start | bytes 18436
  2.2 5.6 %copy-start.14 = (s32[1536]{0:T(1024)S(1)}, s32[1536]{0:T(1024)}, u32[]{:S(2)}) copy-start(s32[1536]{0:T(1024)} %refs_1_.6) | copy-start | bytes 18436
  2.5 5.3 %copy-start.15 = (s32[6]{0:T(128)S(1)}, s32[6]{0:T(128)}, u32[]{:S(2)}) copy-start(s32[6]{0:T(128)} %refs_2_.5) | copy-start | bytes 76
  2.5 5.3 %copy-start.16 = (f32[128]{0:T(128)S(1)}, f32[128]{0:T(128)}, u32[]{:S(2)}) copy-start(f32[128]{0:T(128)} %param.27) | copy-start | bytes 1540
  2.5 6.8 %collective-permute-start.1 = (bf16[256,128]{1,0:T(8,128)(2,1)S(1)}, bf16[256,128]{1,0:T(8,128)(2,1)S(1)}, u32[]{:S(2)}, u32[]{:S(2)}) collective-permute-start(bf16[256,128]{1,0:T(8,128)(2,1)S(1)} %shard_map.217.refs_2_), channel_id=1, source_target_pairs={{0,4},{1,7},{2,6},{3,5},{4,0},{5,3},{6,2},{7,1},{8,12},{9,15},{10,... | collective-permute-start | bytes 196616 | tf_op jit(solution)/shard_map/ppermute | solution.py:125
  5.6 3.8 %collective-permute-start = (bf16[256,128]{1,0:T(8,128)(2,1)S(1)}, bf16[256,128]{1,0:T(8,128)(2,1)S(1)}, u32[]{:S(2)}, u32[]{:S(2)}) collective-permute-start(bf16[256,128]{1,0:T(8,128)(2,1)S(1)} %shard_map.217.refs_2_), channel_id=1, source_target_pairs={{4,10},{5,9},{6,8},{7,11},{8,6},{9,5},{10,4},{11,7},{20,26},{21,25... | collective-permute-start | bytes 196616 | tf_op jit(solution)/shard_map/ppermute | solution.py:125
  6.3 5.3 %collective-permute-start.2 = (bf16[256,128]{1,0:T(8,128)(2,1)S(1)}, bf16[256,128]{1,0:T(8,128)(2,1)S(1)}, u32[]{:S(2)}, u32[]{:S(2)}) collective-permute-start(bf16[256,128]{1,0:T(8,128)(2,1)S(1)} %shard_map.217.refs_2_), channel_id=1, source_target_pairs={{0,2},{1,3},{2,0},{3,1},{4,6},{5,7},{6,4},{7,5},{8,10},{9,11},{10,... | collective-permute-start | bytes 196616 | tf_op jit(solution)/shard_map/ppermute | solution.py:125
  9.3 2.2 %collective-permute-start.4 = (bf16[256,128]{1,0:T(8,128)(2,1)S(1)}, bf16[256,128]{1,0:T(8,128)(2,1)S(1)}, u32[]{:S(2)}, u32[]{:S(2)}) collective-permute-start(bf16[256,128]{1,0:T(8,128)(2,1)S(1)} %collective-permute-done.1.refs_10_), channel_id=1, source_target_pairs={{0,1},{1,0},{2,3},{3,2},{4,5},{5,4},{6,7},{7,6},{8,9},{9,8},{10,11... | collective-permute-start | bytes 196616 | tf_op jit(solution)/shard_map/ppermute | solution.py:171
  9.4 2.1 %collective-permute-start.3 = (bf16[256,128]{1,0:T(8,128)(2,1)S(1)}, bf16[256,128]{1,0:T(8,128)(2,1)S(1)}, u32[]{:S(2)}, u32[]{:S(2)}) collective-permute-start(bf16[256,128]{1,0:T(8,128)(2,1)S(1)} %collective-permute-done.refs_9_), channel_id=1, source_target_pairs={{0,1},{1,0},{2,3},{3,2},{4,5},{5,4},{6,7},{7,6},{8,9},{9,8},{10,11... | collective-permute-start | bytes 196616 | tf_op jit(solution)/shard_map/ppermute | solution.py:171
  15.7 1.4 %collective-permute-start.5 = (bf16[512,128]{1,0:T(8,128)(2,1)S(1)}, bf16[512,128]{1,0:T(8,128)(2,1)S(1)}, u32[]{:S(2)}, u32[]{:S(2)}) collective-permute-start(bf16[512,128]{1,0:T(8,128)(2,1)S(1)} %get-tuple-element.66), channel_id=1, source_target_pairs={{0,1},{1,0},{2,3},{3,2},{4,5},{5,4},{6,7},{7,6},{8,9},{9,8},{10,11... | collective-permute-start | bytes 393224 | tf_op jit(solution)/shard_map/ppermute | solution.py:171
  15.9 8.3 %collective-permute-start.8 = (bf16[256,128]{1,0:T(8,128)(2,1)S(1)}, bf16[256,128]{1,0:T(8,128)(2,1)S(1)}, u32[]{:S(2)}, u32[]{:S(2)}) collective-permute-start(bf16[256,128]{1,0:T(8,128)(2,1)S(1)} %get-tuple-element.69), channel_id=1, source_target_pairs={{0,2},{1,3},{2,0},{3,1},{4,6},{5,7},{6,4},{7,5},{8,10},{9,11},{10,... | collective-permute-start | bytes 196616 | tf_op jit(solution)/shard_map/ppermute | solution.py:125
  17.2 7.1 %collective-permute-start.6 = (bf16[256,128]{1,0:T(8,128)(2,1)S(1)}, bf16[256,128]{1,0:T(8,128)(2,1)S(1)}, u32[]{:S(2)}, u32[]{:S(2)}) collective-permute-start(bf16[256,128]{1,0:T(8,128)(2,1)S(1)} %get-tuple-element.67), channel_id=1, source_target_pairs={{0,4},{1,7},{2,6},{3,5},{4,0},{5,3},{6,2},{7,1},{8,12},{9,15},{10,... | collective-permute-start | bytes 196616 | tf_op jit(solution)/shard_map/ppermute | solution.py:125
  21.8 2.4 %collective-permute-start.7 = (bf16[256,128]{1,0:T(8,128)(2,1)S(1)}, bf16[256,128]{1,0:T(8,128)(2,1)S(1)}, u32[]{:S(2)}, u32[]{:S(2)}) collective-permute-start(bf16[256,128]{1,0:T(8,128)(2,1)S(1)} %get-tuple-element.68), channel_id=1, source_target_pairs={{4,10},{5,9},{6,8},{7,11},{8,6},{9,5},{10,4},{11,7},{20,26},{21,25... | collective-permute-start | bytes 196616 | tf_op jit(solution)/shard_map/ppermute | solution.py:125
  24.7 1.6 %collective-permute-start.9 = (bf16[512,128]{1,0:T(8,128)(2,1)S(1)}, bf16[512,128]{1,0:T(8,128)(2,1)S(1)}, u32[]{:S(2)}, u32[]{:S(2)}) collective-permute-start(bf16[512,128]{1,0:T(8,128)(2,1)S(1)} %shard_map.222.refs_0_), channel_id=1, source_target_pairs={{0,1},{1,0},{2,3},{3,2},{4,5},{5,4},{6,7},{7,6},{8,9},{9,8},{10,11... | collective-permute-start | bytes 393224 | tf_op jit(solution)/shard_map/ppermute | solution.py:171
  27.6 8.3 %collective-permute-start.11 = (bf16[256,128]{1,0:T(8,128)(2,1)S(1)}, bf16[256,128]{1,0:T(8,128)(2,1)S(1)}, u32[]{:S(2)}, u32[]{:S(2)}) collective-permute-start(bf16[256,128]{1,0:T(8,128)(2,1)S(1)} %get-tuple-element.81.refs_4_), channel_id=1, source_target_pairs={{0,4},{1,7},{2,6},{3,5},{4,0},{5,3},{6,2},{7,1},{8,12},{9,15},{10,... | collective-permute-start | bytes 196616 | tf_op jit(solution)/shard_map/ppermute | solution.py:125
  32.2 3.8 %collective-permute-start.10 = (bf16[256,128]{1,0:T(8,128)(2,1)S(1)}, bf16[256,128]{1,0:T(8,128)(2,1)S(1)}, u32[]{:S(2)}, u32[]{:S(2)}) collective-permute-start(bf16[256,128]{1,0:T(8,128)(2,1)S(1)} %get-tuple-element.81.refs_4_), channel_id=1, source_target_pairs={{4,10},{5,9},{6,8},{7,11},{8,6},{9,5},{10,4},{11,7},{20,26},{21,25... | collective-permute-start | bytes 196616 | tf_op jit(solution)/shard_map/ppermute | solution.py:125
  33.0 4.6 %collective-permute-start.12 = (bf16[256,128]{1,0:T(8,128)(2,1)S(1)}, bf16[256,128]{1,0:T(8,128)(2,1)S(1)}, u32[]{:S(2)}, u32[]{:S(2)}) collective-permute-start(bf16[256,128]{1,0:T(8,128)(2,1)S(1)} %get-tuple-element.81.refs_4_), channel_id=1, source_target_pairs={{0,2},{1,3},{2,0},{3,1},{4,6},{5,7},{6,4},{7,5},{8,10},{9,11},{10,... | collective-permute-start | bytes 196616 | tf_op jit(solution)/shard_map/ppermute | solution.py:125
  34.3 2.2 %copy-start.11 = (bf16[1536,128]{1,0:T(8,128)(2,1)S(1)}, bf16[1536,128]{1,0:T(8,128)(2,1)}, u32[]{:S(2)}) copy-start(bf16[1536,128]{1,0:T(8,128)(2,1)} %refs_5_.5) | copy-start | bytes 1179652
  36.0 1.7 %collective-permute-start.14 = (bf16[256,128]{1,0:T(8,128)(2,1)S(1)}, bf16[256,128]{1,0:T(8,128)(2,1)S(1)}, u32[]{:S(2)}, u32[]{:S(2)}) collective-permute-start(bf16[256,128]{1,0:T(8,128)(2,1)S(1)} %collective-permute-done.11.refs_17_), channel_id=1, source_target_pairs={{0,1},{1,0},{2,3},{3,2},{4,5},{5,4},{6,7},{7,6},{8,9},{9,8},{10,11... | collective-permute-start | bytes 196616 | tf_op jit(solution)/shard_map/ppermute | solution.py:171
  36.0 1.7 %collective-permute-start.13 = (bf16[256,128]{1,0:T(8,128)(2,1)S(1)}, bf16[256,128]{1,0:T(8,128)(2,1)S(1)}, u32[]{:S(2)}, u32[]{:S(2)}) collective-permute-start(bf16[256,128]{1,0:T(8,128)(2,1)S(1)} %collective-permute-done.10.refs_16_), channel_id=1, source_target_pairs={{0,1},{1,0},{2,3},{3,2},{4,5},{5,4},{6,7},{7,6},{8,9},{9,8},{10,11... | collective-permute-start | bytes 196616 | tf_op jit(solution)/shard_map/ppermute | solution.py:171
  41.8 1.4 %collective-permute-start.15 = (bf16[608,128]{1,0:T(8,128)(2,1)S(1)}, bf16[608,128]{1,0:T(8,128)(2,1)S(1)}, u32[]{:S(2)}, u32[]{:S(2)}) collective-permute-start(bf16[608,128]{1,0:T(8,128)(2,1)S(1)} %get-tuple-element.94), channel_id=1, source_target_pairs={{0,1},{1,0},{2,3},{3,2},{4,5},{5,4},{6,7},{7,6},{8,9},{9,8},{10,11... | collective-permute-start | bytes 466952 | tf_op jit(solution)/shard_map/ppermute | solution.py:171
  43.3 4.5 %collective-permute-start.16 = (bf16[304,128]{1,0:T(8,128)(2,1)S(1)}, bf16[304,128]{1,0:T(8,128)(2,1)S(1)}, u32[]{:S(2)}, u32[]{:S(2)}) collective-permute-start(bf16[304,128]{1,0:T(8,128)(2,1)S(1)} %get-tuple-element.96), channel_id=1, source_target_pairs={{0,2},{2,0},{1,3},{3,1},{4,6},{6,4},{5,7},{7,5},{8,10},{10,8},{9,1... | collective-permute-start | bytes 233480 | tf_op jit(solution)/shard_map/ppermute | solution.py:171
  45.3 7.0 %collective-permute-start.18 = (bf16[512,128]{1,0:T(8,128)(2,1)S(1)}, bf16[512,128]{1,0:T(8,128)(2,1)S(1)}, u32[]{:S(2)}, u32[]{:S(2)}) collective-permute-start(bf16[512,128]{1,0:T(8,128)(2,1)S(1)} %get-tuple-element.101), channel_id=1, source_target_pairs={{0,1},{1,0},{2,3},{3,2},{4,5},{5,4},{6,7},{7,6},{8,9},{9,8},{10,11... | collective-permute-start | bytes 393224 | tf_op jit(solution)/shard_map/ppermute | solution.py:171
  47.8 5.9 %collective-permute-start.17 = (bf16[304,128]{1,0:T(8,128)(2,1)S(1)}, bf16[304,128]{1,0:T(8,128)(2,1)S(1)}, u32[]{:S(2)}, u32[]{:S(2)}) collective-permute-start(bf16[304,128]{1,0:T(8,128)(2,1)S(1)} %shard_map.228.refs_0_), channel_id=1, source_target_pairs={{0,4},{4,0},{8,12},{12,8},{1,5},{5,1},{9,13},{13,9},{2,6},{6,2},{1... | collective-permute-start | bytes 233480 | tf_op jit(solution)/shard_map/ppermute | solution.py:171
  51.3 8.9 %collective-permute-start.21 = (bf16[256,128]{1,0:T(8,128)(2,1)S(1)}, bf16[256,128]{1,0:T(8,128)(2,1)S(1)}, u32[]{:S(2)}, u32[]{:S(2)}) collective-permute-start(bf16[256,128]{1,0:T(8,128)(2,1)S(1)} %get-tuple-element.104), channel_id=1, source_target_pairs={{0,2},{1,3},{2,0},{3,1},{4,6},{5,7},{6,4},{7,5},{8,10},{9,11},{10,... | collective-permute-start | bytes 196616 | tf_op jit(solution)/shard_map/ppermute | solution.py:125
  52.4 7.8 %collective-permute-start.19 = (bf16[256,128]{1,0:T(8,128)(2,1)S(1)}, bf16[256,128]{1,0:T(8,128)(2,1)S(1)}, u32[]{:S(2)}, u32[]{:S(2)}) collective-permute-start(bf16[256,128]{1,0:T(8,128)(2,1)S(1)} %get-tuple-element.102), channel_id=1, source_target_pairs={{0,4},{1,7},{2,6},{3,5},{4,0},{5,3},{6,2},{7,1},{8,12},{9,15},{10,... | collective-permute-start | bytes 196616 | tf_op jit(solution)/shard_map/ppermute | solution.py:125
  52.5 7.7 %collective-permute-start.20 = (bf16[256,128]{1,0:T(8,128)(2,1)S(1)}, bf16[256,128]{1,0:T(8,128)(2,1)S(1)}, u32[]{:S(2)}, u32[]{:S(2)}) collective-permute-start(bf16[256,128]{1,0:T(8,128)(2,1)S(1)} %get-tuple-element.103), channel_id=1, source_target_pairs={{4,10},{5,9},{6,8},{7,11},{8,6},{9,5},{10,4},{11,7},{20,26},{21,25... | collective-permute-start | bytes 196616 | tf_op jit(solution)/shard_map/ppermute | solution.py:125
  53.7 8.4 %collective-permute-start.23 = (bf16[304,128]{1,0:T(8,128)(2,1)S(1)}, bf16[304,128]{1,0:T(8,128)(2,1)S(1)}, u32[]{:S(2)}, u32[]{:S(2)}) collective-permute-start(bf16[304,128]{1,0:T(8,128)(2,1)S(1)} %get-tuple-element.107.refs_0_), channel_id=1, source_target_pairs={{0,8},{4,12},{8,0},{12,4},{1,9},{5,13},{9,1},{13,5},{2,10},{6,14},... | collective-permute-start | bytes 233480 | tf_op jit(solution)/shard_map/ppermute | solution.py:171
  60.6 6.1 %collective-permute-start.22 = (bf16[512,128]{1,0:T(8,128)(2,1)S(1)}, bf16[512,128]{1,0:T(8,128)(2,1)S(1)}, u32[]{:S(2)}, u32[]{:S(2)}) collective-permute-start(bf16[512,128]{1,0:T(8,128)(2,1)S(1)} %shard_map.233), channel_id=1, source_target_pairs={{0,1},{1,0},{2,3},{3,2},{4,5},{5,4},{6,7},{7,6},{8,9},{9,8},{10,11... | collective-permute-start | bytes 393224 | tf_op jit(solution)/shard_map/ppermute | solution.py:171
  62.2 4.5 %collective-permute-start.24 = (bf16[304,128]{1,0:T(8,128)(2,1)S(1)}, bf16[304,128]{1,0:T(8,128)(2,1)S(1)}, u32[]{:S(2)}, u32[]{:S(2)}) collective-permute-start(bf16[304,128]{1,0:T(8,128)(2,1)S(1)} %shard_map.234.refs_0_), channel_id=1, source_target_pairs={{0,2},{2,0},{1,3},{3,1},{4,6},{6,4},{5,7},{7,5},{8,10},{10,8},{9,1... | collective-permute-start | bytes 233480 | tf_op jit(solution)/shard_map/ppermute | solution.py:171
  66.6 1.4 %collective-permute-start.25 = (bf16[608,128]{1,0:T(8,128)(2,1)S(1)}, bf16[608,128]{1,0:T(8,128)(2,1)S(1)}, u32[]{:S(2)}, u32[]{:S(2)}) collective-permute-start(bf16[608,128]{1,0:T(8,128)(2,1)S(1)} %shard_map.235.refs_0_), channel_id=1, source_target_pairs={{0,1},{1,0},{2,3},{3,2},{4,5},{5,4},{6,7},{7,6},{8,9},{9,8},{10,11... | collective-permute-start | bytes 466952 | tf_op jit(solution)/shard_map/ppermute | solution.py:171
  (11 other events, 17.9 us)

commit v6 on v5

--- a/solution.py
+++ b/solution.py
@@ -135,7 +135,7 @@
     def fetch_theirs(self, got):
         return [swap_axis(value, "inner", 1) for value in got[: self.sub]]
 
-    def give_back(self, mine, own, theirs):
+    def outgoing(self, mine, own, theirs):
         got = swap_axis(theirs, "inner", 1)
         send = self.send
 
@@ -145,13 +145,11 @@
                 out[...] = total[x * send : (x + 1) * send]
 
         rows = [shape(send, mine.shape[1], BF)] * self.sub
-        sums = call(add_kernel, rows, mine, got)
-        arrived = {}
-        order = BACK_ORDER if self.sub == 2 else range(len(self.swaps()))
-        for j in order:
-            value = (*sums, *own)[j]
-            arrived[j] = self.permute(value, *self.swaps()[j])
-        return list(arrived.values())
+        return list(call(add_kernel, rows, mine, got)) + list(own)
+
+    def give(self, values, which):
+        swaps = self.swaps()
+        return [self.permute(values[j], *swaps[j]) for j in which]
 
     def slot_shapes(self, f):
         block = self.sub * self.send
@@ -305,31 +303,31 @@
         for j in range(remote):
             table[pl.ds(j * send, send), :] = halo_refs[j][...]
         folded = fold(table[...])
-        for b in range(blocks):
-            rows = pl.ds(b * size, size)
-            slot = place_ref[b : b + 1, :] - own
-            slot_col = column(slot)
-            far = gather_folded(slot, slot_col, folded)
-            far = (far + far_own_ref[rows, :].astype(F32)).astype(BF)
-            far_ref[rows, :] = far
-            inputs = jnp.concatenate([edge_ref[rows, :], near_ref[rows, :], far], axis=1)
-            act, slope = silu_pair(mm(inputs, entry_ref[...]))
-            h1 = act.astype(BF)
-            h1_ref[rows, :] = h1
+        slots = [place_ref[b : b + 1, :] - own for b in range(blocks)]
+        cols = [column(slot) for slot in slots]
+        parts = [pl.ds(b * size, size) for b in range(blocks)]
+        for slot, col, rows in zip(slots, cols, parts):
+            far = gather_folded(slot, col, folded)
+            far_ref[rows, :] = (far + far_own_ref[rows, :].astype(F32)).astype(BF)
+        for rows in parts:
+            inputs = [edge_ref[rows, :], near_ref[rows, :], far_ref[rows, :]]
+            act, slope = silu_pair(mm(jnp.concatenate(inputs, axis=1), entry_ref[...]))
+            h1_ref[rows, :] = act.astype(BF)
             s1_ref[rows, :] = slope
-            act, slope = silu_pair(mm(h1, middle_ref[...]))
-            h2 = act.astype(BF)
-            h2_ref[rows, :] = h2
+        for rows in parts:
+            act, slope = silu_pair(mm(h1_ref[rows, :], middle_ref[...]))
+            h2_ref[rows, :] = act.astype(BF)
             s2_ref[rows, :] = slope
-            output_pre = mm(h2, outlet_ref[...])
-            out_ref[rows, :] = output_pre
-            normed, _ = layer_norm(output_pre)
+        for rows in parts:
+            out_ref[rows, :] = mm(h2_ref[rows, :], outlet_ref[...])
+        for b, (col, rows) in enumerate(zip(cols, parts)):
+            normed, _ = layer_norm(out_ref[rows, :])
             live = live_column(count_ref, b, size)
             state = edge_ref[rows, :].astype(F32)
             new = (state + live * gain_ref[...] * normed).astype(BF)
             message = new.astype(F32) * live
             message_ref[rows, :] = message.astype(BF)
-            pairs[rows, :] = halves(message, slot_col, half_halo)
+            pairs[rows, :] = halves(message, col, half_halo)
         hot = folded_hot(whole_row(place_ref) - own, half_halo)
         lay.store_slots(unfold(mm(hot, pairs[...])), slot_refs)
 
@@ -345,7 +343,10 @@
         flops=2 * edges * f * (2 * lay.halo + 5 * f),
     )
     message, far_rows, h1, h2, s1, s2, out_pre = edge_outs[:7]
-    received = lay.give_back(edge_outs[7], edge_outs[8:-1], edge_outs[-1])
+    outgoing = lay.outgoing(edge_outs[7], edge_outs[8:-1], edge_outs[-1])
+    near_first = lay.sub // 2
+    other_swaps = [j for j in range(len(outgoing)) if j != near_first]
+    received = lay.give(outgoing, [near_first] + other_swaps)
 
     def local_sums(spot_ref, place_ref, send_ref, near_pairs, far_pairs):
         total = unfold(mm(folded_hot(whole_row(spot_ref), half_near), near_pairs[...]))
@@ -381,7 +382,7 @@
         hot = hot_rows(send_ref[...], nodes)
         total = own_ref[...]
         for ref in refs[:-1]:
-            total += mm(hot, ref[...])
+            total += mm(hot, ref[:send, :])
         refs[-1][...] = total.astype(BF)
 
     def join(part, arrived):
@@ -396,30 +397,40 @@
     def node_kernel(
         part_ref, other_ref, node_ref, cot_ref, send_ref, entry_ref, middle_ref, outlet_ref,
         gain_ref, new_ref, pulls_ref, border_ref, totals_ref, h1_ref, h2_ref, first_ref,
-        second_ref, og_ref, gain_grad_ref,
+        second_ref, og_ref, gain_grad_ref, slope1, slope2,
     ):
-        totals = (part_ref[...].astype(F32) + other_ref[...].astype(F32)).astype(BF)
-        totals_ref[...] = totals
-        state = node_ref[...]
-        act, slope1 = silu_pair(mm(state, entry_ref[:f, :]) + mm(totals, entry_ref[f:, :]))
-        h1n = act.astype(BF)
-        h1_ref[...] = h1n
-        act, slope2 = silu_pair(mm(h1n, middle_ref[...]))
-        h2n = act.astype(BF)
-        h2_ref[...] = h2n
-        normed, inverse = layer_norm(mm(h2n, outlet_ref[...]))
-        new_ref[...] = (state.astype(F32) + gain_ref[...] * normed).astype(BF)
-        up = cot_ref[...].astype(F32)
-        gain_grad_ref[...] = jnp.sum(up * normed, axis=0, keepdims=True)
-        og = norm_backward(up * gain_ref[...], normed, inverse).astype(BF)
-        og_ref[...] = og
-        second = (mm_nt(og, outlet_ref[...]) * slope2).astype(BF)
-        second_ref[...] = second
-        first = (mm_nt(second, middle_ref[...]) * slope1).astype(BF)
-        first_ref[...] = first
-        pulls = mm_nt(first, entry_ref[f:, :]).astype(BF)
-        pulls_ref[...] = pulls
-        border_ref[...] = mm_tn(hot_rows(send_ref[...], nodes), pulls).astype(BF)
+        half_rows = nodes // 2
+        parts = [pl.ds(j * half_rows, half_rows) for j in range(2)]
+        for rows in parts:
+            totals = part_ref[rows, :].astype(F32) + other_ref[rows, :].astype(F32)
+            totals_ref[rows, :] = totals.astype(BF)
+        for rows in parts:
+            inputs = jnp.concatenate([node_ref[rows, :], totals_ref[rows, :]], axis=1)
+            act, slope = silu_pair(mm(inputs, entry_ref[...]))
+            h1_ref[rows, :] = act.astype(BF)
+            slope1[rows, :] = slope
+        for rows in parts:
+            act, slope = silu_pair(mm(h1_ref[rows, :], middle_ref[...]))
+            h2_ref[rows, :] = act.astype(BF)
+            slope2[rows, :] = slope
+        gain_sum = jnp.zeros((1, f), F32)
+        for rows in parts:
+            normed, inverse = layer_norm(mm(h2_ref[rows, :], outlet_ref[...]))
+            new = node_ref[rows, :].astype(F32) + gain_ref[...] * normed
+            new_ref[rows, :] = new.astype(BF)
+            up = cot_ref[rows, :].astype(F32)
+            gain_sum += jnp.sum(up * normed, axis=0, keepdims=True)
+            og_ref[rows, :] = norm_backward(up * gain_ref[...], normed, inverse).astype(BF)
+        gain_grad_ref[...] = gain_sum
+        for rows in parts:
+            grad = mm_nt(og_ref[rows, :], outlet_ref[...])
+            second_ref[rows, :] = (grad * slope2[rows, :]).astype(BF)
+        for rows in parts:
+            grad = mm_nt(second_ref[rows, :], middle_ref[...])
+            first_ref[rows, :] = (grad * slope1[rows, :]).astype(BF)
+        for rows in parts:
+            pulls_ref[rows, :] = mm_nt(first_ref[rows, :], entry_ref[f:, :]).astype(BF)
+        border_ref[...] = mm_tn(hot_rows(send_ref[...], nodes), pulls_ref[...]).astype(BF)
 
     node_outs = call(
         node_kernel,
@@ -432,6 +443,7 @@
         + [shape(1, f, F32)],
         part, part_other, node_state, node_cotangent, sends, node_entry, node_middle,
         node_outlet, gain_n,
+        scratch=[pltpu.VMEM((nodes, f), F32), pltpu.VMEM((nodes, f), F32)],
         flops=2 * nodes * f * f * 8,
     )
     new_rows, pulls, pull_border = node_outs[:3]
@@ -503,21 +515,24 @@
         for j in range(remote):
             table[pl.ds(j * send, send), :] = halo_refs[j][...]
         folded = fold(table[...])
-        gain_sum = jnp.zeros((1, f), F32)
-        for b in range(blocks):
-            rows = pl.ds(b * size, size)
+        parts = [pl.ds(b * size, size) for b in range(blocks)]
+        for b, rows in enumerate(parts):
             live = live_column(count_ref, b, size)
             slot = place_ref[b : b + 1, :] - own
-            up = up_own_ref[rows, :] + live * gather_folded(slot, column(slot), folded)
-            up_ref[rows, :] = up
-            into = live * up
+            got = gather_folded(slot, column(slot), folded)
+            up_ref[rows, :] = up_own_ref[rows, :] + live * got
+        gain_sum = jnp.zeros((1, f), F32)
+        for b, rows in enumerate(parts):
+            into = live_column(count_ref, b, size) * up_ref[rows, :]
             normed, inverse = layer_norm(out_pre_ref[rows, :])
             gain_sum += jnp.sum(into * normed, axis=0, keepdims=True)
-            og = norm_backward(into * gain_ref[...], normed, inverse).astype(BF)
-            output[rows, :] = og
-            second_b = (mm_nt(og, outlet_ref[...]) * s2_ref[rows, :]).astype(BF)
-            second[rows, :] = second_b
-            first_ref[rows, :] = (mm_nt(second_b, middle_ref[...]) * s1_ref[rows, :]).astype(BF)
+            output[rows, :] = norm_backward(into * gain_ref[...], normed, inverse).astype(BF)
+        for rows in parts:
+            grad = mm_nt(output[rows, :], outlet_ref[...])
+            second[rows, :] = (grad * s2_ref[rows, :]).astype(BF)
+        for rows in parts:
+            grad = mm_nt(second[rows, :], middle_ref[...])
+            first_ref[rows, :] = (grad * s1_ref[rows, :]).astype(BF)
         first = first_ref[...]
         acc[:f, :] = mm_tn(edge_ref[...], first).astype(BF)
         acc[f : 2 * f, :] = mm_tn(near_ref[...], first).astype(BF)
@@ -567,12 +582,17 @@
         flops=2 * edges * f * (lay.halo + f),
     )
     far_grad = far_outs[0]
-    back = lay.give_back(far_outs[1], far_outs[2:-1], far_outs[-1])
+    outgoing = lay.outgoing(far_outs[1], far_outs[2:-1], far_outs[-1])
+    back = lay.give(outgoing, other_swaps)
+
+    def kept():
+        swapped = lax.axis_index("inner") & lax.axis_index("dom") & 1
+        return lax.axis_index("sub") ^ swapped
 
     def split_kernel(keep_ref, got_ref, *refs):
         out_refs, acc = refs[:-1], refs[-1]
         acc[...] = (keep_ref[...].astype(F32) + got_ref[...].astype(F32)).astype(BF)
-        t = lax.axis_index("sub")
+        t = kept()
         for x in range(subs):
             out_refs[x][...] = acc[pl.ds(pl.multiple_of((t ^ x) * piece, 16), piece), :]
 
@@ -584,24 +604,33 @@
     )
     arrived = [split[0]] + [swap_axis(split[x], "sub", x) for x in range(1, subs)]
 
-    def add_kernel(*refs):
-        values = [ref[...].astype(F32) for ref in refs[:-1]]
+    def add_values(values):
+        values = [value.astype(F32) for value in values]
         while len(values) > 1:
             values = [values[j] + values[j + 1] for j in range(0, len(values), 2)]
-        refs[-1][...] = values[0].astype(BF)
-
-    def add_all(values, after=()):
-        out = call(add_kernel, [shape(piece, f, BF)], *values, after=after)
-        return out[0], out[1:]
-
-    total, _ = add_all(arrived)
-    stride = 1
+        return values[0].astype(BF)
+
+    def join_pieces(slots_ref, *refs):
+        refs[-1][:send, :] = slots_ref[...]
+        refs[-1][send:, :] = add_values([ref[...] for ref in refs[:-1]])
+
+    (packed,) = call(
+        join_pieces, [shape(send + piece, f, BF)], outgoing[near_first], *arrived
+    )
+    packed_other = lay.permute(packed, 1, (0, 1))
+    back.append(packed_other)
+
+    def add_packed(own_ref, other_ref, out_ref):
+        out_ref[...] = add_values([own_ref[send:, :], other_ref[send:, :]])
+
+    def add_pieces(own_ref, other_ref, out_ref):
+        out_ref[...] = add_values([own_ref[...], other_ref[...]])
+
+    (total,) = call(add_packed, [shape(piece, f, BF)], packed, packed_other)
+    stride = 2
     while stride < doms:
         partner = swap_axis(total, "dom", stride)
-        if stride == 1:
-            total, (far_grad,) = add_all([total, partner], [far_grad])
-        else:
-            total, _ = add_all([total, partner])
+        (total,) = call(add_pieces, [shape(piece, f, BF)], total, partner)
         stride *= 2
     own_pieces = [total] + [swap_axis(total, "sub", x) for x in range(1, subs)]
 
@@ -628,7 +657,7 @@
     )
 
     def order_kernel(*refs):
-        t = lax.axis_index("sub")
+        t = kept()
         for x in range(subs):
             refs[-1][pl.ds(pl.multiple_of((t ^ x) * piece, 16), piece), :] = refs[x][...]
 

time: 69.2 us -> 67.1 us (0.970)
  Pallas kernels: 21.4 us -> 19.5 us
    ppermute x14 -> x13, starting transfers between devices: 12.4 us -> 8.77 us  [swap_axis(): return lax.ppermute(value, axis, [(j, j ^ mask) for j in range(count)])]
    ppermute x12, starting transfers between devices: 19.8 us -> 23.1 us  [permute(): return lax.ppermute(value, AXES, pairs)]
    pallas_call x21, Pallas kernels: 21.4 us -> 19.5 us  [call(): pl.pallas_call(inner, out_shape=list(outs) + [jax.ShapeDtypeStruct(a.shap...]
    ppermute x12, waiting for transfers between devices: 0.09 us -> 1.46 us  [permute(): return lax.ppermute(value, AXES, pairs)]
    ppermute x14 -> x13, waiting for transfers between devices: 11.3 us -> 10 us  [swap_axis(): return lax.ppermute(value, axis, [(j, j ^ mask) for j in range(count)])]
  transfers between devices with their start and end apart: 26 -> 25, of which waited for: 8 -> 7; matrix products, arithmetic and copies ran while one was open for 1% -> 1% of each run, Pallas kernels for 15% -> 15%
where the time goes in v6:
time: 67.1 us; the launch traced here: 66.9 us
  starting transfers between devices  31.9 us (48%)
  Pallas kernels  19.5 us (29%)
  waiting for transfers between devices  11.5 us (17%)
  local copies, waits for them, and re-layouts  1.64 us (2%)
  between operations  1.62 us (2%)
  other arithmetic  0.71 us (1%)
    ppermute x12, starting transfers between devices, permute(): return lax.ppermute(value, AXES, pairs)  23.1 us
    pallas_call x21, Pallas kernels, call(): pl.pallas_call(inner, out_shape=list(outs) + [jax.ShapeDtypeStruct(a.shap...  19.5 us
    ppermute x13, waiting for transfers between devices, swap_axis(): return lax.ppermute(value, axis, [(j, j ^ mask) for j in range(count)])  10 us
    ppermute x13, starting transfers between devices, swap_axis(): return lax.ppermute(value, axis, [(j, j ^ mask) for j in range(count)])  8.77 us
    unnamed x34, local copies, waits for them, and re-layouts  1.64 us
    ppermute x12, waiting for transfers between devices, permute(): return lax.ppermute(value, AXES, pairs)  1.46 us
  transfers between devices with their start and end apart: 25, of which 7 were waited for; matrix products, arithmetic and copies ran while one was open for 1% of the time, Pallas kernels for 15%

profile of v6, /device:TPU:0, one launch (start us, length us, event | category | flops | bytes accessed | tf_op | source)
XLA Modules:
  0.0 66.9 jit_solution(18388057992141810574)
XLA Ops:
  0.6 0.7 %copy-done.9 = s32[256]{0:T(256)S(1)} copy-done((s32[256]{0:T(256)S(1)}, s32[256]{0:T(256)}, u32[]{:S(2)}) %copy-start.9) | copy-done | bytes 1048
  1.3 0.9 %copy-done = bf16[512,128]{1,0:T(8,128)(2,1)S(1)} copy-done((bf16[512,128]{1,0:T(8,128)(2,1)S(1)}, bf16[512,128]{1,0:T(8,128)(2,1)}, u32[]{:S(2)}) %copy-start) | copy-done | bytes 131096
  2.5 3.1 %collective-permute-start.1 = (bf16[256,128]{1,0:T(8,128)(2,1)S(1)}, bf16[256,128]{1,0:T(8,128)(2,1)S(1)}, u32[]{:S(2)}, u32[]{:S(2)}) collective-permute-start(bf16[256,128]{1,0:T(8,128)(2,1)S(1)} %shard_map.217.refs_2_), channel_id=1, source_target_pairs={{0,4},{1,7},{2,6},{3,5},{4,0},{5,3},{6,2},{7,1},{8,12},{9,15},{10,... | collective-permute-start | bytes 196616 | tf_op jit(solution)/shard_map/ppermute | solution.py:125
  5.6 0.7 collective-permute-start
  6.3 1.6 %collective-permute-start.2 = (bf16[256,128]{1,0:T(8,128)(2,1)S(1)}, bf16[256,128]{1,0:T(8,128)(2,1)S(1)}, u32[]{:S(2)}, u32[]{:S(2)}) collective-permute-start(bf16[256,128]{1,0:T(8,128)(2,1)S(1)} %shard_map.217.refs_2_), channel_id=1, source_target_pairs={{0,2},{1,3},{2,0},{3,1},{4,6},{5,7},{6,4},{7,5},{8,10},{9,11},{10,... | collective-permute-start | bytes 196616 | tf_op jit(solution)/shard_map/ppermute | solution.py:125
  7.9 1.5 %shard_map.216 = (bf16[1536,128]{1,0:T(8,128)(2,1)S(1)}, s32[6,256]{1,0:T(8,128)S(1)}, s32[6,256]{1,0:T(8,128)S(1)}, f32[1,128]{1,0:T(1,128)S(1)}) custom-call(s32[1536]{0:T(1024)S(1)} %copy-done.13, s32[1536]{0:T(1024)S(1)} %copy-done.14, s32[6]{0:T(128)S(1)} %copy-done.15, bf16[512,128]{1,0:T(8,128)(2,1)S(1)} %copy-done.1, f32[1,128]{1,0:T(1,128)S(1)} %bitcast.10), custom_call_target="tpu_custom_call" | custom-call | flops 201326592 | bytes 549912 | tf_op jit(solution)/shard_map/pallas_call | solution.py:185
  9.9 1.0 %shard_map.218.refs_3_ = bf16[1536,128]{1,0:T(8,128)(2,1)S(1)} custom-call(s32[6,256]{1,0:T(8,128)S(1)} %get-tuple-element.58.refs_0_.refs_1_, bf16[512,128]{1,0:T(8,128)(2,1)S(1)} %copy-done.1, bf16[256,128]{1,0:T(8,128)(2,1)S(1)} %shard_map.217.refs_2_), custom_call_target="tpu_custom_call" | custom-call | flops 3019898880 | bytes 595968 | tf_op jit(solution)/shard_map/pallas_call | solution.py:185
  11.6 2.9 %shard_map.219 = (bf16[1536,128]{1,0:T(8,128)(2,1)S(1)}, bf16[1536,128]{1,0:T(8,128)(2,1)S(1)}, bf16[1536,128]{1,0:T(8,128)(2,1)S(1)}, bf16[1536,128]{1,0:T(8,12...) custom-call(s32[6,256]{1,0:T(8,128)S(1)} %get-tuple-element.58.refs_, ...), custom_call_target="tpu_custom_call" | custom-call | flops 1258291200 | bytes 6068740 | tf_op jit(solution)/shard_map/pallas_call | solution.py:185
  16.0 4.7 %collective-permute-start.6 = (bf16[256,128]{1,0:T(8,128)(2,1)S(1)}, bf16[256,128]{1,0:T(8,128)(2,1)S(1)}, u32[]{:S(2)}, u32[]{:S(2)}) collective-permute-start(bf16[256,128]{1,0:T(8,128)(2,1)S(1)} %get-tuple-element.65), channel_id=1, source_target_pairs={{0,4},{1,7},{2,6},{3,5},{4,0},{5,3},{6,2},{7,1},{8,12},{9,15},{10,... | collective-permute-start | bytes 196616 | tf_op jit(solution)/shard_map/ppermute | solution.py:125
  21.3 1.7 %shard_map.220 = (bf16[1536,128]{1,0:T(8,128)(2,1)}, f32[512,128]{1,0:T(8,128)S(1)}) custom-call(s32[6,256]{1,0:T(8,128)S(1)} %get-tuple-element.57.refs_0_, s32[6,256]{1,0:T(8,128)S(1)} %get-tuple-element.58.refs_0_.refs_1_, s32[1,256]{1,0:T(1,128)S(1)} %bitcast.4, s32[1]{0:T(128)S(6)} %copy.24.refs_1_.refs_3_, bf16[1536,128]{1,0:T(8,128)(2,1)S(1)} %copy-done.2, ...), custom_call_target="tpu_custom_call" | custom-call | flops 503316480 | bytes 1455108 | tf_op jit(solution)/shard_map/pallas_call | solution.py:185
  24.1 1.0 %collective-permute-done.9.refs_1_ = bf16[512,128]{1,0:T(8,128)(2,1)S(1)} collective-permute-done((bf16[512,128]{1,0:T(8,128)(2,1)S(1)}, bf16[512,128]{1,0:T(8,128)(2,1)S(1)}, u32[]{:S(2)}, u32[]{:S(2)}) %collective-permute-start.9) | collective-permute-done | bytes 131104 | tf_op jit(solution)/shard_map/ppermute | solution.py:169
  25.1 1.4 %shard_map.223 = (bf16[512,128]{1,0:T(8,128)(2,1)S(1)}, bf16[512,128]{1,0:T(8,128)(2,1)S(1)}, bf16[256,128]{1,0:T(8,128)(2,1)S(1)}, bf16[512,128]{1,0:T(8,128)(2...) custom-call(bf16[512,128]{1,0:T(8,128)(2,1)S(1)} %shard_map.222.refs, ...), custom_call_target="tpu_custom_call" | custom-call | flops 134217728 | bytes 1771520 | tf_op jit(solution)/shard_map/pallas_call | solution.py:185
  26.5 4.5 %collective-permute-start.11 = (bf16[256,128]{1,0:T(8,128)(2,1)S(1)}, bf16[256,128]{1,0:T(8,128)(2,1)S(1)}, u32[]{:S(2)}, u32[]{:S(2)}) collective-permute-start(bf16[256,128]{1,0:T(8,128)(2,1)S(1)} %get-tuple-element.79.refs_4_), channel_id=1, source_target_pairs={{0,4},{1,7},{2,6},{3,5},{4,0},{5,3},{6,2},{7,1},{8,12},{9,15},{10,... | collective-permute-start | bytes 196616 | tf_op jit(solution)/shard_map/ppermute | solution.py:125
  31.0 0.8 %collective-permute-start.10 = (bf16[256,128]{1,0:T(8,128)(2,1)S(1)}, bf16[256,128]{1,0:T(8,128)(2,1)S(1)}, u32[]{:S(2)}, u32[]{:S(2)}) collective-permute-start(bf16[256,128]{1,0:T(8,128)(2,1)S(1)} %get-tuple-element.79.refs_4_), channel_id=1, source_target_pairs={{4,10},{5,9},{6,8},{7,11},{8,6},{9,5},{10,4},{11,7},{20,26},{21,25... | collective-permute-start | bytes 196616 | tf_op jit(solution)/shard_map/ppermute | solution.py:125
  31.9 1.3 %collective-permute-start.12 = (bf16[256,128]{1,0:T(8,128)(2,1)S(1)}, bf16[256,128]{1,0:T(8,128)(2,1)S(1)}, u32[]{:S(2)}, u32[]{:S(2)}) collective-permute-start(bf16[256,128]{1,0:T(8,128)(2,1)S(1)} %get-tuple-element.79.refs_4_), channel_id=1, source_target_pairs={{0,2},{1,3},{2,0},{3,1},{4,6},{5,7},{6,4},{7,5},{8,10},{9,11},{10,... | collective-permute-start | bytes 196616 | tf_op jit(solution)/shard_map/ppermute | solution.py:125
  33.2 1.6 %shard_map.224 = (bf16[1536,128]{1,0:T(8,128)(2,1)S(1)}, bf16[512,128]{1,0:T(8,128)(2,1)S(1)}, bf16[512,128]{1,0:T(8,128)(2,1)}) custom-call(s32[6,256]{1,0:T(8,128)S(1)} %get-tuple-element.57.refs_0_, bf16[512,128]{1,0:T(8,128)(2,1)S(1)} %get-tuple-element.68.refs_1_.refs_3_, bf16[512,128]{1,0:T(8,128)(2,1)S(1)} %copy-done.1, ...), custom_call_target="tpu_custom_call" | custom-call | flops 268435456 | bytes 1841152 | tf_op jit(solution)/shard_map/pallas_call | solution.py:185
  35.3 1.1 %shard_map.225 = (f32[1536,128]{1,0:T(8,128)S(1)}, f32[512,128]{1,0:T(8,128)S(1)}) custom-call(s32[6,256]{1,0:T(8,128)S(1)} %get-tuple-element.58.refs_0_.refs_1_, s32[1]{0:T(128)S(6)} %copy.24.refs_1_.refs_3_, bf16[1536,128]{1,0:T(8,128)(2,1)S(1)} %get-tuple-element.78.refs_2_, bf16[512,128]{1,0:T(8,128)(2,1)S(1)} %get-tuple-element.68.refs_1_.refs_3_, ...), custom_call_target="tpu_custom_call" | custom-call | flops 3019898880 | bytes 2365444 | tf_op jit(solution)/shard_map/pallas_call | solution.py:185
  36.5 3.3 %shard_map.226 = (f32[1536,128]{1,0:T(8,128)S(1)}, bf16[1536,128]{1,0:T(8,128)(2,1)S(1)}, bf16[608,128]{1,0:T(8,128)(2,1)S(1)}, bf16[608,128]{1,0:T(8,128)(2,1)S(1)}) custom-call(s32[6,256]{1,0:T(8,128)S(1)} %get-tuple-element.58.refs_0_.refs_1_, s32[1]{0:T(128)S(6)} %copy.24.refs_1_.refs_3_, f32[1536,128]{1,0:T(8,128)S(1)} %get-tuple-element.80.refs_2_, ...), custom_call_target="tpu_custom_call" | custom-call | flops 855638016 | bytes 7134212 | tf_op jit(solution)/shard_map/pallas_call | solution.py:185
  40.0 1.0 %shard_map.227 = (bf16[1536,128]{1,0:T(8,128)(2,1)S(1)}, f32[512,128]{1,0:T(8,128)S(1)}, bf16[256,128]{1,0:T(8,128)(2,1)S(1)}, bf16[512,128]{1,0:T(8,128)(2,1)S(1)}) custom-call(s32[6,256]{1,0:T(8,128)S(1)} %get-tuple-element.58.refs_0_.refs_1_, bf16[1536,128]{1,0:T(8,128)(2,1)S(1)} %get-tuple-element.90.refs_1_.refs_4_, bf16[384,128]{1,0:T(8,128)(2,1)S(1)} %copy-done.12), custom_call_target="tpu_custom_call" | custom-call | flops 553648128 | bytes 1349632 | tf_op jit(solution)/shard_map/pallas_call | solution.py:185
  41.6 1.0 %collective-permute-start.19 = (bf16[304,128]{1,0:T(8,128)(2,1)S(1)}, bf16[304,128]{1,0:T(8,128)(2,1)S(1)}, u32[]{:S(2)}, u32[]{:S(2)}) collective-permute-start(bf16[304,128]{1,0:T(8,128)(2,1)S(1)} %get-tuple-element.101), channel_id=1, source_target_pairs={{0,2},{2,0},{1,3},{3,1},{4,6},{6,4},{5,7},{7,5},{8,10},{10,8},{9,1... | collective-permute-start | bytes 233480 | tf_op jit(solution)/shard_map/ppermute | solution.py:169
  42.6 3.4 %collective-permute-done.19.refs_2_ = bf16[304,128]{1,0:T(8,128)(2,1)S(1)} collective-permute-done((bf16[304,128]{1,0:T(8,128)(2,1)S(1)}, bf16[304,128]{1,0:T(8,128)(2,1)S(1)}, u32[]{:S(2)}, u32[]{:S(2)}) %collective-permute-start.19) | collective-permute-done | bytes 77856 | tf_op jit(solution)/shard_map/ppermute | solution.py:169
  46.1 3.5 %collective-permute-start.20 = (bf16[560,128]{1,0:T(8,128)(2,1)S(1)}, bf16[560,128]{1,0:T(8,128)(2,1)S(1)}, u32[]{:S(2)}, u32[]{:S(2)}) collective-permute-start(bf16[560,128]{1,0:T(8,128)(2,1)S(1)} %shard_map.231.refs_0_), channel_id=1, source_target_pairs={{0,4},{1,7},{2,6},{3,5},{4,0},{5,3},{6,2},{7,1},{8,12},{9,15},{10,... | collective-permute-start | bytes 430088 | tf_op jit(solution)/shard_map/ppermute | solution.py:125
  49.6 1.0 %collective-permute-start.17 = (bf16[256,128]{1,0:T(8,128)(2,1)S(1)}, bf16[256,128]{1,0:T(8,128)(2,1)S(1)}, u32[]{:S(2)}, u32[]{:S(2)}) collective-permute-start(bf16[256,128]{1,0:T(8,128)(2,1)S(1)} %get-tuple-element.96), channel_id=1, source_target_pairs={{0,2},{1,3},{2,0},{3,1},{4,6},{5,7},{6,4},{7,5},{8,10},{9,11},{10,... | collective-permute-start | bytes 196616 | tf_op jit(solution)/shard_map/ppermute | solution.py:125
  50.6 0.7 collective-permute-start.16
  51.3 1.4 %collective-permute-done.20.refs_4_.refs_1_ = bf16[560,128]{1,0:T(8,128)(2,1)S(1)} collective-permute-done((bf16[560,128]{1,0:T(8,128)(2,1)S(1)}, bf16[560,128]{1,0:T(8,128)(2,1)S(1)}, u32[]{:S(2)}, u32[]{:S(2)}) %collective-permute-start.20) | collective-permute-done | bytes 143392 | tf_op jit(solution)/shard_map/ppermute | solution.py:125
  52.7 3.9 %collective-permute-start.22 = (bf16[304,128]{1,0:T(8,128)(2,1)S(1)}, bf16[304,128]{1,0:T(8,128)(2,1)S(1)}, u32[]{:S(2)}, u32[]{:S(2)}) collective-permute-start(bf16[304,128]{1,0:T(8,128)(2,1)S(1)} %shard_map.233.refs_0_), channel_id=1, source_target_pairs={{0,8},{4,12},{8,0},{12,4},{1,9},{5,13},{9,1},{13,5},{2,10},{6,14},... | collective-permute-start | bytes 233480 | tf_op jit(solution)/shard_map/ppermute | solution.py:169
  56.6 1.8 %shard_map.228 = (bf16[1536,128]{1,0:T(8,128)(2,1)}, f32[512,128]{1,0:T(8,128)S(1)}) custom-call(s32[6,256]{1,0:T(8,128)S(1)} %get-tuple-element.57.refs_0_, s32[6,256]{1,0:T(8,128)S(1)} %get-tuple-element.58.refs_0_.refs_1_, s32[1,256]{1,0:T(1,128)S(1)} %bitcast.7, f32[1536,128]{1,0:T(8,128)S(1)} %get-tuple-element.89.refs_3_, ...), custom_call_target="tpu_custom_call" | custom-call | flops 603979776 | bytes 2339840 | tf_op jit(solution)/shard_map/pallas_call | solution.py:185
  58.9 1.1 %collective-permute-done.22.refs_1_ = bf16[304,128]{1,0:T(8,128)(2,1)S(1)} collective-permute-done((bf16[304,128]{1,0:T(8,128)(2,1)S(1)}, bf16[304,128]{1,0:T(8,128)(2,1)S(1)}, u32[]{:S(2)}, u32[]{:S(2)}) %collective-permute-start.22) | collective-permute-done | bytes 77856 | tf_op jit(solution)/shard_map/ppermute | solution.py:169
  60.1 1.2 %collective-permute-start.23 = (bf16[304,128]{1,0:T(8,128)(2,1)S(1)}, bf16[304,128]{1,0:T(8,128)(2,1)S(1)}, u32[]{:S(2)}, u32[]{:S(2)}) collective-permute-start(bf16[304,128]{1,0:T(8,128)(2,1)S(1)} %shard_map.234.refs_0_), channel_id=1, source_target_pairs={{0,2},{2,0},{1,3},{3,1},{4,6},{6,4},{5,7},{7,5},{8,10},{10,8},{9,1... | collective-permute-start | bytes 233480 | tf_op jit(solution)/shard_map/ppermute | solution.py:169
  61.3 3.2 %collective-permute-done.23.refs_1_ = bf16[304,128]{1,0:T(8,128)(2,1)S(1)} collective-permute-done((bf16[304,128]{1,0:T(8,128)(2,1)S(1)}, bf16[304,128]{1,0:T(8,128)(2,1)S(1)}, u32[]{:S(2)}, u32[]{:S(2)}) %collective-permute-start.23) | collective-permute-done | bytes 77856 | tf_op jit(solution)/shard_map/ppermute | solution.py:169
  64.6 0.7 %add_convert_fusion = bf16[512,128]{1,0:T(8,128)(2,1)} fusion(f32[512,128]{1,0:T(8,128)S(1)} %get-tuple-element.102, bf16[512,128]{1,0:T(8,128)(2,1)S(1)} %collective-permute-done.21, bf16[512,128]{1,0:T(8,128)(2,1)S(1)} %shard_map.232), kind=kLoop, calls=%fused_computation | loop fusion | flops 327680 | bytes 655360 | tf_op jit(solution)/shard_map/convert_element_type | solution.py:685
  66.0 0.9 %shard_map.236 = (f32[640,128]{1,0:T(8,128)}, f32[512,128]{1,0:T(8,128)}, f32[2,128]{1,0:T(2,128)}) custom-call(bf16[608,128]{1,0:T(8,128)(2,1)S(1)} %shard_map.235.refs_0_, bf16[608,128]{1,0:T(8,128)(2,1)S(1)} %collective-permute-done.24.refs_1_), custom_call_target="tpu_custom_call" | custom-call | bytes 902144 | tf_op jit(solution)/shard_map/pallas_call | solution.py:185
  (74 shorter events, 6.6 us)
Async XLA Ops:
  2.2 5.6 %copy-start.1 = (bf16[512,128]{1,0:T(8,128)(2,1)S(1)}, bf16[512,128]{1,0:T(8,128)(2,1)}, u32[]{:S(2)}) copy-start(bf16[512,128]{1,0:T(8,128)(2,1)} %refs_2_.8) | copy-start | bytes 393220
  2.2 5.6 %copy-start.13 = (s32[1536]{0:T(1024)S(1)}, s32[1536]{0:T(1024)}, u32[]{:S(2)}) copy-start(s32[1536]{0:T(1024)} %refs_0_.1) | copy-start | bytes 18436
  2.2 5.6 %copy-start.14 = (s32[1536]{0:T(1024)S(1)}, s32[1536]{0:T(1024)}, u32[]{:S(2)}) copy-start(s32[1536]{0:T(1024)} %refs_1_.6) | copy-start | bytes 18436
  2.5 5.3 %copy-start.15 = (s32[6]{0:T(128)S(1)}, s32[6]{0:T(128)}, u32[]{:S(2)}) copy-start(s32[6]{0:T(128)} %refs_2_.5) | copy-start | bytes 76
  2.5 5.3 %copy-start.16 = (f32[128]{0:T(128)S(1)}, f32[128]{0:T(128)}, u32[]{:S(2)}) copy-start(f32[128]{0:T(128)} %param.27) | copy-start | bytes 1540
  2.5 6.8 %collective-permute-start.1 = (bf16[256,128]{1,0:T(8,128)(2,1)S(1)}, bf16[256,128]{1,0:T(8,128)(2,1)S(1)}, u32[]{:S(2)}, u32[]{:S(2)}) collective-permute-start(bf16[256,128]{1,0:T(8,128)(2,1)S(1)} %shard_map.217.refs_2_), channel_id=1, source_target_pairs={{0,4},{1,7},{2,6},{3,5},{4,0},{5,3},{6,2},{7,1},{8,12},{9,15},{10,... | collective-permute-start | bytes 196616 | tf_op jit(solution)/shard_map/ppermute | solution.py:125
  5.6 3.8 %collective-permute-start = (bf16[256,128]{1,0:T(8,128)(2,1)S(1)}, bf16[256,128]{1,0:T(8,128)(2,1)S(1)}, u32[]{:S(2)}, u32[]{:S(2)}) collective-permute-start(bf16[256,128]{1,0:T(8,128)(2,1)S(1)} %shard_map.217.refs_2_), channel_id=1, source_target_pairs={{4,10},{5,9},{6,8},{7,11},{8,6},{9,5},{10,4},{11,7},{20,26},{21,25... | collective-permute-start | bytes 196616 | tf_op jit(solution)/shard_map/ppermute | solution.py:125
  6.3 5.3 %collective-permute-start.2 = (bf16[256,128]{1,0:T(8,128)(2,1)S(1)}, bf16[256,128]{1,0:T(8,128)(2,1)S(1)}, u32[]{:S(2)}, u32[]{:S(2)}) collective-permute-start(bf16[256,128]{1,0:T(8,128)(2,1)S(1)} %shard_map.217.refs_2_), channel_id=1, source_target_pairs={{0,2},{1,3},{2,0},{3,1},{4,6},{5,7},{6,4},{7,5},{8,10},{9,11},{10,... | collective-permute-start | bytes 196616 | tf_op jit(solution)/shard_map/ppermute | solution.py:125
  9.3 2.2 %collective-permute-start.4 = (bf16[256,128]{1,0:T(8,128)(2,1)S(1)}, bf16[256,128]{1,0:T(8,128)(2,1)S(1)}, u32[]{:S(2)}, u32[]{:S(2)}) collective-permute-start(bf16[256,128]{1,0:T(8,128)(2,1)S(1)} %collective-permute-done.1.refs_10_), channel_id=1, source_target_pairs={{0,1},{1,0},{2,3},{3,2},{4,5},{5,4},{6,7},{7,6},{8,9},{9,8},{10,11... | collective-permute-start | bytes 196616 | tf_op jit(solution)/shard_map/ppermute | solution.py:169
  9.4 2.1 %collective-permute-start.3 = (bf16[256,128]{1,0:T(8,128)(2,1)S(1)}, bf16[256,128]{1,0:T(8,128)(2,1)S(1)}, u32[]{:S(2)}, u32[]{:S(2)}) collective-permute-start(bf16[256,128]{1,0:T(8,128)(2,1)S(1)} %collective-permute-done.refs_9_), channel_id=1, source_target_pairs={{0,1},{1,0},{2,3},{3,2},{4,5},{5,4},{6,7},{7,6},{8,9},{9,8},{10,11... | collective-permute-start | bytes 196616 | tf_op jit(solution)/shard_map/ppermute | solution.py:169
  14.5 1.4 %collective-permute-start.5 = (bf16[512,128]{1,0:T(8,128)(2,1)S(1)}, bf16[512,128]{1,0:T(8,128)(2,1)S(1)}, u32[]{:S(2)}, u32[]{:S(2)}) collective-permute-start(bf16[512,128]{1,0:T(8,128)(2,1)S(1)} %get-tuple-element.64), channel_id=1, source_target_pairs={{0,1},{1,0},{2,3},{3,2},{4,5},{5,4},{6,7},{7,6},{8,9},{9,8},{10,11... | collective-permute-start | bytes 393224 | tf_op jit(solution)/shard_map/ppermute | solution.py:169
  14.7 8.3 %collective-permute-start.8 = (bf16[256,128]{1,0:T(8,128)(2,1)S(1)}, bf16[256,128]{1,0:T(8,128)(2,1)S(1)}, u32[]{:S(2)}, u32[]{:S(2)}) collective-permute-start(bf16[256,128]{1,0:T(8,128)(2,1)S(1)} %get-tuple-element.67), channel_id=1, source_target_pairs={{0,2},{1,3},{2,0},{3,1},{4,6},{5,7},{6,4},{7,5},{8,10},{9,11},{10,... | collective-permute-start | bytes 196616 | tf_op jit(solution)/shard_map/ppermute | solution.py:125
  16.0 7.1 %collective-permute-start.6 = (bf16[256,128]{1,0:T(8,128)(2,1)S(1)}, bf16[256,128]{1,0:T(8,128)(2,1)S(1)}, u32[]{:S(2)}, u32[]{:S(2)}) collective-permute-start(bf16[256,128]{1,0:T(8,128)(2,1)S(1)} %get-tuple-element.65), channel_id=1, source_target_pairs={{0,4},{1,7},{2,6},{3,5},{4,0},{5,3},{6,2},{7,1},{8,12},{9,15},{10,... | collective-permute-start | bytes 196616 | tf_op jit(solution)/shard_map/ppermute | solution.py:125
  20.6 2.4 %collective-permute-start.7 = (bf16[256,128]{1,0:T(8,128)(2,1)S(1)}, bf16[256,128]{1,0:T(8,128)(2,1)S(1)}, u32[]{:S(2)}, u32[]{:S(2)}) collective-permute-start(bf16[256,128]{1,0:T(8,128)(2,1)S(1)} %get-tuple-element.66), channel_id=1, source_target_pairs={{4,10},{5,9},{6,8},{7,11},{8,6},{9,5},{10,4},{11,7},{20,26},{21,25... | collective-permute-start | bytes 196616 | tf_op jit(solution)/shard_map/ppermute | solution.py:125
  23.0 2.0 %copy-start.7 = (bf16[128,128]{1,0:T(8,128)(2,1)S(1)}, bf16[128,128]{1,0:T(8,128)(2,1)}, u32[]{:S(2)}) copy-start(bf16[128,128]{1,0:T(8,128)(2,1)} %refs_6_.4) | copy-start | bytes 98308
  23.5 1.6 %collective-permute-start.9 = (bf16[512,128]{1,0:T(8,128)(2,1)S(1)}, bf16[512,128]{1,0:T(8,128)(2,1)S(1)}, u32[]{:S(2)}, u32[]{:S(2)}) collective-permute-start(bf16[512,128]{1,0:T(8,128)(2,1)S(1)} %shard_map.222.refs_0_), channel_id=1, source_target_pairs={{0,1},{1,0},{2,3},{3,2},{4,5},{5,4},{6,7},{7,6},{8,9},{9,8},{10,11... | collective-permute-start | bytes 393224 | tf_op jit(solution)/shard_map/ppermute | solution.py:169
  26.5 8.3 %collective-permute-start.11 = (bf16[256,128]{1,0:T(8,128)(2,1)S(1)}, bf16[256,128]{1,0:T(8,128)(2,1)S(1)}, u32[]{:S(2)}, u32[]{:S(2)}) collective-permute-start(bf16[256,128]{1,0:T(8,128)(2,1)S(1)} %get-tuple-element.79.refs_4_), channel_id=1, source_target_pairs={{0,4},{1,7},{2,6},{3,5},{4,0},{5,3},{6,2},{7,1},{8,12},{9,15},{10,... | collective-permute-start | bytes 196616 | tf_op jit(solution)/shard_map/ppermute | solution.py:125
  31.0 3.8 %collective-permute-start.10 = (bf16[256,128]{1,0:T(8,128)(2,1)S(1)}, bf16[256,128]{1,0:T(8,128)(2,1)S(1)}, u32[]{:S(2)}, u32[]{:S(2)}) collective-permute-start(bf16[256,128]{1,0:T(8,128)(2,1)S(1)} %get-tuple-element.79.refs_4_), channel_id=1, source_target_pairs={{4,10},{5,9},{6,8},{7,11},{8,6},{9,5},{10,4},{11,7},{20,26},{21,25... | collective-permute-start | bytes 196616 | tf_op jit(solution)/shard_map/ppermute | solution.py:125
  31.9 4.6 %collective-permute-start.12 = (bf16[256,128]{1,0:T(8,128)(2,1)S(1)}, bf16[256,128]{1,0:T(8,128)(2,1)S(1)}, u32[]{:S(2)}, u32[]{:S(2)}) collective-permute-start(bf16[256,128]{1,0:T(8,128)(2,1)S(1)} %get-tuple-element.79.refs_4_), channel_id=1, source_target_pairs={{0,2},{1,3},{2,0},{3,1},{4,6},{5,7},{6,4},{7,5},{8,10},{9,11},{10,... | collective-permute-start | bytes 196616 | tf_op jit(solution)/shard_map/ppermute | solution.py:125
  33.2 2.2 %copy-start.11 = (bf16[1536,128]{1,0:T(8,128)(2,1)S(1)}, bf16[1536,128]{1,0:T(8,128)(2,1)}, u32[]{:S(2)}) copy-start(bf16[1536,128]{1,0:T(8,128)(2,1)} %refs_5_.5) | copy-start | bytes 1179652
  34.8 1.7 %collective-permute-start.14 = (bf16[256,128]{1,0:T(8,128)(2,1)S(1)}, bf16[256,128]{1,0:T(8,128)(2,1)S(1)}, u32[]{:S(2)}, u32[]{:S(2)}) collective-permute-start(bf16[256,128]{1,0:T(8,128)(2,1)S(1)} %collective-permute-done.11.refs_17_), channel_id=1, source_target_pairs={{0,1},{1,0},{2,3},{3,2},{4,5},{5,4},{6,7},{7,6},{8,9},{9,8},{10,11... | collective-permute-start | bytes 196616 | tf_op jit(solution)/shard_map/ppermute | solution.py:169
  34.8 1.7 %collective-permute-start.13 = (bf16[256,128]{1,0:T(8,128)(2,1)S(1)}, bf16[256,128]{1,0:T(8,128)(2,1)S(1)}, u32[]{:S(2)}, u32[]{:S(2)}) collective-permute-start(bf16[256,128]{1,0:T(8,128)(2,1)S(1)} %collective-permute-done.10.refs_16_), channel_id=1, source_target_pairs={{0,1},{1,0},{2,3},{3,2},{4,5},{5,4},{6,7},{7,6},{8,9},{9,8},{10,11... | collective-permute-start | bytes 196616 | tf_op jit(solution)/shard_map/ppermute | solution.py:169
  39.8 1.7 %collective-permute-start.18 = (bf16[608,128]{1,0:T(8,128)(2,1)S(1)}, bf16[608,128]{1,0:T(8,128)(2,1)S(1)}, u32[]{:S(2)}, u32[]{:S(2)}) collective-permute-start(bf16[608,128]{1,0:T(8,128)(2,1)S(1)} %get-tuple-element.99), channel_id=1, source_target_pairs={{0,1},{1,0},{2,3},{3,2},{4,5},{5,4},{6,7},{7,6},{8,9},{9,8},{10,11... | collective-permute-start | bytes 466952 | tf_op jit(solution)/shard_map/ppermute | solution.py:169
  41.0 1.6 %collective-permute-start.15 = (bf16[512,128]{1,0:T(8,128)(2,1)S(1)}, bf16[512,128]{1,0:T(8,128)(2,1)S(1)}, u32[]{:S(2)}, u32[]{:S(2)}) collective-permute-start(bf16[512,128]{1,0:T(8,128)(2,1)S(1)} %get-tuple-element.94), channel_id=1, source_target_pairs={{0,1},{1,0},{2,3},{3,2},{4,5},{5,4},{6,7},{7,6},{8,9},{9,8},{10,11... | collective-permute-start | bytes 393224 | tf_op jit(solution)/shard_map/ppermute | solution.py:169
  41.6 4.5 %collective-permute-start.19 = (bf16[304,128]{1,0:T(8,128)(2,1)S(1)}, bf16[304,128]{1,0:T(8,128)(2,1)S(1)}, u32[]{:S(2)}, u32[]{:S(2)}) collective-permute-start(bf16[304,128]{1,0:T(8,128)(2,1)S(1)} %get-tuple-element.101), channel_id=1, source_target_pairs={{0,2},{2,0},{1,3},{3,1},{4,6},{6,4},{5,7},{7,5},{8,10},{10,8},{9,1... | collective-permute-start | bytes 233480 | tf_op jit(solution)/shard_map/ppermute | solution.py:169
  46.1 6.6 %collective-permute-start.20 = (bf16[560,128]{1,0:T(8,128)(2,1)S(1)}, bf16[560,128]{1,0:T(8,128)(2,1)S(1)}, u32[]{:S(2)}, u32[]{:S(2)}) collective-permute-start(bf16[560,128]{1,0:T(8,128)(2,1)S(1)} %shard_map.231.refs_0_), channel_id=1, source_target_pairs={{0,4},{1,7},{2,6},{3,5},{4,0},{5,3},{6,2},{7,1},{8,12},{9,15},{10,... | collective-permute-start | bytes 430088 | tf_op jit(solution)/shard_map/ppermute | solution.py:125
  49.6 8.9 %collective-permute-start.17 = (bf16[256,128]{1,0:T(8,128)(2,1)S(1)}, bf16[256,128]{1,0:T(8,128)(2,1)S(1)}, u32[]{:S(2)}, u32[]{:S(2)}) collective-permute-start(bf16[256,128]{1,0:T(8,128)(2,1)S(1)} %get-tuple-element.96), channel_id=1, source_target_pairs={{0,2},{1,3},{2,0},{3,1},{4,6},{5,7},{6,4},{7,5},{8,10},{9,11},{10,... | collective-permute-start | bytes 196616 | tf_op jit(solution)/shard_map/ppermute | solution.py:125
  50.6 7.8 %collective-permute-start.16 = (bf16[256,128]{1,0:T(8,128)(2,1)S(1)}, bf16[256,128]{1,0:T(8,128)(2,1)S(1)}, u32[]{:S(2)}, u32[]{:S(2)}) collective-permute-start(bf16[256,128]{1,0:T(8,128)(2,1)S(1)} %get-tuple-element.95), channel_id=1, source_target_pairs={{4,10},{5,9},{6,8},{7,11},{8,6},{9,5},{10,4},{11,7},{20,26},{21,25... | collective-permute-start | bytes 196616 | tf_op jit(solution)/shard_map/ppermute | solution.py:125
  52.7 7.4 %collective-permute-start.22 = (bf16[304,128]{1,0:T(8,128)(2,1)S(1)}, bf16[304,128]{1,0:T(8,128)(2,1)S(1)}, u32[]{:S(2)}, u32[]{:S(2)}) collective-permute-start(bf16[304,128]{1,0:T(8,128)(2,1)S(1)} %shard_map.233.refs_0_), channel_id=1, source_target_pairs={{0,8},{4,12},{8,0},{12,4},{1,9},{5,13},{9,1},{13,5},{2,10},{6,14},... | collective-permute-start | bytes 233480 | tf_op jit(solution)/shard_map/ppermute | solution.py:169
  58.8 5.8 %collective-permute-start.21 = (bf16[512,128]{1,0:T(8,128)(2,1)S(1)}, bf16[512,128]{1,0:T(8,128)(2,1)S(1)}, u32[]{:S(2)}, u32[]{:S(2)}) collective-permute-start(bf16[512,128]{1,0:T(8,128)(2,1)S(1)} %shard_map.232), channel_id=1, source_target_pairs={{0,1},{1,0},{2,3},{3,2},{4,5},{5,4},{6,7},{7,6},{8,9},{9,8},{10,11... | collective-permute-start | bytes 393224 | tf_op jit(solution)/shard_map/ppermute | solution.py:169
  60.1 4.5 %collective-permute-start.23 = (bf16[304,128]{1,0:T(8,128)(2,1)S(1)}, bf16[304,128]{1,0:T(8,128)(2,1)S(1)}, u32[]{:S(2)}, u32[]{:S(2)}) collective-permute-start(bf16[304,128]{1,0:T(8,128)(2,1)S(1)} %shard_map.234.refs_0_), channel_id=1, source_target_pairs={{0,2},{2,0},{1,3},{3,1},{4,6},{6,4},{5,7},{7,5},{8,10},{10,8},{9,1... | collective-permute-start | bytes 233480 | tf_op jit(solution)/shard_map/ppermute | solution.py:169
  64.5 1.4 %collective-permute-start.24 = (bf16[608,128]{1,0:T(8,128)(2,1)S(1)}, bf16[608,128]{1,0:T(8,128)(2,1)S(1)}, u32[]{:S(2)}, u32[]{:S(2)}) collective-permute-start(bf16[608,128]{1,0:T(8,128)(2,1)S(1)} %shard_map.235.refs_0_), channel_id=1, source_target_pairs={{0,1},{1,0},{2,3},{3,2},{4,5},{5,4},{6,7},{7,6},{8,9},{9,8},{10,11... | collective-permute-start | bytes 466952 | tf_op jit(solution)/shard_map/ppermute | solution.py:169
  (10 other events, 15.9 us)

commit v7 on v6

--- a/solution.py
+++ b/solution.py
@@ -198,7 +198,11 @@
     return jax.ShapeDtypeStruct((rows, cols), dtype)
 
 
-def border_kernel(send_ref, table_ref, out_ref):
+def first_kernel(out_ref):
+    out_ref[...] = jnp.zeros(out_ref.shape, F32)
+
+
+def border_kernel(send_ref, table_ref, first_ref, out_ref):
     hot = hot_rows(send_ref[...], table_ref.shape[0])
     out_ref[...] = mm_tn(hot, table_ref[...]).astype(BF)
 
@@ -247,7 +251,8 @@
     gain_e = edge_gain.reshape(1, f)
     gain_n = node_gain.reshape(1, f)
 
-    (border,) = call(border_kernel, [shape(send, f, BF)], sends, node_state)
+    (first,) = call(first_kernel, [shape(8, f, F32)])
+    (border,) = call(border_kernel, [shape(send, f, BF)], sends, node_state, first)
     halo = lay.fetch(border)
 
     def edge_near(
@@ -399,8 +404,8 @@
         gain_ref, new_ref, pulls_ref, border_ref, totals_ref, h1_ref, h2_ref, first_ref,
         second_ref, og_ref, gain_grad_ref, slope1, slope2,
     ):
-        half_rows = nodes // 2
-        parts = [pl.ds(j * half_rows, half_rows) for j in range(2)]
+        part_rows = nodes // 4
+        parts = [pl.ds(j * part_rows, part_rows) for j in range(4)]
         for rows in parts:
             totals = part_ref[rows, :].astype(F32) + other_ref[rows, :].astype(F32)
             totals_ref[rows, :] = totals.astype(BF)
@@ -534,9 +539,8 @@
             grad = mm_nt(second[rows, :], middle_ref[...])
             first_ref[rows, :] = (grad * s1_ref[rows, :]).astype(BF)
         first = first_ref[...]
-        acc[:f, :] = mm_tn(edge_ref[...], first).astype(BF)
-        acc[f : 2 * f, :] = mm_tn(near_ref[...], first).astype(BF)
-        acc[2 * f : 3 * f, :] = mm_tn(far_ref[...], first).astype(BF)
+        inputs = jnp.concatenate([edge_ref[...], near_ref[...], far_ref[...]], axis=1)
+        acc[: 3 * f, :] = mm_tn(inputs, first).astype(BF)
         acc[3 * f : 4 * f, :] = mm_tn(h1_ref[...], second[...]).astype(BF)
         acc[4 * f : 5 * f, :] = mm_tn(h2_ref[...], output[...]).astype(BF)
         acc[5 * f : 9 * f, :] = node_ref[...]

time: 67.1 us -> 66.3 us (0.988)
  waiting for transfers between devices: 11.5 us -> 9.87 us
  starting transfers between devices: 31.9 us -> 32.8 us
    ppermute x13, waiting for transfers between devices: 10 us -> 8.43 us  [swap_axis(): return lax.ppermute(value, axis, [(j, j ^ mask) for j in range(count)])]
    ppermute x13, starting transfers between devices: 8.77 us -> 9.61 us  [swap_axis(): return lax.ppermute(value, axis, [(j, j ^ mask) for j in range(count)])]
    pallas_call x21 -> x22, Pallas kernels: 19.5 us -> 19.4 us  [call(): pl.pallas_call(inner, out_shape=list(outs) + [jax.ShapeDtypeStruct(a.shap...]
  transfers between devices with their start and end apart: 25 -> 25, of which waited for: 7 -> 7; matrix products, arithmetic and copies ran while one was open for 1% -> 1% of each run, Pallas kernels for 15% -> 16%
where the time goes in v7:
time: 66.3 us; the launch traced here: 66.1 us
  starting transfers between devices  32.8 us (49%)
  Pallas kernels  19.4 us (29%)
  waiting for transfers between devices  9.87 us (15%)
  local copies, waits for them, and re-layouts  1.64 us (2%)
  between operations  1.63 us (2%)
  other arithmetic  0.71 us (1%)
    ppermute x12, starting transfers between devices, permute(): return lax.ppermute(value, AXES, pairs)  23.1 us
    pallas_call x22, Pallas kernels, call(): pl.pallas_call(inner, out_shape=list(outs) + [jax.ShapeDtypeStruct(a.shap...  19.4 us
    ppermute x13, starting transfers between devices, swap_axis(): return lax.ppermute(value, axis, [(j, j ^ mask) for j in range(count)])  9.61 us
    ppermute x13, waiting for transfers between devices, swap_axis(): return lax.ppermute(value, axis, [(j, j ^ mask) for j in range(count)])  8.43 us
    unnamed x34, local copies, waits for them, and re-layouts  1.64 us
    ppermute x12, waiting for transfers between devices, permute(): return lax.ppermute(value, AXES, pairs)  1.44 us
  transfers between devices with their start and end apart: 25, of which 7 were waited for; matrix products, arithmetic and copies ran while one was open for 1% of the time, Pallas kernels for 16%

profile of v7, /device:TPU:0, one launch (start us, length us, event | category | flops | bytes accessed | tf_op | source)
XLA Modules:
  0.0 66.1 jit_solution(15078532116491210938)
XLA Ops:
  0.7 0.7 %copy-done.9 = s32[256]{0:T(256)S(1)} copy-done((s32[256]{0:T(256)S(1)}, s32[256]{0:T(256)}, u32[]{:S(2)}) %copy-start.9) | copy-done | bytes 1048
  1.3 0.9 %copy-done = bf16[512,128]{1,0:T(8,128)(2,1)S(1)} copy-done((bf16[512,128]{1,0:T(8,128)(2,1)S(1)}, bf16[512,128]{1,0:T(8,128)(2,1)}, u32[]{:S(2)}) %copy-start) | copy-done | bytes 131096
  2.5 3.1 %collective-permute-start.1 = (bf16[256,128]{1,0:T(8,128)(2,1)S(1)}, bf16[256,128]{1,0:T(8,128)(2,1)S(1)}, u32[]{:S(2)}, u32[]{:S(2)}) collective-permute-start(bf16[256,128]{1,0:T(8,128)(2,1)S(1)} %shard_map.218.refs_2_), channel_id=1, source_target_pairs={{0,4},{1,7},{2,6},{3,5},{4,0},{5,3},{6,2},{7,1},{8,12},{9,15},{10,... | collective-permute-start | bytes 196616 | tf_op jit(solution)/shard_map/ppermute | solution.py:125
  5.6 0.7 collective-permute-start
  6.3 1.6 %collective-permute-start.2 = (bf16[256,128]{1,0:T(8,128)(2,1)S(1)}, bf16[256,128]{1,0:T(8,128)(2,1)S(1)}, u32[]{:S(2)}, u32[]{:S(2)}) collective-permute-start(bf16[256,128]{1,0:T(8,128)(2,1)S(1)} %shard_map.218.refs_2_), channel_id=1, source_target_pairs={{0,2},{1,3},{2,0},{3,1},{4,6},{5,7},{6,4},{7,5},{8,10},{9,11},{10,... | collective-permute-start | bytes 196616 | tf_op jit(solution)/shard_map/ppermute | solution.py:125
  7.9 1.5 %shard_map.216 = (bf16[1536,128]{1,0:T(8,128)(2,1)S(1)}, s32[6,256]{1,0:T(8,128)S(1)}, s32[6,256]{1,0:T(8,128)S(1)}, f32[1,128]{1,0:T(1,128)S(1)}) custom-call(s32[1536]{0:T(1024)S(1)} %copy-done.13, s32[1536]{0:T(1024)S(1)} %copy-done.14, s32[6]{0:T(128)S(1)} %copy-done.15, bf16[512,128]{1,0:T(8,128)(2,1)S(1)} %copy-done.1, f32[1,128]{1,0:T(1,128)S(1)} %bitcast.10), custom_call_target="tpu_custom_call" | custom-call | flops 201326592 | bytes 549912 | tf_op jit(solution)/shard_map/pallas_call | solution.py:185
  9.9 1.0 %shard_map.219.refs_3_ = bf16[1536,128]{1,0:T(8,128)(2,1)S(1)} custom-call(s32[6,256]{1,0:T(8,128)S(1)} %get-tuple-element.58.refs_0_.refs_1_, bf16[512,128]{1,0:T(8,128)(2,1)S(1)} %copy-done.1, bf16[256,128]{1,0:T(8,128)(2,1)S(1)} %shard_map.218.refs_2_), custom_call_target="tpu_custom_call" | custom-call | flops 3019898880 | bytes 595968 | tf_op jit(solution)/shard_map/pallas_call | solution.py:185
  11.6 2.9 %shard_map.220 = (bf16[1536,128]{1,0:T(8,128)(2,1)S(1)}, bf16[1536,128]{1,0:T(8,128)(2,1)S(1)}, bf16[1536,128]{1,0:T(8,128)(2,1)S(1)}, bf16[1536,128]{1,0:T(8,12...) custom-call(s32[6,256]{1,0:T(8,128)S(1)} %get-tuple-element.58.refs_, ...), custom_call_target="tpu_custom_call" | custom-call | flops 1258291200 | bytes 6068740 | tf_op jit(solution)/shard_map/pallas_call | solution.py:185
  16.0 4.7 %collective-permute-start.6 = (bf16[256,128]{1,0:T(8,128)(2,1)S(1)}, bf16[256,128]{1,0:T(8,128)(2,1)S(1)}, u32[]{:S(2)}, u32[]{:S(2)}) collective-permute-start(bf16[256,128]{1,0:T(8,128)(2,1)S(1)} %get-tuple-element.65), channel_id=1, source_target_pairs={{0,4},{1,7},{2,6},{3,5},{4,0},{5,3},{6,2},{7,1},{8,12},{9,15},{10,... | collective-permute-start | bytes 196616 | tf_op jit(solution)/shard_map/ppermute | solution.py:125
  20.6 0.7 collective-permute-start.7
  21.3 1.7 %shard_map.221 = (bf16[1536,128]{1,0:T(8,128)(2,1)}, f32[512,128]{1,0:T(8,128)S(1)}) custom-call(s32[6,256]{1,0:T(8,128)S(1)} %get-tuple-element.57.refs_0_, s32[6,256]{1,0:T(8,128)S(1)} %get-tuple-element.58.refs_0_.refs_1_, s32[1,256]{1,0:T(1,128)S(1)} %bitcast.4, s32[1]{0:T(128)S(6)} %copy.24.refs_1_.refs_3_, bf16[1536,128]{1,0:T(8,128)(2,1)S(1)} %copy-done.2, ...), custom_call_target="tpu_custom_call" | custom-call | flops 503316480 | bytes 1455108 | tf_op jit(solution)/shard_map/pallas_call | solution.py:185
  24.1 1.0 %collective-permute-done.9.refs_1_ = bf16[512,128]{1,0:T(8,128)(2,1)S(1)} collective-permute-done((bf16[512,128]{1,0:T(8,128)(2,1)S(1)}, bf16[512,128]{1,0:T(8,128)(2,1)S(1)}, u32[]{:S(2)}, u32[]{:S(2)}) %collective-permute-start.9) | collective-permute-done | bytes 131104 | tf_op jit(solution)/shard_map/ppermute | solution.py:169
  25.1 1.4 %shard_map.224 = (bf16[512,128]{1,0:T(8,128)(2,1)S(1)}, bf16[512,128]{1,0:T(8,128)(2,1)S(1)}, bf16[256,128]{1,0:T(8,128)(2,1)S(1)}, bf16[512,128]{1,0:T(8,128)(2...) custom-call(bf16[512,128]{1,0:T(8,128)(2,1)S(1)} %shard_map.223.refs, ...), custom_call_target="tpu_custom_call" | custom-call | flops 134217728 | bytes 1771520 | tf_op jit(solution)/shard_map/pallas_call | solution.py:185
  26.5 4.5 %collective-permute-start.11 = (bf16[256,128]{1,0:T(8,128)(2,1)S(1)}, bf16[256,128]{1,0:T(8,128)(2,1)S(1)}, u32[]{:S(2)}, u32[]{:S(2)}) collective-permute-start(bf16[256,128]{1,0:T(8,128)(2,1)S(1)} %get-tuple-element.79.refs_4_), channel_id=1, source_target_pairs={{0,4},{1,7},{2,6},{3,5},{4,0},{5,3},{6,2},{7,1},{8,12},{9,15},{10,... | collective-permute-start | bytes 196616 | tf_op jit(solution)/shard_map/ppermute | solution.py:125
  31.0 0.8 %collective-permute-start.10 = (bf16[256,128]{1,0:T(8,128)(2,1)S(1)}, bf16[256,128]{1,0:T(8,128)(2,1)S(1)}, u32[]{:S(2)}, u32[]{:S(2)}) collective-permute-start(bf16[256,128]{1,0:T(8,128)(2,1)S(1)} %get-tuple-element.79.refs_4_), channel_id=1, source_target_pairs={{4,10},{5,9},{6,8},{7,11},{8,6},{9,5},{10,4},{11,7},{20,26},{21,25... | collective-permute-start | bytes 196616 | tf_op jit(solution)/shard_map/ppermute | solution.py:125
  31.9 1.3 %collective-permute-start.12 = (bf16[256,128]{1,0:T(8,128)(2,1)S(1)}, bf16[256,128]{1,0:T(8,128)(2,1)S(1)}, u32[]{:S(2)}, u32[]{:S(2)}) collective-permute-start(bf16[256,128]{1,0:T(8,128)(2,1)S(1)} %get-tuple-element.79.refs_4_), channel_id=1, source_target_pairs={{0,2},{1,3},{2,0},{3,1},{4,6},{5,7},{6,4},{7,5},{8,10},{9,11},{10,... | collective-permute-start | bytes 196616 | tf_op jit(solution)/shard_map/ppermute | solution.py:125
  33.2 1.6 %shard_map.225 = (bf16[1536,128]{1,0:T(8,128)(2,1)S(1)}, bf16[512,128]{1,0:T(8,128)(2,1)S(1)}, bf16[512,128]{1,0:T(8,128)(2,1)}) custom-call(s32[6,256]{1,0:T(8,128)S(1)} %get-tuple-element.57.refs_0_, bf16[512,128]{1,0:T(8,128)(2,1)S(1)} %get-tuple-element.68.refs_1_.refs_3_, bf16[512,128]{1,0:T(8,128)(2,1)S(1)} %copy-done.1, ...), custom_call_target="tpu_custom_call" | custom-call | flops 268435456 | bytes 1841152 | tf_op jit(solution)/shard_map/pallas_call | solution.py:185
  35.4 1.1 %shard_map.226 = (f32[1536,128]{1,0:T(8,128)S(1)}, f32[512,128]{1,0:T(8,128)S(1)}) custom-call(s32[6,256]{1,0:T(8,128)S(1)} %get-tuple-element.58.refs_0_.refs_1_, s32[1]{0:T(128)S(6)} %copy.24.refs_1_.refs_3_, bf16[1536,128]{1,0:T(8,128)(2,1)S(1)} %get-tuple-element.78.refs_2_, bf16[512,128]{1,0:T(8,128)(2,1)S(1)} %get-tuple-element.68.refs_1_.refs_3_, ...), custom_call_target="tpu_custom_call" | custom-call | flops 3019898880 | bytes 2365444 | tf_op jit(solution)/shard_map/pallas_call | solution.py:185
  36.5 3.3 %shard_map.227 = (f32[1536,128]{1,0:T(8,128)S(1)}, bf16[1536,128]{1,0:T(8,128)(2,1)S(1)}, bf16[608,128]{1,0:T(8,128)(2,1)S(1)}, bf16[608,128]{1,0:T(8,128)(2,1)S(1)}) custom-call(s32[6,256]{1,0:T(8,128)S(1)} %get-tuple-element.58.refs_0_.refs_1_, s32[1]{0:T(128)S(6)} %copy.24.refs_1_.refs_3_, f32[1536,128]{1,0:T(8,128)S(1)} %get-tuple-element.80.refs_2_, ...), custom_call_target="tpu_custom_call" | custom-call | flops 855638016 | bytes 7134212 | tf_op jit(solution)/shard_map/pallas_call | solution.py:185
  39.9 1.0 %shard_map.228 = (bf16[1536,128]{1,0:T(8,128)(2,1)S(1)}, f32[512,128]{1,0:T(8,128)S(1)}, bf16[256,128]{1,0:T(8,128)(2,1)S(1)}, bf16[512,128]{1,0:T(8,128)(2,1)S(1)}) custom-call(s32[6,256]{1,0:T(8,128)S(1)} %get-tuple-element.58.refs_0_.refs_1_, bf16[1536,128]{1,0:T(8,128)(2,1)S(1)} %get-tuple-element.90.refs_1_.refs_4_, bf16[384,128]{1,0:T(8,128)(2,1)S(1)} %copy-done.12), custom_call_target="tpu_custom_call" | custom-call | flops 553648128 | bytes 1349632 | tf_op jit(solution)/shard_map/pallas_call | solution.py:185
  41.6 1.0 %collective-permute-start.19 = (bf16[304,128]{1,0:T(8,128)(2,1)S(1)}, bf16[304,128]{1,0:T(8,128)(2,1)S(1)}, u32[]{:S(2)}, u32[]{:S(2)}) collective-permute-start(bf16[304,128]{1,0:T(8,128)(2,1)S(1)} %get-tuple-element.101), channel_id=1, source_target_pairs={{0,2},{2,0},{1,3},{3,1},{4,6},{6,4},{5,7},{7,5},{8,10},{10,8},{9,1... | collective-permute-start | bytes 233480 | tf_op jit(solution)/shard_map/ppermute | solution.py:169
  42.6 3.4 %collective-permute-done.19.refs_2_ = bf16[304,128]{1,0:T(8,128)(2,1)S(1)} collective-permute-done((bf16[304,128]{1,0:T(8,128)(2,1)S(1)}, bf16[304,128]{1,0:T(8,128)(2,1)S(1)}, u32[]{:S(2)}, u32[]{:S(2)}) %collective-permute-start.19) | collective-permute-done | bytes 77856 | tf_op jit(solution)/shard_map/ppermute | solution.py:169
  46.0 3.5 %collective-permute-start.20 = (bf16[560,128]{1,0:T(8,128)(2,1)S(1)}, bf16[560,128]{1,0:T(8,128)(2,1)S(1)}, u32[]{:S(2)}, u32[]{:S(2)}) collective-permute-start(bf16[560,128]{1,0:T(8,128)(2,1)S(1)} %shard_map.232.refs_0_), channel_id=1, source_target_pairs={{0,4},{1,7},{2,6},{3,5},{4,0},{5,3},{6,2},{7,1},{8,12},{9,15},{10,... | collective-permute-start | bytes 430088 | tf_op jit(solution)/shard_map/ppermute | solution.py:125
  49.5 1.1 %collective-permute-start.17 = (bf16[256,128]{1,0:T(8,128)(2,1)S(1)}, bf16[256,128]{1,0:T(8,128)(2,1)S(1)}, u32[]{:S(2)}, u32[]{:S(2)}) collective-permute-start(bf16[256,128]{1,0:T(8,128)(2,1)S(1)} %get-tuple-element.96), channel_id=1, source_target_pairs={{0,2},{1,3},{2,0},{3,1},{4,6},{5,7},{6,4},{7,5},{8,10},{9,11},{10,... | collective-permute-start | bytes 196616 | tf_op jit(solution)/shard_map/ppermute | solution.py:125
  50.6 0.7 collective-permute-start.16
  51.2 1.4 %collective-permute-done.20.refs_4_.refs_1_ = bf16[560,128]{1,0:T(8,128)(2,1)S(1)} collective-permute-done((bf16[560,128]{1,0:T(8,128)(2,1)S(1)}, bf16[560,128]{1,0:T(8,128)(2,1)S(1)}, u32[]{:S(2)}, u32[]{:S(2)}) %collective-permute-start.20) | collective-permute-done | bytes 143392 | tf_op jit(solution)/shard_map/ppermute | solution.py:125
  52.6 3.9 %collective-permute-start.22 = (bf16[304,128]{1,0:T(8,128)(2,1)S(1)}, bf16[304,128]{1,0:T(8,128)(2,1)S(1)}, u32[]{:S(2)}, u32[]{:S(2)}) collective-permute-start(bf16[304,128]{1,0:T(8,128)(2,1)S(1)} %shard_map.234.refs_0_), channel_id=1, source_target_pairs={{0,8},{4,12},{8,0},{12,4},{1,9},{5,13},{9,1},{13,5},{2,10},{6,14},... | collective-permute-start | bytes 233480 | tf_op jit(solution)/shard_map/ppermute | solution.py:169
  56.6 1.8 %shard_map.229 = (bf16[1536,128]{1,0:T(8,128)(2,1)}, f32[512,128]{1,0:T(8,128)S(1)}) custom-call(s32[6,256]{1,0:T(8,128)S(1)} %get-tuple-element.57.refs_0_, s32[6,256]{1,0:T(8,128)S(1)} %get-tuple-element.58.refs_0_.refs_1_, s32[1,256]{1,0:T(1,128)S(1)} %bitcast.7, f32[1536,128]{1,0:T(8,128)S(1)} %get-tuple-element.89.refs_3_, ...), custom_call_target="tpu_custom_call" | custom-call | flops 603979776 | bytes 2339840 | tf_op jit(solution)/shard_map/pallas_call | solution.py:185
  59.2 2.1 %collective-permute-start.23 = (bf16[304,128]{1,0:T(8,128)(2,1)S(1)}, bf16[304,128]{1,0:T(8,128)(2,1)S(1)}, u32[]{:S(2)}, u32[]{:S(2)}) collective-permute-start(bf16[304,128]{1,0:T(8,128)(2,1)S(1)} %shard_map.235.refs_0_), channel_id=1, source_target_pairs={{0,2},{2,0},{1,3},{3,1},{4,6},{6,4},{5,7},{7,5},{8,10},{10,8},{9,1... | collective-permute-start | bytes 233480 | tf_op jit(solution)/shard_map/ppermute | solution.py:169
  61.3 2.5 %collective-permute-done.23.refs_1_ = bf16[304,128]{1,0:T(8,128)(2,1)S(1)} collective-permute-done((bf16[304,128]{1,0:T(8,128)(2,1)S(1)}, bf16[304,128]{1,0:T(8,128)(2,1)S(1)}, u32[]{:S(2)}, u32[]{:S(2)}) %collective-permute-start.23) | collective-permute-done | bytes 77856 | tf_op jit(solution)/shard_map/ppermute | solution.py:169
  63.8 0.7 %add_convert_fusion = bf16[512,128]{1,0:T(8,128)(2,1)} fusion(f32[512,128]{1,0:T(8,128)S(1)} %get-tuple-element.102, bf16[512,128]{1,0:T(8,128)(2,1)S(1)} %collective-permute-done.21, bf16[512,128]{1,0:T(8,128)(2,1)S(1)} %shard_map.233), kind=kLoop, calls=%fused_computation | loop fusion | flops 327680 | bytes 655360 | tf_op jit(solution)/shard_map/convert_element_type | solution.py:689
  65.2 0.9 %shard_map.237 = (f32[640,128]{1,0:T(8,128)}, f32[512,128]{1,0:T(8,128)}, f32[2,128]{1,0:T(2,128)}) custom-call(bf16[608,128]{1,0:T(8,128)(2,1)S(1)} %shard_map.236.refs_0_, bf16[608,128]{1,0:T(8,128)(2,1)S(1)} %collective-permute-done.24.refs_1_), custom_call_target="tpu_custom_call" | custom-call | bytes 902144 | tf_op jit(solution)/shard_map/pallas_call | solution.py:185
  (75 shorter events, 6.2 us)
Async XLA Ops:
  2.2 5.6 %copy-start.1 = (bf16[512,128]{1,0:T(8,128)(2,1)S(1)}, bf16[512,128]{1,0:T(8,128)(2,1)}, u32[]{:S(2)}) copy-start(bf16[512,128]{1,0:T(8,128)(2,1)} %refs_2_.8) | copy-start | bytes 393220
  2.2 5.6 %copy-start.13 = (s32[1536]{0:T(1024)S(1)}, s32[1536]{0:T(1024)}, u32[]{:S(2)}) copy-start(s32[1536]{0:T(1024)} %refs_0_.1) | copy-start | bytes 18436
  2.2 5.6 %copy-start.14 = (s32[1536]{0:T(1024)S(1)}, s32[1536]{0:T(1024)}, u32[]{:S(2)}) copy-start(s32[1536]{0:T(1024)} %refs_1_.6) | copy-start | bytes 18436
  2.5 5.3 %copy-start.15 = (s32[6]{0:T(128)S(1)}, s32[6]{0:T(128)}, u32[]{:S(2)}) copy-start(s32[6]{0:T(128)} %refs_2_.5) | copy-start | bytes 76
  2.5 5.3 %copy-start.16 = (f32[128]{0:T(128)S(1)}, f32[128]{0:T(128)}, u32[]{:S(2)}) copy-start(f32[128]{0:T(128)} %param.27) | copy-start | bytes 1540
  2.5 6.8 %collective-permute-start.1 = (bf16[256,128]{1,0:T(8,128)(2,1)S(1)}, bf16[256,128]{1,0:T(8,128)(2,1)S(1)}, u32[]{:S(2)}, u32[]{:S(2)}) collective-permute-start(bf16[256,128]{1,0:T(8,128)(2,1)S(1)} %shard_map.218.refs_2_), channel_id=1, source_target_pairs={{0,4},{1,7},{2,6},{3,5},{4,0},{5,3},{6,2},{7,1},{8,12},{9,15},{10,... | collective-permute-start | bytes 196616 | tf_op jit(solution)/shard_map/ppermute | solution.py:125
  5.6 3.8 %collective-permute-start = (bf16[256,128]{1,0:T(8,128)(2,1)S(1)}, bf16[256,128]{1,0:T(8,128)(2,1)S(1)}, u32[]{:S(2)}, u32[]{:S(2)}) collective-permute-start(bf16[256,128]{1,0:T(8,128)(2,1)S(1)} %shard_map.218.refs_2_), channel_id=1, source_target_pairs={{4,10},{5,9},{6,8},{7,11},{8,6},{9,5},{10,4},{11,7},{20,26},{21,25... | collective-permute-start | bytes 196616 | tf_op jit(solution)/shard_map/ppermute | solution.py:125
  6.3 5.3 %collective-permute-start.2 = (bf16[256,128]{1,0:T(8,128)(2,1)S(1)}, bf16[256,128]{1,0:T(8,128)(2,1)S(1)}, u32[]{:S(2)}, u32[]{:S(2)}) collective-permute-start(bf16[256,128]{1,0:T(8,128)(2,1)S(1)} %shard_map.218.refs_2_), channel_id=1, source_target_pairs={{0,2},{1,3},{2,0},{3,1},{4,6},{5,7},{6,4},{7,5},{8,10},{9,11},{10,... | collective-permute-start | bytes 196616 | tf_op jit(solution)/shard_map/ppermute | solution.py:125
  9.3 2.2 %collective-permute-start.4 = (bf16[256,128]{1,0:T(8,128)(2,1)S(1)}, bf16[256,128]{1,0:T(8,128)(2,1)S(1)}, u32[]{:S(2)}, u32[]{:S(2)}) collective-permute-start(bf16[256,128]{1,0:T(8,128)(2,1)S(1)} %collective-permute-done.1.refs_10_), channel_id=1, source_target_pairs={{0,1},{1,0},{2,3},{3,2},{4,5},{5,4},{6,7},{7,6},{8,9},{9,8},{10,11... | collective-permute-start | bytes 196616 | tf_op jit(solution)/shard_map/ppermute | solution.py:169
  9.4 2.1 %collective-permute-start.3 = (bf16[256,128]{1,0:T(8,128)(2,1)S(1)}, bf16[256,128]{1,0:T(8,128)(2,1)S(1)}, u32[]{:S(2)}, u32[]{:S(2)}) collective-permute-start(bf16[256,128]{1,0:T(8,128)(2,1)S(1)} %collective-permute-done.refs_9_), channel_id=1, source_target_pairs={{0,1},{1,0},{2,3},{3,2},{4,5},{5,4},{6,7},{7,6},{8,9},{9,8},{10,11... | collective-permute-start | bytes 196616 | tf_op jit(solution)/shard_map/ppermute | solution.py:169
  14.5 1.4 %collective-permute-start.5 = (bf16[512,128]{1,0:T(8,128)(2,1)S(1)}, bf16[512,128]{1,0:T(8,128)(2,1)S(1)}, u32[]{:S(2)}, u32[]{:S(2)}) collective-permute-start(bf16[512,128]{1,0:T(8,128)(2,1)S(1)} %get-tuple-element.64), channel_id=1, source_target_pairs={{0,1},{1,0},{2,3},{3,2},{4,5},{5,4},{6,7},{7,6},{8,9},{9,8},{10,11... | collective-permute-start | bytes 393224 | tf_op jit(solution)/shard_map/ppermute | solution.py:169
  14.7 8.3 %collective-permute-start.8 = (bf16[256,128]{1,0:T(8,128)(2,1)S(1)}, bf16[256,128]{1,0:T(8,128)(2,1)S(1)}, u32[]{:S(2)}, u32[]{:S(2)}) collective-permute-start(bf16[256,128]{1,0:T(8,128)(2,1)S(1)} %get-tuple-element.67), channel_id=1, source_target_pairs={{0,2},{1,3},{2,0},{3,1},{4,6},{5,7},{6,4},{7,5},{8,10},{9,11},{10,... | collective-permute-start | bytes 196616 | tf_op jit(solution)/shard_map/ppermute | solution.py:125
  16.0 7.1 %collective-permute-start.6 = (bf16[256,128]{1,0:T(8,128)(2,1)S(1)}, bf16[256,128]{1,0:T(8,128)(2,1)S(1)}, u32[]{:S(2)}, u32[]{:S(2)}) collective-permute-start(bf16[256,128]{1,0:T(8,128)(2,1)S(1)} %get-tuple-element.65), channel_id=1, source_target_pairs={{0,4},{1,7},{2,6},{3,5},{4,0},{5,3},{6,2},{7,1},{8,12},{9,15},{10,... | collective-permute-start | bytes 196616 | tf_op jit(solution)/shard_map/ppermute | solution.py:125
  20.6 2.4 %collective-permute-start.7 = (bf16[256,128]{1,0:T(8,128)(2,1)S(1)}, bf16[256,128]{1,0:T(8,128)(2,1)S(1)}, u32[]{:S(2)}, u32[]{:S(2)}) collective-permute-start(bf16[256,128]{1,0:T(8,128)(2,1)S(1)} %get-tuple-element.66), channel_id=1, source_target_pairs={{4,10},{5,9},{6,8},{7,11},{8,6},{9,5},{10,4},{11,7},{20,26},{21,25... | collective-permute-start | bytes 196616 | tf_op jit(solution)/shard_map/ppermute | solution.py:125
  23.1 2.0 %copy-start.7 = (bf16[128,128]{1,0:T(8,128)(2,1)S(1)}, bf16[128,128]{1,0:T(8,128)(2,1)}, u32[]{:S(2)}) copy-start(bf16[128,128]{1,0:T(8,128)(2,1)} %refs_6_.4) | copy-start | bytes 98308
  23.5 1.6 %collective-permute-start.9 = (bf16[512,128]{1,0:T(8,128)(2,1)S(1)}, bf16[512,128]{1,0:T(8,128)(2,1)S(1)}, u32[]{:S(2)}, u32[]{:S(2)}) collective-permute-start(bf16[512,128]{1,0:T(8,128)(2,1)S(1)} %shard_map.223.refs_0_), channel_id=1, source_target_pairs={{0,1},{1,0},{2,3},{3,2},{4,5},{5,4},{6,7},{7,6},{8,9},{9,8},{10,11... | collective-permute-start | bytes 393224 | tf_op jit(solution)/shard_map/ppermute | solution.py:169
  26.5 8.3 %collective-permute-start.11 = (bf16[256,128]{1,0:T(8,128)(2,1)S(1)}, bf16[256,128]{1,0:T(8,128)(2,1)S(1)}, u32[]{:S(2)}, u32[]{:S(2)}) collective-permute-start(bf16[256,128]{1,0:T(8,128)(2,1)S(1)} %get-tuple-element.79.refs_4_), channel_id=1, source_target_pairs={{0,4},{1,7},{2,6},{3,5},{4,0},{5,3},{6,2},{7,1},{8,12},{9,15},{10,... | collective-permute-start | bytes 196616 | tf_op jit(solution)/shard_map/ppermute | solution.py:125
  31.0 3.8 %collective-permute-start.10 = (bf16[256,128]{1,0:T(8,128)(2,1)S(1)}, bf16[256,128]{1,0:T(8,128)(2,1)S(1)}, u32[]{:S(2)}, u32[]{:S(2)}) collective-permute-start(bf16[256,128]{1,0:T(8,128)(2,1)S(1)} %get-tuple-element.79.refs_4_), channel_id=1, source_target_pairs={{4,10},{5,9},{6,8},{7,11},{8,6},{9,5},{10,4},{11,7},{20,26},{21,25... | collective-permute-start | bytes 196616 | tf_op jit(solution)/shard_map/ppermute | solution.py:125
  31.9 4.6 %collective-permute-start.12 = (bf16[256,128]{1,0:T(8,128)(2,1)S(1)}, bf16[256,128]{1,0:T(8,128)(2,1)S(1)}, u32[]{:S(2)}, u32[]{:S(2)}) collective-permute-start(bf16[256,128]{1,0:T(8,128)(2,1)S(1)} %get-tuple-element.79.refs_4_), channel_id=1, source_target_pairs={{0,2},{1,3},{2,0},{3,1},{4,6},{5,7},{6,4},{7,5},{8,10},{9,11},{10,... | collective-permute-start | bytes 196616 | tf_op jit(solution)/shard_map/ppermute | solution.py:125
  33.2 2.2 %copy-start.11 = (bf16[1536,128]{1,0:T(8,128)(2,1)S(1)}, bf16[1536,128]{1,0:T(8,128)(2,1)}, u32[]{:S(2)}) copy-start(bf16[1536,128]{1,0:T(8,128)(2,1)} %refs_5_.5) | copy-start | bytes 1179652
  34.8 1.7 %collective-permute-start.14 = (bf16[256,128]{1,0:T(8,128)(2,1)S(1)}, bf16[256,128]{1,0:T(8,128)(2,1)S(1)}, u32[]{:S(2)}, u32[]{:S(2)}) collective-permute-start(bf16[256,128]{1,0:T(8,128)(2,1)S(1)} %collective-permute-done.11.refs_17_), channel_id=1, source_target_pairs={{0,1},{1,0},{2,3},{3,2},{4,5},{5,4},{6,7},{7,6},{8,9},{9,8},{10,11... | collective-permute-start | bytes 196616 | tf_op jit(solution)/shard_map/ppermute | solution.py:169
  34.8 1.7 %collective-permute-start.13 = (bf16[256,128]{1,0:T(8,128)(2,1)S(1)}, bf16[256,128]{1,0:T(8,128)(2,1)S(1)}, u32[]{:S(2)}, u32[]{:S(2)}) collective-permute-start(bf16[256,128]{1,0:T(8,128)(2,1)S(1)} %collective-permute-done.10.refs_16_), channel_id=1, source_target_pairs={{0,1},{1,0},{2,3},{3,2},{4,5},{5,4},{6,7},{7,6},{8,9},{9,8},{10,11... | collective-permute-start | bytes 196616 | tf_op jit(solution)/shard_map/ppermute | solution.py:169
  39.8 1.7 %collective-permute-start.18 = (bf16[608,128]{1,0:T(8,128)(2,1)S(1)}, bf16[608,128]{1,0:T(8,128)(2,1)S(1)}, u32[]{:S(2)}, u32[]{:S(2)}) collective-permute-start(bf16[608,128]{1,0:T(8,128)(2,1)S(1)} %get-tuple-element.99), channel_id=1, source_target_pairs={{0,1},{1,0},{2,3},{3,2},{4,5},{5,4},{6,7},{7,6},{8,9},{9,8},{10,11... | collective-permute-start | bytes 466952 | tf_op jit(solution)/shard_map/ppermute | solution.py:169
  41.0 1.6 %collective-permute-start.15 = (bf16[512,128]{1,0:T(8,128)(2,1)S(1)}, bf16[512,128]{1,0:T(8,128)(2,1)S(1)}, u32[]{:S(2)}, u32[]{:S(2)}) collective-permute-start(bf16[512,128]{1,0:T(8,128)(2,1)S(1)} %get-tuple-element.94), channel_id=1, source_target_pairs={{0,1},{1,0},{2,3},{3,2},{4,5},{5,4},{6,7},{7,6},{8,9},{9,8},{10,11... | collective-permute-start | bytes 393224 | tf_op jit(solution)/shard_map/ppermute | solution.py:169
  41.6 4.5 %collective-permute-start.19 = (bf16[304,128]{1,0:T(8,128)(2,1)S(1)}, bf16[304,128]{1,0:T(8,128)(2,1)S(1)}, u32[]{:S(2)}, u32[]{:S(2)}) collective-permute-start(bf16[304,128]{1,0:T(8,128)(2,1)S(1)} %get-tuple-element.101), channel_id=1, source_target_pairs={{0,2},{2,0},{1,3},{3,1},{4,6},{6,4},{5,7},{7,5},{8,10},{10,8},{9,1... | collective-permute-start | bytes 233480 | tf_op jit(solution)/shard_map/ppermute | solution.py:169
  46.0 6.6 %collective-permute-start.20 = (bf16[560,128]{1,0:T(8,128)(2,1)S(1)}, bf16[560,128]{1,0:T(8,128)(2,1)S(1)}, u32[]{:S(2)}, u32[]{:S(2)}) collective-permute-start(bf16[560,128]{1,0:T(8,128)(2,1)S(1)} %shard_map.232.refs_0_), channel_id=1, source_target_pairs={{0,4},{1,7},{2,6},{3,5},{4,0},{5,3},{6,2},{7,1},{8,12},{9,15},{10,... | collective-permute-start | bytes 430088 | tf_op jit(solution)/shard_map/ppermute | solution.py:125
  49.5 8.9 %collective-permute-start.17 = (bf16[256,128]{1,0:T(8,128)(2,1)S(1)}, bf16[256,128]{1,0:T(8,128)(2,1)S(1)}, u32[]{:S(2)}, u32[]{:S(2)}) collective-permute-start(bf16[256,128]{1,0:T(8,128)(2,1)S(1)} %get-tuple-element.96), channel_id=1, source_target_pairs={{0,2},{1,3},{2,0},{3,1},{4,6},{5,7},{6,4},{7,5},{8,10},{9,11},{10,... | collective-permute-start | bytes 196616 | tf_op jit(solution)/shard_map/ppermute | solution.py:125
  50.6 7.8 %collective-permute-start.16 = (bf16[256,128]{1,0:T(8,128)(2,1)S(1)}, bf16[256,128]{1,0:T(8,128)(2,1)S(1)}, u32[]{:S(2)}, u32[]{:S(2)}) collective-permute-start(bf16[256,128]{1,0:T(8,128)(2,1)S(1)} %get-tuple-element.95), channel_id=1, source_target_pairs={{4,10},{5,9},{6,8},{7,11},{8,6},{9,5},{10,4},{11,7},{20,26},{21,25... | collective-permute-start | bytes 196616 | tf_op jit(solution)/shard_map/ppermute | solution.py:125
  52.6 6.5 %collective-permute-start.22 = (bf16[304,128]{1,0:T(8,128)(2,1)S(1)}, bf16[304,128]{1,0:T(8,128)(2,1)S(1)}, u32[]{:S(2)}, u32[]{:S(2)}) collective-permute-start(bf16[304,128]{1,0:T(8,128)(2,1)S(1)} %shard_map.234.refs_0_), channel_id=1, source_target_pairs={{0,8},{4,12},{8,0},{12,4},{1,9},{5,13},{9,1},{13,5},{2,10},{6,14},... | collective-permute-start | bytes 233480 | tf_op jit(solution)/shard_map/ppermute | solution.py:169
  58.8 5.0 %collective-permute-start.21 = (bf16[512,128]{1,0:T(8,128)(2,1)S(1)}, bf16[512,128]{1,0:T(8,128)(2,1)S(1)}, u32[]{:S(2)}, u32[]{:S(2)}) collective-permute-start(bf16[512,128]{1,0:T(8,128)(2,1)S(1)} %shard_map.233), channel_id=1, source_target_pairs={{0,1},{1,0},{2,3},{3,2},{4,5},{5,4},{6,7},{7,6},{8,9},{9,8},{10,11... | collective-permute-start | bytes 393224 | tf_op jit(solution)/shard_map/ppermute | solution.py:169
  59.2 4.5 %collective-permute-start.23 = (bf16[304,128]{1,0:T(8,128)(2,1)S(1)}, bf16[304,128]{1,0:T(8,128)(2,1)S(1)}, u32[]{:S(2)}, u32[]{:S(2)}) collective-permute-start(bf16[304,128]{1,0:T(8,128)(2,1)S(1)} %shard_map.235.refs_0_), channel_id=1, source_target_pairs={{0,2},{2,0},{1,3},{3,1},{4,6},{6,4},{5,7},{7,5},{8,10},{10,8},{9,1... | collective-permute-start | bytes 233480 | tf_op jit(solution)/shard_map/ppermute | solution.py:169
  63.7 1.4 %collective-permute-start.24 = (bf16[608,128]{1,0:T(8,128)(2,1)S(1)}, bf16[608,128]{1,0:T(8,128)(2,1)S(1)}, u32[]{:S(2)}, u32[]{:S(2)}) collective-permute-start(bf16[608,128]{1,0:T(8,128)(2,1)S(1)} %shard_map.236.refs_0_), channel_id=1, source_target_pairs={{0,1},{1,0},{2,3},{3,2},{4,5},{5,4},{6,7},{7,6},{8,9},{9,8},{10,11... | collective-permute-start | bytes 466952 | tf_op jit(solution)/shard_map/ppermute | solution.py:169
  (10 other events, 15.9 us)
